TPU v7x, 32 devices: a whole 2x2x4 slice. The times are simulated.
32 devices in a mesh: groups: 2 (over y), adapter: 4 (over z), lane: 4 (over x, core).
Axes of the slice: x: 2, y: 2, z: 4, core: 2. Of those that a mesh axis runs over, the one named last changes fastest.
Arguments:
- residual_input: bfloat16 [128, 8192], P(('groups', 'adapter')), parts along dimension 0, may hold values from -6 to 6
- attention_norm_gain: float32 [8192], replicated, may hold values from 0.25 to 1.75
- query_weight: bfloat16 [8192, 8192], P('adapter', 'lane'), may hold values from -0.0625 to 0.0625
- key_weight: bfloat16 [8192, 1024], P('adapter', 'lane'), may hold values from -0.0625 to 0.0625
- value_weight: bfloat16 [8192, 1024], P('adapter', 'lane'), may hold values from -0.0625 to 0.0625
- query_down_weight: bfloat16 [8, 8192, 64], P('adapter', 'lane'), may hold values from -0.0625 to 0.0625
- query_up_weight: bfloat16 [8, 64, 8192], P('adapter', None, 'lane'), may hold values from -0.75 to 0.75
- value_down_weight: bfloat16 [8, 8192, 64], P('adapter', 'lane'), may hold values from -0.0625 to 0.0625
- value_up_weight: bfloat16 [8, 64, 1024], P('adapter', None, 'lane'), may hold values from -0.75 to 0.75
- cached_key_rows: bfloat16 [128, 8, 256, 128], P(('groups', 'adapter'), 'lane'), parts along dimension 0, may hold values from -200 to 200
- cached_value_rows: bfloat16 [128, 8, 256, 128], P(('groups', 'adapter'), 'lane'), parts along dimension 0, may hold values from -6 to 6
- row_adapter_index: int32 [128], P('groups'), parts along dimension 0, may hold values from 0 to 7, as said below
- cached_length: int32 [128], P(('groups', 'adapter')), parts along dimension 0, may hold values from 1 to 256, as said below
Outputs:
- attended: bfloat16 [128, 8192], P(('groups', 'adapter'), 'lane'), parts along dimension 0
- fresh_kv: bfloat16 [128, 2, 1024], P(('groups', 'adapter'), None, 'lane'), parts along dimension 0
There are 2 independent parts, one for each index of `groups`. A program takes and returns all parts, laid end to end along the dimension named above; an argument that names none is the same for every part. Nothing has to cross between parts.
Inputs may be any that keep to these rules, and one draw needn't show every extreme that they name: `row_adapter_index`: rows come in aligned blocks of 16, one block per index of adapter. Adapter a belongs to owner a // 2. No block has more than 8 rows whose adapters belong to one owner, and in every block some owner has exactly 8. `cached_length`: some row has exactly 256 cached positions.
All inputs are finite; a program needn't handle non-finite values.
Results may differ from a plain program's by a relative error of at most 0.029.
Values may be sent and summed in bfloat16 or wider, within the bound.
No kernel may reach another device: no remote copies, remote signals or barrier semaphores. Data moves between devices by JAX's collectives and lax.ppermute only.
A program may use at most 64 MiB of HBM per device.

v0:
```python
import jax
import jax.numpy as jnp
from jax import lax
from jax.sharding import PartitionSpec as P

EPS = 1e-05
ADAPTER_SCALE = 0.5


def on_device(
    residual_input,
    attention_norm_gain,
    query_weight,
    key_weight,
    value_weight,
    query_down_weight,
    query_up_weight,
    value_down_weight,
    value_up_weight,
    cached_key_rows,
    cached_value_rows,
    row_adapter_index,
    cached_length,
):
    owners_count = lax.axis_size("adapter")
    lane_count = lax.axis_size("lane")
    my_index = lax.axis_index("adapter")
    lane_index = lax.axis_index("lane")
    block_rows, width = residual_input.shape
    nearby_count = query_down_weight.shape[0]
    capacity = max(2, 2 * block_rows // owners_count)
    part_width = width // lane_count
    query_cols = query_weight.shape[1]
    kv_cols = key_weight.shape[1]
    slot_total = owners_count * capacity
    widened = residual_input.astype(jnp.float32)
    normalized_input = (
        widened
        * lax.rsqrt(jnp.mean(widened * widened, axis=-1, keepdims=True) + EPS)
        * attention_norm_gain
    ).astype(jnp.bfloat16)
    ids_blocks = row_adapter_index.reshape(owners_count, block_rows)
    owners = ids_blocks // nearby_count
    local_ids = ids_blocks % nearby_count
    owner_hot = (owners[:, :, None] == jnp.arange(owners_count)[None, None, :]).astype(jnp.int32)
    before = jnp.cumsum(owner_hot, axis=1) - owner_hot
    slot_pos = jnp.sum(before * owner_hot, axis=-1)
    slot_dest = owners * capacity + slot_pos
    mine_dest = lax.dynamic_index_in_dim(slot_dest, my_index, 0, keepdims=False)
    placement = (jnp.arange(slot_total)[:, None] == mine_dest[None, :]).astype(jnp.bfloat16)
    x_part = lax.dynamic_slice_in_dim(normalized_input, lane_index * part_width, part_width, 1)
    outgoing = jnp.dot(placement, x_part, preferred_element_type=jnp.float32).astype(jnp.bfloat16)
    outgoing = outgoing.reshape(owners_count, capacity, part_width)
    gathered_rows = lax.all_to_all(
        outgoing, "adapter", split_axis=0, concat_axis=0, tiled=True
    ).reshape(slot_total, part_width)
    to_mine = owners == my_index
    slot_code = slot_pos * nearby_count + local_ids
    code_range = jnp.arange(capacity * nearby_count)
    selector = jnp.sum(
        ((slot_code[:, :, None] == code_range[None, None, :]) & to_mine[:, :, None]).astype(
            jnp.float32
        ),
        axis=1,
    )
    chooser = selector.reshape(slot_total, nearby_count)
    query_down_every = jnp.einsum(
        "xi,yig->xyg", gathered_rows, query_down_weight, preferred_element_type=jnp.float32
    )
    value_down_every = jnp.einsum(
        "xi,yig->xyg", gathered_rows, value_down_weight, preferred_element_type=jnp.float32
    )
    down_q_part = jnp.einsum("skr,sk->sr", query_down_every, chooser)
    down_v_part = jnp.einsum("skr,sk->sr", value_down_every, chooser)
    rank_total = lax.psum((down_q_part, down_v_part), "lane")
    chooser_low = chooser.astype(jnp.bfloat16)
    query_spread = rank_total[0].astype(jnp.bfloat16)[:, None, :] * chooser_low[:, :, None]
    value_spread = rank_total[1].astype(jnp.bfloat16)[:, None, :] * chooser_low[:, :, None]
    query_update = (
        ADAPTER_SCALE
        * jnp.einsum(
            "igz,gzu->iu", query_spread, query_up_weight, preferred_element_type=jnp.float32
        )
    ).astype(jnp.bfloat16)
    value_update = (
        ADAPTER_SCALE
        * jnp.einsum(
            "igz,gzu->iu", value_spread, value_up_weight, preferred_element_type=jnp.float32
        )
    ).astype(jnp.bfloat16)
    full_rows = lax.all_to_all(normalized_input, "adapter", split_axis=1, concat_axis=0, tiled=True)
    summand = jnp.concatenate(
        [
            jnp.dot(full_rows, query_weight, preferred_element_type=jnp.float32),
            jnp.dot(full_rows, key_weight, preferred_element_type=jnp.float32),
            jnp.dot(full_rows, value_weight, preferred_element_type=jnp.float32),
        ],
        axis=1,
    )
    summed = lax.psum_scatter(summand, "adapter", scatter_dimension=0, tiled=True)
    going_back = jnp.concatenate([query_update, value_update], axis=1).reshape(
        owners_count, capacity, query_cols + kv_cols
    )
    returned_rows = lax.all_to_all(going_back, "adapter", split_axis=0, concat_axis=0, tiled=True)
    row_delta = jnp.dot(
        placement.T,
        returned_rows.reshape(slot_total, query_cols + kv_cols),
        preferred_element_type=jnp.float32,
    )
    queries = (summed[:, :query_cols] + row_delta[:, :query_cols]).astype(jnp.bfloat16)
    value_new = (summed[:, query_cols + kv_cols :] + row_delta[:, query_cols:]).astype(jnp.bfloat16)
    key_new = summed[:, query_cols : query_cols + kv_cols].astype(jnp.bfloat16)
    fresh_kv = jnp.stack([key_new, value_new], axis=1)
    kv_local = cached_key_rows.shape[1]
    head_dim = cached_key_rows.shape[3]
    context = cached_key_rows.shape[2]
    group_size = query_cols // head_dim // kv_local
    scale = head_dim ** (-0.5)
    grouped = queries.reshape(block_rows, kv_local, group_size, head_dim)
    key_heads = key_new.reshape(block_rows, kv_local, head_dim)
    value_heads = value_new.reshape(block_rows, kv_local, 1, head_dim).astype(jnp.float32)
    scores = (
        jnp.einsum("rkgd,rksd->rkgs", grouped, cached_key_rows, preferred_element_type=jnp.float32)
        * scale
    )
    own_score = (
        jnp.einsum("rkgd,rkd->rkg", grouped, key_heads, preferred_element_type=jnp.float32) * scale
    )
    visible = jnp.arange(context)[None, None, None, :] < cached_length[:, None, None, None]
    peak = jnp.maximum(jnp.max(jnp.where(visible, scores, -jnp.inf), axis=-1), own_score)
    lifted = jnp.where(visible, jnp.exp(scores - peak[..., None]), 0.0)
    own_lift = jnp.exp(own_score - peak)
    row_total = jnp.sum(lifted, axis=-1) + own_lift
    weights = (lifted / row_total[..., None]).astype(jnp.bfloat16)
    own_weight = (own_lift / row_total).astype(jnp.bfloat16)
    mixed = jnp.einsum(
        "rkgs,rksd->rkgd", weights, cached_value_rows, preferred_element_type=jnp.float32
    )
    mixed = mixed + own_weight.astype(jnp.float32)[..., None] * value_heads
    attended = mixed.reshape(block_rows, query_cols).astype(jnp.bfloat16)
    return (attended, fresh_kv)


def solution(mesh):
    in_specs = (
        P(("groups", "adapter"), None),
        P(),
        P("adapter", "lane"),
        P("adapter", "lane"),
        P("adapter", "lane"),
        P("adapter", "lane", None),
        P("adapter", None, "lane"),
        P("adapter", "lane", None),
        P("adapter", None, "lane"),
        P(("groups", "adapter"), "lane", None, None),
        P(("groups", "adapter"), "lane", None, None),
        P("groups"),
        P(("groups", "adapter")),
    )
    out_specs = (P(("groups", "adapter"), "lane"), P(("groups", "adapter"), None, "lane"))
    return jax.shard_map(
        on_device, mesh=mesh, in_specs=in_specs, out_specs=out_specs, check_vma=False
    )
```

profile of v0, /device:TPU:0, one launch (start us, length us, event | category | flops | bytes accessed | tf_op | source)
XLA Modules:
  0.0 79.0 jit_solution(11097026009091515777)
XLA Ops:
  7.2 0.0 copy-start
  7.2 0.9 %reshape.146 = s32[4,16]{1,0:T(4,128)S(1)} reshape(s32[64]{0:T(128)} %param.24) | data formatting | bytes 512 | tf_op jit(solution)/shard_map/reshape | solution.py:42
  8.1 0.1 fusion.23
  8.2 0.2 select_reduce_fusion.1
  8.5 1.1 %fusion.6 = f32[16]{0:T(128)S(1)} fusion(bf16[16,8192]{1,0:T(8,128)(2,1)} %param.13), kind=kLoop, calls=%fused_computation.14 | loop fusion | flops 393200 | bytes 262208 | tf_op jit(solution)/shard_map/reduce_sum | solution.py:39
  9.6 1.1 %fusion.8 = bf16[16,8192]{1,0:T(8,128)(2,1)S(1)} fusion(bf16[16,8192]{1,0:T(8,128)(2,1)} %param.13, f32[8192]{0:T(1024)} %param.14, f32[16]{0:T(128)S(1)} %add_rsqrt_fusion), kind=kLoop, calls=%fused_computation.16 | loop fusion | flops 524288 | bytes 557120 | tf_op jit(solution)/shard_map/convert_element_type | solution.py:41
  10.7 0.8 %fusion.2 = bf16[4,8,2048]{2,1,0:T(8,128)(2,1)} fusion(bf16[16,8192]{1,0:T(8,128)(2,1)S(1)} %fusion.8, s32[]{:T(128)S(6)} %select_n.39, s32[16]{0:T(128)S(1)} %dynamic-slice_bitcast_fusion), kind=kOutput, calls=%fused_computation.4 | convolution fusion | flops 2163200 | bytes 197124 | tf_op jit(solution)/shard_map/dot_general | solution.py:52
  11.5 6.3 %all-to-all-start.1 = ((bf16[4,8,2048]{2,1,0:T(8,128)(2,1)}), bf16[4,8,2048]{2,1,0:T(8,128)(2,1)S(1)}, u32[]{:S(2)}, u32[]{:S(2)}) async-start(bf16[4,8,2048]{2,1,0:T(8,128)(2,1)} %fusion.2), calls=%async_computation.2 | async-start | bytes 262144 | tf_op jit(solution)/shard_map/all_to_all | solution.py:54
  17.9 0.1 convert_reduce_fusion
  18.0 0.7 reshape.156
  18.7 0.1 reshape.149
  18.7 0.7 copy.26
  19.4 0.7 copy.44
  20.1 3.8 %all-to-all-done.1 = bf16[4,8,2048]{2,1,0:T(8,128)(2,1)S(1)} async-done(((bf16[4,8,2048]{2,1,0:T(8,128)(2,1)}), bf16[4,8,2048]{2,1,0:T(8,128)(2,1)S(1)}, u32[]{:S(2)}, u32[]{:S(2)}) %all-to-all-start.1) | async-done | bytes 131104 | tf_op jit(solution)/shard_map/all_to_all | solution.py:54
  23.9 3.4 %all-to-all-start = ((bf16[16,4,2048]{2,0,1:T(8,128)(2,1)}), bf16[16,4,2048]{2,0,1:T(8,128)(2,1)S(1)}, u32[]{:S(2)}, u32[]{:S(2)}) async-start(bf16[16,4,2048]{2,0,1:T(8,128)(2,1)} %bitcast.69), calls=%async_computation | async-start | bytes 524288 | tf_op jit(solution)/shard_map/all_to_all | solution.py:91
  27.4 0.0 reduce-scatter.2.cloned.1.call-start
  27.4 0.3 fusion.15
  27.8 1.5 %fusion.26 = f32[32,1,64]{2,1,0:T(1,128)} fusion(f32[32,2,1]{1,2,0:T(1,128)} %bitcast.82, bf16[32,2,64]{2,0,1:T(8,128)(2,1)S(1)} %fusion.15), kind=kOutput, calls=%fused_computation.45 | convolution fusion | flops 8192 | bytes 16640 | tf_op jit(solution)/shard_map/skr,sk->sr/dot_general | solution.py:73
  29.2 1.0 %fusion.13 = bf16[32,2,64]{2,0,1:T(8,128)(2,1)} fusion(bf16[2,2048,64]{1,2,0:T(8,128)(2,1)S(1)} %copy-done.4, bf16[4,8,2048]{2,1,0:T(8,128)(2,1)S(1)} %all-to-all-done.1), kind=kOutput, calls=%fused_computation.27 | convolution fusion | flops 16777216 | bytes 663552 | tf_op jit(solution)/shard_map/xi,yig->xyg/dot_general | solution.py:70
  30.2 4.9 %all-to-all-done = bf16[16,4,2048]{2,0,1:T(8,128)(2,1)S(1)} async-done(((bf16[16,4,2048]{2,0,1:T(8,128)(2,1)}), bf16[16,4,2048]{2,0,1:T(8,128)(2,1)S(1)}, u32[]{:S(2)}, u32[]{:S(2)}) %all-to-all-start) | async-done | bytes 262176 | tf_op jit(solution)/shard_map/all_to_all | solution.py:91
  35.2 5.1 %fusion.44 = f32[64,2048]{1,0:T(8,128)S(1)} fusion(bf16[64,2048]{1,0:T(8,128)(2,1)S(1)} %bitcast.71, bf16[2048,2048]{1,0:T(8,128)(2,1)} %param.15), kind=kOutput, calls=%fused_computation.83 | convolution fusion | flops 536870912 | bytes 9175040 | tf_op jit(solution)/shard_map/dot_general | solution.py:94
  40.3 0.0 copy-start.6
  40.3 0.3 fusion.45
  40.6 0.3 fusion.46
  41.0 0.9 %pad_maximum_fusion = f32[64,2560]{1,0:T(8,128)} fusion(f32[64,256]{1,0:T(8,128)S(1)} %fusion.46, f32[64,256]{1,0:T(8,128)S(1)} %fusion.45, f32[64,2048]{1,0:T(8,128)S(1)} %fusion.44), kind=kLoop, calls=%fused_computation.13 | loop fusion | flops 327680 | bytes 1310720 | tf_op jit(solution)/shard_map/concatenate | solution.py:92
  41.8 0.0 reduce-scatter.2.cloned.1.call-update
  41.9 0.9 %fusion.24 = f32[32,1,64]{2,1,0:T(1,128)S(1)} fusion(f32[32,2,1]{1,2,0:T(1,128)S(1)} %bitcast.83, bf16[32,2,64]{2,0,1:T(8,128)(2,1)} %fusion.13), kind=kOutput, calls=%fused_computation.43 | convolution fusion | flops 8192 | bytes 16640 | tf_op jit(solution)/shard_map/skr,sk->sr/dot_general | solution.py:74
  42.7 11.2 %all-reduce = (bf16[32,64]{1,0:T(8,128)(2,1)S(1)}, bf16[32,64]{1,0:T(8,128)(2,1)S(1)}) all-reduce(f32[32,64]{1,0:T(8,128)S(1)} %bitcast.85, f32[32,64]{1,0:T(8,128)} %bitcast.84), channel_id=1, replica_groups=mesh['groups'=2,'adapter'=4,'lane'=4] {'lane'}, use_global_device_ids=true, to_apply=%region_6.7 | all-reduce | flops 4096 | bytes 24576 | tf_op jit(solution)/shard_map/psum | solution.py:75
  54.0 0.3 fusion.5
  54.3 0.3 fusion.1
  54.6 0.7 maximum_bitcast_fusion
  55.3 3.3 %all-to-all-start.2 = ((bf16[4,8,2304]{2,1,0:T(8,128)(2,1)}), bf16[4,8,2304]{2,1,0:T(8,128)(2,1)S(1)}, u32[]{:S(2)}, u32[]{:S(2)}) async-start(bf16[4,8,2304]{2,1,0:T(8,128)(2,1)} %maximum_bitcast_fusion), calls=%async_computation.3 | async-start | bytes 294912 | tf_op jit(solution)/shard_map/all_to_all | solution.py:104
  58.6 0.1 iota_compare_fusion.5
  58.7 6.7 %all-to-all-done.2 = bf16[4,8,2304]{2,1,0:T(8,128)(2,1)S(1)} async-done(((bf16[4,8,2304]{2,1,0:T(8,128)(2,1)}), bf16[4,8,2304]{2,1,0:T(8,128)(2,1)S(1)}, u32[]{:S(2)}, u32[]{:S(2)}) %all-to-all-start.2) | async-done | bytes 147488 | tf_op jit(solution)/shard_map/all_to_all | solution.py:104
  65.4 0.2 fusion.10
  65.6 0.0 reduce-scatter.2.cloned.1.call-done
  65.7 0.7 fusion.29
  66.4 0.7 slice_bitcast_fusion
  67.1 0.6 copy.27
  67.8 0.9 %fusion.21 = bf16[2,8,16,128]{3,1,2,0:T(8,128)(2,1)S(1)} fusion(f32[16,2304]{1,0:T(8,128)S(1)} %fusion.10, f32[16,2560]{1,0:T(8,128)} %reduce-scatter.2.cloned.1.call-done), kind=kLoop, calls=%fused_computation.35 | loop fusion | flops 65536 | bytes 327680
  68.7 0.7 slice.39
  69.4 0.1 fusion.47
  69.6 0.0 copy-done
  69.6 0.7 select_reduce_fusion
  70.4 0.2 fusion.9
  70.6 0.4 copy-done.11
  71.0 0.4 fusion.3
  71.5 0.7 copy.45
  (33 shorter events, 0.2 us)
Async XLA Ops:
  7.2 62.4 %copy-start = (bf16[16,2,256,128]{3,2,1,0:T(8,128)(2,1)S(1)}, bf16[16,2,256,128]{3,2,1,0:T(8,128)(2,1)}, u32[]{:S(2)}) copy-start(bf16[16,2,256,128]{3,2,1,0:T(8,128)(2,1)} %param.22) | copy-start | bytes 6291460
  7.2 20.2 %copy-start.3 = (bf16[2,2048,64]{1,2,0:T(8,128)(2,1)S(1)}, bf16[2,2048,64]{1,2,0:T(8,128)(2,1)}, u32[]{:S(2)}) copy-start(bf16[2,2048,64]{1,2,0:T(8,128)(2,1)} %param.18) | copy-start | bytes 1572868
  7.2 22.1 %copy-start.4 = (bf16[2,2048,64]{1,2,0:T(8,128)(2,1)S(1)}, bf16[2,2048,64]{1,2,0:T(8,128)(2,1)}, u32[]{:S(2)}) copy-start(bf16[2,2048,64]{1,2,0:T(8,128)(2,1)} %param.20) | copy-start | bytes 1572868
  9.6 8.2 %copy-start.7 = (s32[16]{0:T(128)}, s32[16]{0:T(128)S(1)}, u32[]{:S(2)}) copy-start(s32[16]{0:T(128)S(1)} %dynamic-slice_bitcast_fusion) | copy-start | bytes 196
  11.5 12.4 %all-to-all-start.1 = ((bf16[4,8,2048]{2,1,0:T(8,128)(2,1)}), bf16[4,8,2048]{2,1,0:T(8,128)(2,1)S(1)}, u32[]{:S(2)}, u32[]{:S(2)}) async-start(bf16[4,8,2048]{2,1,0:T(8,128)(2,1)} %fusion.2), calls=%async_computation.2 | async-start | bytes 262144 | tf_op jit(solution)/shard_map/all_to_all | solution.py:54
  23.9 11.2 %all-to-all-start = ((bf16[16,4,2048]{2,0,1:T(8,128)(2,1)}), bf16[16,4,2048]{2,0,1:T(8,128)(2,1)S(1)}, u32[]{:S(2)}, u32[]{:S(2)}) async-start(bf16[16,4,2048]{2,0,1:T(8,128)(2,1)} %bitcast.69), calls=%async_computation | async-start | bytes 524288 | tf_op jit(solution)/shard_map/all_to_all | solution.py:91
  27.4 38.3 %reduce-scatter.2.cloned.1.call-start = ((), (), s32[]{:S(2)}) async-start(), calls=%async_computation.4 | async-start | bytes 819200 | tf_op jit(solution)/shard_map/reduce_scatter | solution.py:100
  35.2 5.1 %copy-start.1 = (bf16[2048,256]{1,0:T(8,128)(2,1)S(1)}, bf16[2048,256]{1,0:T(8,128)(2,1)}, u32[]{:S(2)}) copy-start(bf16[2048,256]{1,0:T(8,128)(2,1)} %param.16) | copy-start | bytes 3145732
  35.2 5.4 %copy-start.2 = (bf16[2048,256]{1,0:T(8,128)(2,1)S(1)}, bf16[2048,256]{1,0:T(8,128)(2,1)}, u32[]{:S(2)}) copy-start(bf16[2048,256]{1,0:T(8,128)(2,1)} %param.17) | copy-start | bytes 3145732
  40.3 1.6 %copy-start.6 = (f32[32,2,1]{1,0,2:T(8,128)S(1)}, f32[32,2,1]{1,0,2:T(8,128)}, u32[]{:S(2)}) copy-start(f32[32,2,1]{1,0,2:T(8,128)} %reshape.156) | copy-start | bytes 772
  40.6 13.7 %copy-start.5 = (bf16[2,64,2048]{2,1,0:T(8,128)(2,1)S(1)}, bf16[2,64,2048]{2,1,0:T(8,128)(2,1)}, u32[]{:S(2)}) copy-start(bf16[2,64,2048]{2,1,0:T(8,128)(2,1)} %param.19) | copy-start | bytes 1572868
  40.9 13.1 %copy-start.9 = (bf16[32,2]{0,1:T(2,128)(2,1)S(1)}, bf16[32,2]{0,1:T(2,128)(2,1)}, u32[]{:S(2)}) copy-start(bf16[32,2]{0,1:T(2,128)(2,1)} %copy.26) | copy-start | bytes 388
  40.9 13.1 %copy-start.12 = (bf16[2,64,256]{2,1,0:T(8,128)(2,1)S(1)}, bf16[2,64,256]{2,1,0:T(8,128)(2,1)}, u32[]{:S(2)}) copy-start(bf16[2,64,256]{2,1,0:T(8,128)(2,1)} %param.21) | copy-start | bytes 196612
  40.9 17.7 %copy-start.10 = (s32[16]{0:T(128)S(1)}, s32[16]{0:T(128)}, u32[]{:S(2)}) copy-start(s32[16]{0:T(128)} %param.25) | copy-start | bytes 196
  41.0 24.5 %copy-start.8 = (s32[16]{0:T(128)S(1)}, s32[16]{0:T(128)}, u32[]{:S(2)}) copy-start(s32[16]{0:T(128)} %copy-done.7) | copy-start | bytes 196
  55.3 10.2 %all-to-all-start.2 = ((bf16[4,8,2304]{2,1,0:T(8,128)(2,1)}), bf16[4,8,2304]{2,1,0:T(8,128)(2,1)S(1)}, u32[]{:S(2)}, u32[]{:S(2)}) async-start(bf16[4,8,2304]{2,1,0:T(8,128)(2,1)} %maximum_bitcast_fusion), calls=%async_computation.3 | async-start | bytes 294912 | tf_op jit(solution)/shard_map/all_to_all | solution.py:104
  69.4 1.6 %copy-start.11 = (bf16[16,2,256,128]{3,2,1,0:T(8,128)(2,1)S(1)}, bf16[16,2,256,128]{3,2,1,0:T(8,128)(2,1)}, u32[]{:S(2)}) copy-start(bf16[16,2,256,128]{3,2,1,0:T(8,128)(2,1)} %param.23) | copy-start | bytes 6291460
Sparse Core Ops, SparseCore 0:
  42.0 21.4 reduce-scatter.1
where the time goes:
time: 79.8 us; the launch traced here: 79 us
  waiting for transfers between devices  15.5 us (19%)
  between operations  14.3 us (18%)
  starting transfers between devices  13.1 us (16%)
  matrix products  12.3 us (15%)
  blocking collectives  11.2 us (14%)
  local copies, waits for them, and re-layouts  6.28 us (8%)
  other arithmetic  6.24 us (8%)
    psum x1, blocking collectives, on_device(): rank_total = lax.psum((down_q_part, down_v_part), 'lane')  11.2 us
    all_to_all x1, waiting for transfers between devices, on_device(): lax.all_to_all(going_back, 'adapter', split_axis=0, concat_axis=0, tiled=...  6.74 us
    all_to_all x1, starting transfers between devices, on_device(): lax.all_to_all(outgoing, 'adapter', split_axis=0, concat_axis=0, tiled=True)  6.32 us
    dot_general x1, matrix products, on_device(): jnp.dot(full_rows, query_weight, preferred_element_type=jnp.float32)  5.09 us
    all_to_all x1, waiting for transfers between devices, on_device(): lax.all_to_all(normalized_input, 'adapter', split_axis=1, concat_axis=0,...  4.94 us
    all_to_all x1, waiting for transfers between devices, on_device(): lax.all_to_all(outgoing, 'adapter', split_axis=0, concat_axis=0, tiled=True)  3.82 us
    all_to_all x1, starting transfers between devices, on_device(): lax.all_to_all(normalized_input, 'adapter', split_axis=1, concat_axis=0,...  3.4 us
    all_to_all x1, starting transfers between devices, on_device(): lax.all_to_all(going_back, 'adapter', split_axis=0, concat_axis=0, tiled=...  3.33 us
  transfers between devices with their start and end apart: 4, of which 3 were waited for; matrix products, arithmetic and copies ran while one was open for 9% of the time, Pallas kernels for 0%

commit v1 on v0

v1 whole, which is shorter than its diff:
```python
import jax
import jax.numpy as jnp
from jax import lax
from jax.sharding import PartitionSpec as P

EPS = 1e-05
ADAPTER_SCALE = 0.5


def partner(array, axis, step):
    count = lax.axis_size(axis)
    return lax.ppermute(array, axis, [(i, i ^ step) for i in range(count)])


def on_device(
    residual_input,
    attention_norm_gain,
    query_weight,
    key_weight,
    value_weight,
    query_down_weight,
    query_up_weight,
    value_down_weight,
    value_up_weight,
    cached_key_rows,
    cached_value_rows,
    row_adapter_index,
    cached_length,
):
    owners_count = lax.axis_size("adapter")
    lane_count = lax.axis_size("lane")
    my_index = lax.axis_index("adapter")
    lane_index = lax.axis_index("lane")
    block_rows, width = residual_input.shape
    nearby_count, _, rank = query_down_weight.shape
    capacity = max(2, 2 * block_rows // owners_count)
    lane_width = width // lane_count
    base_width = width // owners_count
    query_cols = query_weight.shape[1]
    kv_cols = key_weight.shape[1]
    steps = range(owners_count)

    order = jnp.bitwise_xor(my_index, jnp.arange(owners_count))
    blocks = row_adapter_index.reshape(owners_count, block_rows)

    def slot_map(ids, owner):
        hit = (ids // nearby_count == owner).astype(jnp.int32)
        place = jnp.cumsum(hit) - hit
        return (jnp.arange(capacity)[:, None] == place[None, :]) & (hit[None, :] > 0)

    mine = lax.dynamic_index_in_dim(blocks, my_index, 0, keepdims=False)
    lane_part = lax.dynamic_slice_in_dim(residual_input, lane_index * lane_width, lane_width, 1)
    base_rows, adapter_rows = [], []
    for step in steps:
        other = my_index ^ step
        base = lax.dynamic_slice_in_dim(residual_input, other * base_width, base_width, 1)
        placed = jnp.dot(
            slot_map(mine, other).astype(jnp.bfloat16), lane_part, preferred_element_type=jnp.float32
        ).astype(jnp.bfloat16)
        if step == 0:
            base_rows.append(base)
            adapter_rows.append(placed)
        elif base_width == lane_width:
            both = partner(jnp.concatenate([base, placed], axis=0), "adapter", step)
            base_rows.append(both[:block_rows])
            adapter_rows.append(both[block_rows:])
        else:
            base_rows.append(partner(base, "adapter", step))
            adapter_rows.append(partner(placed, "adapter", step))

    base_gain = lax.dynamic_slice_in_dim(attention_norm_gain, my_index * base_width, base_width, 0)
    lane_gain = lax.dynamic_slice_in_dim(attention_norm_gain, lane_index * lane_width, lane_width, 0)

    gained = (jnp.concatenate(adapter_rows, axis=0).astype(jnp.float32) * lane_gain).astype(
        jnp.bfloat16
    )
    down_parts = []
    for weight in (query_down_weight, value_down_weight):
        down_parts.append(
            jnp.einsum("xi,yig->xyg", gained, weight, preferred_element_type=jnp.float32)
        )
    down = jnp.concatenate(down_parts, axis=2)
    seen = lax.dynamic_index_in_dim
    row_maps, row_hot = [], []
    for step in steps:
        ids = seen(blocks, my_index ^ step, 0, keepdims=False)
        row_maps.append(slot_map(ids, my_index))
        row_hot.append(ids[:, None] == my_index * nearby_count + jnp.arange(nearby_count)[None, :])
    maps = jnp.stack(row_maps).astype(jnp.float32)
    hot = jnp.concatenate(row_hot, axis=0)
    slots = down.reshape(owners_count, capacity, nearby_count, 2 * rank)
    slot_hot = jnp.einsum(
        "bsr,brg->bsg", maps, hot.reshape(owners_count, block_rows, nearby_count).astype(jnp.float32)
    )
    chosen = jnp.sum(slots * slot_hot[..., None], axis=2).reshape(owners_count * capacity, 2 * rank)
    total = chosen
    for step in range(1, lane_count):
        total = total + partner(chosen, "lane", step)

    rows = (jnp.concatenate(base_rows, axis=0).astype(jnp.float32) * base_gain).astype(jnp.bfloat16)
    base_q = jnp.dot(rows, query_weight, preferred_element_type=jnp.float32)
    base_k = jnp.dot(rows, key_weight, preferred_element_type=jnp.float32)
    base_v = jnp.dot(rows, value_weight, preferred_element_type=jnp.float32)

    low = total.astype(jnp.bfloat16).reshape(owners_count, capacity, 2 * rank)
    low = jnp.einsum(
        "bsr,bsg->brg", maps.astype(jnp.bfloat16), low, preferred_element_type=jnp.float32
    ).astype(jnp.bfloat16).reshape(owners_count * block_rows, 2 * rank)
    hot_low = hot.astype(jnp.bfloat16)
    low_q = (low[:, None, :rank] * hot_low[:, :, None]).reshape(-1, nearby_count * rank)
    low_v = (low[:, None, rank:] * hot_low[:, :, None]).reshape(-1, nearby_count * rank)
    base_q = base_q + ADAPTER_SCALE * jnp.dot(
        low_q, query_up_weight.reshape(-1, query_cols), preferred_element_type=jnp.float32
    )
    base_v = base_v + ADAPTER_SCALE * jnp.dot(
        low_v, value_up_weight.reshape(-1, kv_cols), preferred_element_type=jnp.float32
    )
    summand = jnp.concatenate([base_q, base_k, base_v], axis=1)
    summed = summand[:block_rows]
    for step in range(1, owners_count):
        part = summand[step * block_rows : (step + 1) * block_rows].astype(jnp.bfloat16)
        summed = summed + partner(part, "adapter", step).astype(jnp.float32)
    widened = residual_input.astype(jnp.float32)
    scaling = lax.rsqrt(jnp.mean(widened * widened, axis=-1, keepdims=True) + EPS)
    summed = summed * scaling

    queries = summed[:, :query_cols].astype(jnp.bfloat16)
    key_new = summed[:, query_cols : query_cols + kv_cols].astype(jnp.bfloat16)
    value_new = summed[:, query_cols + kv_cols :].astype(jnp.bfloat16)
    fresh_kv = jnp.stack([key_new, value_new], axis=1)
    kv_local = cached_key_rows.shape[1]
    head_dim = cached_key_rows.shape[3]
    context = cached_key_rows.shape[2]
    group_size = query_cols // head_dim // kv_local
    scale = head_dim ** (-0.5)
    grouped = queries.reshape(block_rows, kv_local, group_size, head_dim)
    key_heads = key_new.reshape(block_rows, kv_local, head_dim)
    value_heads = value_new.reshape(block_rows, kv_local, 1, head_dim).astype(jnp.float32)
    scores = (
        jnp.einsum("rkgd,rksd->rkgs", grouped, cached_key_rows, preferred_element_type=jnp.float32)
        * scale
    )
    own_score = (
        jnp.einsum("rkgd,rkd->rkg", grouped, key_heads, preferred_element_type=jnp.float32) * scale
    )
    visible = jnp.arange(context)[None, None, None, :] < cached_length[:, None, None, None]
    peak = jnp.maximum(jnp.max(jnp.where(visible, scores, -jnp.inf), axis=-1), own_score)
    lifted = jnp.where(visible, jnp.exp(scores - peak[..., None]), 0.0)
    own_lift = jnp.exp(own_score - peak)
    row_total = jnp.sum(lifted, axis=-1) + own_lift
    weights = (lifted / row_total[..., None]).astype(jnp.bfloat16)
    own_weight = (own_lift / row_total).astype(jnp.bfloat16)
    mixed = jnp.einsum(
        "rkgs,rksd->rkgd", weights, cached_value_rows, preferred_element_type=jnp.float32
    )
    mixed = mixed + own_weight.astype(jnp.float32)[..., None] * value_heads
    attended = mixed.reshape(block_rows, query_cols).astype(jnp.bfloat16)
    return (attended, fresh_kv)


def solution(mesh):
    in_specs = (
        P(("groups", "adapter"), None),
        P(),
        P("adapter", "lane"),
        P("adapter", "lane"),
        P("adapter", "lane"),
        P("adapter", "lane", None),
        P("adapter", None, "lane"),
        P("adapter", "lane", None),
        P("adapter", None, "lane"),
        P(("groups", "adapter"), "lane", None, None),
        P(("groups", "adapter"), "lane", None, None),
        P("groups"),
        P(("groups", "adapter")),
    )
    out_specs = (P(("groups", "adapter"), "lane"), P(("groups", "adapter"), None, "lane"))
    return jax.shard_map(
        on_device, mesh=mesh, in_specs=in_specs, out_specs=out_specs, check_vma=False
    )
```

time: 79.8 us -> 47.6 us (0.60)
  between operations: 14.3 us -> 0.98 us
  blocking collectives: 11.2 us -> 0 us
  waiting for transfers between devices: 15.5 us -> 10.5 us
  matrix products: 12.3 us -> 15 us
  other arithmetic: 6.24 us -> 4.08 us
  local copies, waits for them, and re-layouts: 6.28 us -> 4.32 us
  starting transfers between devices: 13.1 us -> 12.2 us
    all_to_all x3 -> x0, waiting for transfers between devices: 15.5 us -> none  [the longest x1 6.74 us: on_device(): lax.all_to_all(going_back, 'adapter', split_axis=0, concat_axis=0, tiled=...]
    all_to_all x3 -> x0, starting transfers between devices: 13.1 us -> none  [the longest x1 6.32 us: on_device(): lax.all_to_all(outgoing, 'adapter', split_axis=0, concat_axis=0, tiled=True)]
    ppermute x0 -> x9, starting transfers between devices: none -> 12.2 us  [partner(): return lax.ppermute(array, axis, [(i, i ^ step) for i in range(count)])]
    psum x1 -> x0, blocking collectives: 11.2 us -> none  [on_device(): rank_total = lax.psum((down_q_part, down_v_part), 'lane')]
    ppermute x0 -> x9, waiting for transfers between devices: none -> 10.5 us  [partner(): return lax.ppermute(array, axis, [(i, i ^ step) for i in range(count)])]
    convert_element_type x3 -> x1, other arithmetic: 1.88 us -> 0.08 us  [on_device(): hot_low = hot.astype(jnp.bfloat16)]
    dynamic_slice x0 -> x2, local copies, waits for them, and re-layouts: none -> 1.73 us  [the longest x1 0.95 us: on_device(): lax.dynamic_slice_in_dim(residual_input, other * base_width, base_width, 1)]
    dot_general x1, matrix products: 0.44 us -> 2.03 us  [on_device(): jnp.einsum('rkgs,rksd->rkgd', weights, cached_value_rows, preferred_eleme...]
  transfers between devices with their start and end apart: 4 -> 9, of which waited for: 3 -> 6; matrix products, arithmetic and copies ran while one was open for 9% -> 17% of each run, Pallas kernels for 0% -> 0%
where the time goes in v1:
time: 47.6 us; the launch traced here: 47.1 us
  matrix products  15 us (32%)
  starting transfers between devices  12.2 us (26%)
  waiting for transfers between devices  10.5 us (22%)
  local copies, waits for them, and re-layouts  4.32 us (9%)
  other arithmetic  4.08 us (9%)
  between operations  0.98 us (2%)
    ppermute x9, starting transfers between devices, partner(): return lax.ppermute(array, axis, [(i, i ^ step) for i in range(count)])  12.2 us
    ppermute x9, waiting for transfers between devices, partner(): return lax.ppermute(array, axis, [(i, i ^ step) for i in range(count)])  10.5 us
    dot_general x1, matrix products, on_device(): base_q = jnp.dot(rows, query_weight, preferred_element_type=jnp.float32)  4.99 us
    dot_general x4, matrix products, on_device(): jnp.dot(slot_map(mine, other).astype(jnp.bfloat16), lane_part, preferred_...  3.87 us
    dot_general x1, matrix products, on_device(): jnp.einsum('rkgs,rksd->rkgd', weights, cached_value_rows, preferred_eleme...  2.03 us
    dot_general x2, matrix products, on_device(): jnp.einsum('xi,yig->xyg', gained, weight, preferred_element_type=jnp.floa...  1.74 us
    another operation x9, other arithmetic  1.44 us
    unnamed x16, local copies, waits for them, and re-layouts  1.33 us
  transfers between devices with their start and end apart: 9, of which 6 were waited for; matrix products, arithmetic and copies ran while one was open for 17% of the time, Pallas kernels for 0%

profile of v1, /device:TPU:0, one launch (start us, length us, event | category | flops | bytes accessed | tf_op | source)
XLA Modules:
  0.0 47.1 jit_solution(12416498242084864224)
XLA Ops:
  0.7 0.9 %reshape.579 = s32[4,16]{1,0:T(4,128)S(1)} reshape(s32[64]{0:T(128)} %param.24) | data formatting | bytes 512 | tf_op jit(solution)/shard_map/reshape | solution.py:44
  1.6 0.2 reduce-window_clone.1
  1.8 1.0 %convolution_convert_fusion.3 = bf16[8,2048]{1,0:T(8,128)(2,1)S(1)} fusion(bf16[16,8192]{1,0:T(8,128)(2,1)} %param.13, s32[]{:T(128)S(6)} %select_n.99, s32[16]{0:T(128)S(1)} %subtract_bitcast_fusion.6, pred[16]{0:T(512)(128)(4,1)S(1)} %get-tuple-element.15), kind=kOutput, calls=%fused_computation.6 | convolution fusion | flops 540928 | bytes 98388 | tf_op jit(solution)/shard_map/dot_general | solution.py:57
  2.8 1.0 %constant_dynamic-slice_fusion.7 = (bf16[16,2048]{1,0:T(8,128)(2,1)S(1)}, bf16[16,2048]{1,0:T(8,128)(2,1)S(1)}, bf16[16,2048]{1,0:T(8,128)(2,1)S(1)}, bf16[16,2048]{1,0:T(8,128)(2,1)S(1)}) fusion(bf16[16,8192]{1,0:T(8,128)(2,1)} %param.13, s32[]{:T(128)S(6)} %select_n.95, s32[]{:T(128)S(6)} %select_n.100, s32[]{:T(128)S(6)} %select_n.96, s32[]{:T(128)S(6)} %select_n.101), kind=kLoop, calls=%fused_computation.92 | loop fusion | bytes 524304 | tf_op jit(solution)/shard_map/dynamic_slice | solution.py:56
  3.8 3.1 %collective-permute-start = (bf16[24,2048]{1,0:T(8,128)(2,1)S(1)}, bf16[24,2048]{1,0:T(8,128)(2,1)S(1)}, u32[]{:S(2)}, u32[]{:S(2)}) collective-permute-start(bf16[24,2048]{1,0:T(8,128)(2,1)S(1)} %pad_maximum_fusion.1), channel_id=1, source_target_pairs={{0,4},{4,0},{8,12},{12,8},{1,5},{5,1},{9,13},{13,9},{2,6},{6,2},{1... | collective-permute-start | bytes 294920 | tf_op jit(solution)/shard_map/ppermute | solution.py:12
  6.9 0.2 reduce-window_1_clone.1
  7.1 0.2 reduce-window_2_clone.1
  7.3 1.0 %convolution_convert_fusion.2 = bf16[8,2048]{1,0:T(8,128)(2,1)S(1)} fusion(bf16[16,8192]{1,0:T(8,128)(2,1)} %param.13, s32[]{:T(128)S(6)} %select_n.99, s32[16]{0:T(128)S(1)} %get-tuple-element.64, pred[16]{0:T(512)(128)(4,1)S(1)} %get-tuple-element.55), kind=kOutput, calls=%fused_computation.5 | convolution fusion | flops 540928 | bytes 98388 | tf_op jit(solution)/shard_map/dot_general | solution.py:57
  8.2 2.7 %collective-permute-start.1 = (bf16[24,2048]{1,0:T(8,128)(2,1)S(1)}, bf16[24,2048]{1,0:T(8,128)(2,1)S(1)}, u32[]{:S(2)}, u32[]{:S(2)}) collective-permute-start(bf16[24,2048]{1,0:T(8,128)(2,1)S(1)} %pad_maximum_fusion.2), channel_id=1, source_target_pairs={{0,8},{4,12},{8,0},{12,4},{1,9},{5,13},{9,1},{13,5},{2,10},{6,14},... | collective-permute-start | bytes 294920 | tf_op jit(solution)/shard_map/ppermute | solution.py:12
  10.9 1.0 %convolution_convert_fusion.1 = bf16[8,2048]{1,0:T(8,128)(2,1)S(1)} fusion(bf16[16,8192]{1,0:T(8,128)(2,1)} %param.13, s32[]{:T(128)S(6)} %select_n.99, s32[16]{0:T(128)S(1)} %get-tuple-element.63, pred[16]{0:T(512)(128)(4,1)S(1)} %get-tuple-element.53), kind=kOutput, calls=%fused_computation.4 | convolution fusion | flops 540928 | bytes 98388 | tf_op jit(solution)/shard_map/dot_general | solution.py:57
  12.0 1.1 %multiply_reduce_fusion = f32[16]{0:T(128)S(1)} fusion(bf16[16,8192]{1,0:T(8,128)(2,1)} %param.13), kind=kLoop, calls=%fused_computation.15 | loop fusion | flops 393200 | bytes 262208 | tf_op jit(solution)/shard_map/reduce_sum | solution.py:124
  13.1 0.2 reduce-window_3_clone.1
  13.4 0.1 fusion.69
  13.5 0.1 reshape.580
  13.6 0.2 reduce-window_4_clone.1
  13.7 0.2 reduce-window_6_clone.1
  13.9 0.2 reduce-window_5_clone.1
  14.1 1.0 %convolution_convert_fusion = bf16[8,2048]{1,0:T(8,128)(2,1)S(1)} fusion(bf16[16,8192]{1,0:T(8,128)(2,1)} %param.13, s32[]{:T(128)S(6)} %select_n.99, s32[16]{0:T(128)S(1)} %subtract_bitcast_fusion.3, pred[16]{0:T(512)(128)(4,1)S(1)} %get-tuple-element.42), kind=kOutput, calls=%fused_computation.3 | convolution fusion | flops 540928 | bytes 98388 | tf_op jit(solution)/shard_map/dot_general | solution.py:57
  15.1 0.1 fusion.31
  15.3 0.1 mul.132
  15.4 0.8 %iota_compare_fusion = pred[16,256]{1,0:T(8,128)(4,1)S(1)} fusion(s32[16]{0:T(128)} %param.25), kind=kLoop, calls=%fused_computation.55 | loop fusion | flops 4096 | bytes 4160 | tf_op jit(solution)/shard_map/lt | solution.py:146
  16.2 0.8 %fusion.71 = (f32[2048]{0:T(1024)S(1)}, f32[2048]{0:T(1024)S(1)}) fusion(f32[8192]{0:T(1024)} %param.14, s32[]{:T(128)S(6)} %select_n.99, s32[]{:T(128)S(6)} %select_n.95), kind=kLoop, calls=%fused_computation.159 | loop fusion | bytes 32776 | tf_op jit(solution)/shard_map/dynamic_slice | solution.py:72
  17.0 0.3 collective-permute-done.1
  17.3 1.1 %collective-permute-done.2 = bf16[24,2048]{1,0:T(8,128)(2,1)S(1)} collective-permute-done((bf16[24,2048]{1,0:T(8,128)(2,1)S(1)}, bf16[24,2048]{1,0:T(8,128)(2,1)S(1)}, u32[]{:S(2)}, u32[]{:S(2)}) %collective-permute-start.2) | collective-permute-done | bytes 98336 | tf_op jit(solution)/shard_map/ppermute | solution.py:12
  18.5 0.3 fusion.20
  18.8 1.4 %fusion.18 = f32[32,2,64]{2,0,1:T(8,128)S(1)} fusion(bf16[2,2048,64]{1,2,0:T(8,128)(2,1)} %param.20, bf16[8,2048]{1,0:T(8,128)(2,1)S(1)} %slice.71, bf16[8,2048]{1,0:T(8,128)(2,1)S(1)} %slice.70, bf16[8,2048]{1,0:T(8,128)(2,1)S(1)} %slice.69, bf16[8,2048]{1,0:T(8,128)(2,1)S(1)} %convolution_convert_fusion, f32[2048]{0:T(1024)S(1)} %get-tuple-element.34), kind=kOutput, calls=%fused_computation.41 | convolution fusion | flops 17432576 | bytes 679936 | tf_op jit(solution)/shard_map/xi,yig->xyg/dot_general | solution.py:80
  20.2 0.1 fusion.22
  20.4 1.6 %collective-permute-start.4 = (f32[32,128]{1,0:T(8,128)S(1)}, f32[32,128]{1,0:T(8,128)S(1)}, u32[]{:S(2)}, u32[]{:S(2)}) collective-permute-start(f32[32,128]{1,0:T(8,128)S(1)} %fusion.22), channel_id=1, source_target_pairs={{0,2},{1,3},{2,0},{3,1},{4,6},{5,7},{6,4},{7,5},{8,10},{9,11},{10,... | collective-permute-start | bytes 49160 | tf_op jit(solution)/shard_map/ppermute | solution.py:12
  22.0 0.3 collective-permute-start.5
  22.3 0.3 fusion.68
  22.6 0.3 fusion.67
  22.9 1.3 %collective-permute-done.4 = f32[32,128]{1,0:T(8,128)S(1)} collective-permute-done((f32[32,128]{1,0:T(8,128)S(1)}, f32[32,128]{1,0:T(8,128)S(1)}, u32[]{:S(2)}, u32[]{:S(2)}) %collective-permute-start.4) | collective-permute-done | bytes 16416 | tf_op jit(solution)/shard_map/ppermute | solution.py:12
  24.2 0.9 %collective-permute-done.5 = f32[32,128]{1,0:T(8,128)S(1)} collective-permute-done((f32[32,128]{1,0:T(8,128)S(1)}, f32[32,128]{1,0:T(8,128)S(1)}, u32[]{:S(2)}, u32[]{:S(2)}) %collective-permute-start.5) | collective-permute-done | bytes 16416 | tf_op jit(solution)/shard_map/ppermute | solution.py:12
  25.1 0.2 convolution_convert_fusion.4
  25.4 0.3 fusion
  25.8 5.0 %convolution_add_fusion = f32[64,2048]{1,0:T(8,128)S(1)} fusion(f32[64,2048]{1,0:T(8,128)S(1)} %fusion, bf16[2048,2048]{1,0:T(8,128)(2,1)} %param.15, bf16[16,2048]{1,0:T(8,128)(2,1)S(1)} %slice.68, bf16[16,2048]{1,0:T(8,128)(2,1)S(1)} %slice.67, bf16[16,2048]{1,0:T(8,128)(2,1)S(1)} %slice.66, bf16[16,2048]{1,0:T(8,128)(2,1)S(1)} %get-tuple-element.24, ...), kind=kOutput, calls=%fused_computation | convolution fusion | flops 538312704 | bytes 9707520 | tf_op jit(solution)/shard_map/dot_general | solution.py:101
  30.8 0.3 fusion.3
  31.1 1.8 %collective-permute-start.6 = (bf16[16,2560]{1,0:T(8,128)(2,1)S(1)}, bf16[16,2560]{1,0:T(8,128)(2,1)S(1)}, u32[]{:S(2)}, u32[]{:S(2)}) collective-permute-start(bf16[16,2560]{1,0:T(8,128)(2,1)S(1)} %get-tuple-element.21), channel_id=1, source_target_pairs={{0,4},{4,0},{8,12},{12,8},{1,5},{5,1},{9,13},{13,9},{2,6},{6,2},{1... | collective-permute-start | bytes 245768 | tf_op jit(solution)/shard_map/ppermute | solution.py:12
  32.9 1.5 %collective-permute-start.7 = (bf16[16,2560]{1,0:T(8,128)(2,1)S(1)}, bf16[16,2560]{1,0:T(8,128)(2,1)S(1)}, u32[]{:S(2)}, u32[]{:S(2)}) collective-permute-start(bf16[16,2560]{1,0:T(8,128)(2,1)S(1)} %get-tuple-element.23), channel_id=1, source_target_pairs={{0,8},{4,12},{8,0},{12,4},{1,9},{5,13},{9,1},{13,5},{2,10},{6,14},... | collective-permute-start | bytes 245768 | tf_op jit(solution)/shard_map/ppermute | solution.py:12
  34.5 1.1 %collective-permute-start.8 = (bf16[16,2560]{1,0:T(8,128)(2,1)S(1)}, bf16[16,2560]{1,0:T(8,128)(2,1)S(1)}, u32[]{:S(2)}, u32[]{:S(2)}) collective-permute-start(bf16[16,2560]{1,0:T(8,128)(2,1)S(1)} %get-tuple-element.22), channel_id=1, source_target_pairs={{0,12},{4,8},{8,4},{12,0},{1,13},{5,9},{9,5},{13,1},{2,14},{6,10},... | collective-permute-start | bytes 245768 | tf_op jit(solution)/shard_map/ppermute | solution.py:12
  35.6 0.1 collective-permute-done.6
  35.7 6.7 %collective-permute-done.7 = bf16[16,2560]{1,0:T(8,128)(2,1)S(1)} collective-permute-done((bf16[16,2560]{1,0:T(8,128)(2,1)S(1)}, bf16[16,2560]{1,0:T(8,128)(2,1)S(1)}, u32[]{:S(2)}, u32[]{:S(2)}) %collective-permute-start.7) | collective-permute-done | bytes 81952 | tf_op jit(solution)/shard_map/ppermute | solution.py:12
  42.6 0.6 %copy.17 = bf16[16,2,256]{2,1,0:T(2,128)(2,1)} copy(bf16[16,2,256]{2,0,1:T(8,128)(2,1)S(1)} %pad_maximum_fusion.4) | data formatting | bytes 32768
  43.2 0.1 fusion.73
  43.4 0.7 %select_reduce_fusion = (f32[16,2,8]{2,1,0:T(2,128)S(1)}, f32[16,2,8,256]{3,2,1,0:T(8,128)S(1)}) fusion(pred[16,256]{1,0:T(8,128)(4,1)S(1)} %iota_compare_fusion, bf16[16,2,8,128]{3,2,1,0:T(8,128)(2,1)S(1)} %bitcast.86, bf16[16,2,256,128]{3,2,1,0:T(8,128)(2,1)S(1)} %copy-done), kind=kOutput, calls=%fused_computation.19 | convolution fusion | flops 16973568 | bytes 2429952 | tf_op jit(solution)/shard_map/rkgd,rksd->rkgs/dot_general | solution.py:140
  44.1 0.2 fusion.4
  44.4 2.0 %fusion.1 = bf16[16,2,8,128]{3,2,1,0:T(8,128)(2,1)S(1)} fusion(bf16[16,2,256,128]{3,2,1,0:T(8,128)(2,1)} %param.23, f32[16,2,8,256]{3,2,1,0:T(8,128)S(1)} %get-tuple-element.58, f32[16,2,8]{2,1,0:T(2,128)S(1)} %get-tuple-element.33, f32[16,2,8]{2,1,0:T(2,128)S(1)} %multiply_maximum_fusion, pred[16,256]{1,0:T(8,128)(4,1)S(1)} %iota_compare_fusion, ...), kind=kOutput, calls=%fused_computation.9 | convolution fusion | flops 17137664 | bytes 2448384 | tf_op jit(solution)/shard_map/rkgs,rksd->rkgd/dot_general | solution.py:153
  46.5 0.7 %copy.25 = bf16[2,8,16,128]{3,1,2,0:T(8,128)(2,1)} copy(bf16[2,8,16,128]{3,2,1,0:T(8,128)(2,1)S(1)} %bitcast.91) | data formatting | bytes 131072
  (54 shorter events, 0.8 us)
Async XLA Ops:
  0.6 42.7 %copy-start = (bf16[16,2,256,128]{3,2,1,0:T(8,128)(2,1)S(1)}, bf16[16,2,256,128]{3,2,1,0:T(8,128)(2,1)}, u32[]{:S(2)}) copy-start(bf16[16,2,256,128]{3,2,1,0:T(8,128)(2,1)} %param.22) | copy-start | bytes 6291460
  0.6 17.8 %copy-start.5 = (bf16[2,2048,64]{1,2,0:T(8,128)(2,1)S(1)}, bf16[2,2048,64]{1,2,0:T(8,128)(2,1)}, u32[]{:S(2)}) copy-start(bf16[2,2048,64]{1,2,0:T(8,128)(2,1)} %param.18) | copy-start | bytes 1572868
  3.8 13.2 %collective-permute-start = (bf16[24,2048]{1,0:T(8,128)(2,1)S(1)}, bf16[24,2048]{1,0:T(8,128)(2,1)S(1)}, u32[]{:S(2)}, u32[]{:S(2)}) collective-permute-start(bf16[24,2048]{1,0:T(8,128)(2,1)S(1)} %pad_maximum_fusion.1), channel_id=1, source_target_pairs={{0,4},{4,0},{8,12},{12,8},{1,5},{5,1},{9,13},{13,9},{2,6},{6,2},{1... | collective-permute-start | bytes 294920 | tf_op jit(solution)/shard_map/ppermute | solution.py:12
  8.2 9.1 %collective-permute-start.1 = (bf16[24,2048]{1,0:T(8,128)(2,1)S(1)}, bf16[24,2048]{1,0:T(8,128)(2,1)S(1)}, u32[]{:S(2)}, u32[]{:S(2)}) collective-permute-start(bf16[24,2048]{1,0:T(8,128)(2,1)S(1)} %pad_maximum_fusion.2), channel_id=1, source_target_pairs={{0,8},{4,12},{8,0},{12,4},{1,9},{5,13},{9,1},{13,5},{2,10},{6,14},... | collective-permute-start | bytes 294920 | tf_op jit(solution)/shard_map/ppermute | solution.py:12
  11.9 6.6 %collective-permute-start.2 = (bf16[24,2048]{1,0:T(8,128)(2,1)S(1)}, bf16[24,2048]{1,0:T(8,128)(2,1)S(1)}, u32[]{:S(2)}, u32[]{:S(2)}) collective-permute-start(bf16[24,2048]{1,0:T(8,128)(2,1)S(1)} %pad_maximum_fusion.3), channel_id=1, source_target_pairs={{0,12},{4,8},{8,4},{12,0},{1,13},{5,9},{9,5},{13,1},{2,14},{6,10},... | collective-permute-start | bytes 294920 | tf_op jit(solution)/shard_map/ppermute | solution.py:12
  15.4 6.9 %copy-start.3 = (bf16[2048,256]{1,0:T(8,128)(2,1)S(1)}, bf16[2048,256]{1,0:T(8,128)(2,1)}, u32[]{:S(2)}) copy-start(bf16[2048,256]{1,0:T(8,128)(2,1)} %param.16) | copy-start | bytes 3145732
  17.0 5.6 %copy-start.4 = (bf16[2048,256]{1,0:T(8,128)(2,1)S(1)}, bf16[2048,256]{1,0:T(8,128)(2,1)}, u32[]{:S(2)}) copy-start(bf16[2048,256]{1,0:T(8,128)(2,1)} %param.17) | copy-start | bytes 3145732
  20.2 5.2 %copy-start.1 = (bf16[2,64,2048]{2,1,0:T(8,128)(2,1)S(1)}, bf16[2,64,2048]{2,1,0:T(8,128)(2,1)}, u32[]{:S(2)}) copy-start(bf16[2,64,2048]{2,1,0:T(8,128)(2,1)} %param.19) | copy-start | bytes 1572868
  20.3 2.6 %collective-permute-start.3 = (f32[32,128]{1,0:T(8,128)S(1)}, f32[32,128]{1,0:T(8,128)S(1)}, u32[]{:S(2)}, u32[]{:S(2)}) collective-permute-start(f32[32,128]{1,0:T(8,128)S(1)} %fusion.22), channel_id=1, source_target_pairs={{0,1},{1,0},{2,3},{3,2},{4,5},{5,4},{6,7},{7,6},{8,9},{9,8},{10,11... | collective-permute-start | bytes 49160 | tf_op jit(solution)/shard_map/ppermute | solution.py:12
  20.4 3.8 %collective-permute-start.4 = (f32[32,128]{1,0:T(8,128)S(1)}, f32[32,128]{1,0:T(8,128)S(1)}, u32[]{:S(2)}, u32[]{:S(2)}) collective-permute-start(f32[32,128]{1,0:T(8,128)S(1)} %fusion.22), channel_id=1, source_target_pairs={{0,2},{1,3},{2,0},{3,1},{4,6},{5,7},{6,4},{7,5},{8,10},{9,11},{10,... | collective-permute-start | bytes 49160 | tf_op jit(solution)/shard_map/ppermute | solution.py:12
  22.0 3.2 %collective-permute-start.5 = (f32[32,128]{1,0:T(8,128)S(1)}, f32[32,128]{1,0:T(8,128)S(1)}, u32[]{:S(2)}, u32[]{:S(2)}) collective-permute-start(f32[32,128]{1,0:T(8,128)S(1)} %fusion.22), channel_id=1, source_target_pairs={{0,3},{1,2},{2,1},{3,0},{4,7},{5,6},{6,5},{7,4},{8,11},{9,10},{10,... | collective-permute-start | bytes 49160 | tf_op jit(solution)/shard_map/ppermute | solution.py:12
  25.8 5.0 %copy-start.2 = (bf16[2,64,256]{2,1,0:T(8,128)(2,1)S(1)}, bf16[2,64,256]{2,1,0:T(8,128)(2,1)}, u32[]{:S(2)}) copy-start(bf16[2,64,256]{2,1,0:T(8,128)(2,1)} %param.21) | copy-start | bytes 196612
  31.1 4.6 %collective-permute-start.6 = (bf16[16,2560]{1,0:T(8,128)(2,1)S(1)}, bf16[16,2560]{1,0:T(8,128)(2,1)S(1)}, u32[]{:S(2)}, u32[]{:S(2)}) collective-permute-start(bf16[16,2560]{1,0:T(8,128)(2,1)S(1)} %get-tuple-element.21), channel_id=1, source_target_pairs={{0,4},{4,0},{8,12},{12,8},{1,5},{5,1},{9,13},{13,9},{2,6},{6,2},{1... | collective-permute-start | bytes 245768 | tf_op jit(solution)/shard_map/ppermute | solution.py:12
  32.9 9.5 %collective-permute-start.7 = (bf16[16,2560]{1,0:T(8,128)(2,1)S(1)}, bf16[16,2560]{1,0:T(8,128)(2,1)S(1)}, u32[]{:S(2)}, u32[]{:S(2)}) collective-permute-start(bf16[16,2560]{1,0:T(8,128)(2,1)S(1)} %get-tuple-element.23), channel_id=1, source_target_pairs={{0,8},{4,12},{8,0},{12,4},{1,9},{5,13},{9,1},{13,5},{2,10},{6,14},... | collective-permute-start | bytes 245768 | tf_op jit(solution)/shard_map/ppermute | solution.py:12
  34.5 7.9 %collective-permute-start.8 = (bf16[16,2560]{1,0:T(8,128)(2,1)S(1)}, bf16[16,2560]{1,0:T(8,128)(2,1)S(1)}, u32[]{:S(2)}, u32[]{:S(2)}) collective-permute-start(bf16[16,2560]{1,0:T(8,128)(2,1)S(1)} %get-tuple-element.22), channel_id=1, source_target_pairs={{0,12},{4,8},{8,4},{12,0},{1,13},{5,9},{9,5},{13,1},{2,14},{6,10},... | collective-permute-start | bytes 245768 | tf_op jit(solution)/shard_map/ppermute | solution.py:12

commit v2 on v0

v2 whole, which is shorter than its diff:
```python
import jax
import jax.numpy as jnp
from jax import lax
from jax.experimental import pallas as pl
from jax.experimental.pallas import tpu as pltpu
from jax.sharding import PartitionSpec as P

EPS = 1e-05
ADAPTER_SCALE = 0.5
MIB = 2**20
F32 = jnp.float32
BF16 = jnp.bfloat16
VMEM = pl.BlockSpec(memory_space=pltpu.VMEM)
SMEM = pl.BlockSpec(memory_space=pltpu.SMEM)
HBM = pl.BlockSpec(memory_space=pltpu.HBM)


def partner(array, axis, step):
    count = lax.axis_size(axis)
    return lax.ppermute(array, axis, [(i, i ^ step) for i in range(count)])


def call(body, name, outs, in_specs, out_specs, args, scratch=(), limit=16, flops=0, moved=0):
    return pl.pallas_call(
        body,
        name=name,
        out_shape=outs,
        in_specs=in_specs,
        out_specs=out_specs,
        scratch_shapes=scratch,
        compiler_params=pltpu.CompilerParams(vmem_limit_bytes=limit * MIB),
        cost_estimate=pl.CostEstimate(flops=flops, bytes_accessed=moved, transcendentals=0),
    )(*args)


def iota(shape, axis):
    return lax.broadcasted_iota(jnp.int32, shape, axis)


def slot_map(ids, owner, block, capacity, block_rows, nearby):
    slots, rows = owner.shape[0], ids.shape[1]
    first = owner * nearby
    spot = iota((slots, rows), 1)
    hit = (ids >= first) & (ids < first + nearby)
    hit = hit & (spot >= block * block_rows) & (spot < (block + 1) * block_rows)
    before = (iota((rows, rows), 0) < iota((rows, rows), 1)).astype(BF16)
    place = jnp.dot(
        jnp.where(hit, 1.0, 0.0).astype(BF16), before, preferred_element_type=F32
    )
    which = lax.rem(iota((slots, rows), 0), capacity).astype(F32)
    return jnp.where(hit & (place == which), 1.0, 0.0)


def on_device(
    residual_input,
    attention_norm_gain,
    query_weight,
    key_weight,
    value_weight,
    query_down_weight,
    query_up_weight,
    value_down_weight,
    value_up_weight,
    cached_key_rows,
    cached_value_rows,
    row_adapter_index,
    cached_length,
):
    owners_count = lax.axis_size("adapter")
    lane_count = lax.axis_size("lane")
    block_rows, width = residual_input.shape
    nearby, _, rank = query_down_weight.shape
    capacity = max(2, 2 * block_rows // owners_count)
    lane_width = width // lane_count
    base_width = width // owners_count
    query_cols = query_weight.shape[1]
    kv_cols = key_weight.shape[1]
    all_cols = query_cols + 2 * kv_cols
    slots = owners_count * capacity
    rows = owners_count * block_rows
    low_cols = nearby * rank
    joined = base_width == lane_width
    kv_local, context, head_dim = cached_key_rows.shape[1:]
    group_size = query_cols // head_dim // kv_local
    heads = kv_local * group_size

    ids = row_adapter_index.reshape(1, rows)
    gain = attention_norm_gain.reshape(1, width)
    query_down = jnp.swapaxes(query_down_weight, 1, 2).reshape(low_cols, lane_width)
    value_down = jnp.swapaxes(value_down_weight, 1, 2).reshape(low_cols, lane_width)
    query_up = query_up_weight.reshape(low_cols, query_cols)
    value_up = value_up_weight.reshape(low_cols, kv_cols)

    def prepare(ids_ref, x_ref, *out_refs):
        me = lax.axis_index("adapter")
        lane = lax.axis_index("lane")
        owner = jnp.bitwise_xor(me, iota((slots, 1), 0) // capacity)
        chosen = slot_map(
            ids_ref[...], owner, jnp.full((slots, 1), me), capacity, block_rows, nearby
        )
        fold = lax.rem(iota((rows, block_rows), 0), block_rows) == iota((rows, block_rows), 1)
        chosen = jnp.dot(
            chosen.astype(BF16), jnp.where(fold, 1.0, 0.0).astype(BF16), preferred_element_type=F32
        )
        part = x_ref[:, pl.ds(pl.multiple_of(lane * lane_width, lane_width), lane_width)]
        placed = jnp.dot(chosen.astype(BF16), part, preferred_element_type=F32)
        for step in range(owners_count):
            other = jnp.bitwise_xor(me, step)
            base = x_ref[:, pl.ds(pl.multiple_of(other * base_width, base_width), base_width)]
            mine = placed[step * capacity : (step + 1) * capacity].astype(BF16)
            if joined:
                out_refs[step][...] = jnp.concatenate([base, mine], axis=0)
            else:
                out_refs[2 * step][...] = base
                out_refs[2 * step + 1][...] = mine

    if joined:
        shapes = [jax.ShapeDtypeStruct((block_rows + capacity, base_width), BF16)] * owners_count
    else:
        shapes = [
            jax.ShapeDtypeStruct((block_rows, base_width), BF16),
            jax.ShapeDtypeStruct((capacity, lane_width), BF16),
        ] * owners_count
    sent = call(
        prepare, "prepare", shapes, [VMEM] * 2, [VMEM] * len(shapes), (ids, residual_input),
        moved=2**19,
    )
    per = len(sent) // owners_count
    arrived = list(sent[:per])
    for step in range(1, owners_count):
        for piece in sent[per * step : per * (step + 1)]:
            arrived.append(partner(piece, "adapter", step))

    held = (
        query_weight, key_weight, value_weight, query_down, value_down, query_up, value_up,
        cached_key_rows, cached_value_rows,
    )

    def fetch(x_ref, *refs):
        sources, targets, rms_ref, sems = refs[: len(held)], refs[len(held) : -2], refs[-2], refs[-1]
        copies = [
            pltpu.make_async_copy(source, target, sems.at[i])
            for i, (source, target) in enumerate(zip(sources, targets))
        ]
        for copy in copies:
            copy.start()
        x = x_ref[...].astype(F32)
        mean = jnp.sum(x * x, axis=1, keepdims=True) * (1.0 / width)
        rms_ref[...] = jnp.broadcast_to(lax.rsqrt(mean + EPS), rms_ref.shape)
        for copy in copies:
            copy.wait()

    fetched = call(
        fetch,
        "fetch",
        [pltpu.VMEM(a.shape, a.dtype) for a in held]
        + [jax.ShapeDtypeStruct((block_rows, 128), F32)],
        [VMEM] + [HBM] * len(held),
        [VMEM] * (len(held) + 1),
        (residual_input, *(pltpu.with_memory_space_constraint(a, pltpu.HBM) for a in held)),
        scratch=[pltpu.SemaphoreType.DMA((len(held),))],
        moved=16 * MIB,
    )
    (w_query, w_key, w_value, w_query_down, w_value_down, w_query_up, w_value_up,
     keys, values, row_scale) = fetched

    def base_of(refs, step):
        return refs[step][:block_rows, :] if joined else refs[2 * step][...]

    def slots_of(refs, step):
        return refs[step][block_rows:, :] if joined else refs[2 * step + 1][...]

    def lower(gain_ref, dq_ref, dv_ref, *refs):
        part_refs, out_ref = refs[:-1], refs[-1]
        lane = lax.axis_index("lane")
        scaled = gain_ref[:, pl.ds(pl.multiple_of(lane * lane_width, lane_width), lane_width)]
        taken = jnp.concatenate(
            [slots_of(part_refs, step).astype(F32) for step in range(owners_count)], axis=0
        )
        taken = (taken * scaled).astype(BF16)
        contract = (((1,), (1,)), ((), ()))
        out_ref[:, :low_cols] = lax.dot_general(
            taken, dq_ref[...], contract, preferred_element_type=F32
        )
        out_ref[:, low_cols:] = lax.dot_general(
            taken, dv_ref[...], contract, preferred_element_type=F32
        )

    low = call(
        lower, "lower", jax.ShapeDtypeStruct((slots, 2 * low_cols), F32),
        [VMEM] * (3 + len(arrived)), VMEM, (gain, w_query_down, w_value_down, *arrived), moved=MIB,
    )
    lows = [low] + [partner(low, "lane", step) for step in range(1, lane_count)]

    def project(gain_ref, wq_ref, wk_ref, wv_ref, *refs):
        part_refs, out_ref, x_ref = refs[:-2], refs[-2], refs[-1]
        me = lax.axis_index("adapter")
        scaled = gain_ref[:, pl.ds(pl.multiple_of(me * base_width, base_width), base_width)]
        for step in range(owners_count):
            start = pl.multiple_of(jnp.bitwise_xor(me, step) * block_rows, block_rows)
            x_ref[pl.ds(start, block_rows), :] = (
                base_of(part_refs, step).astype(F32) * scaled
            ).astype(BF16)
        tile = min(1024, query_cols)
        for at in range(0, query_cols, tile):
            out_ref[:, at : at + tile] = jnp.dot(
                x_ref[...], wq_ref[:, at : at + tile], preferred_element_type=F32
            )
        out_ref[:, query_cols : query_cols + kv_cols] = jnp.dot(
            x_ref[...], wk_ref[...], preferred_element_type=F32
        )
        out_ref[:, query_cols + kv_cols :] = jnp.dot(
            x_ref[...], wv_ref[...], preferred_element_type=F32
        )

    based = call(
        project, "project", jax.ShapeDtypeStruct((rows, all_cols), F32),
        [VMEM] * (4 + len(arrived)), VMEM, (gain, w_query, w_key, w_value, *arrived),
        scratch=[pltpu.VMEM((rows, base_width), BF16)],
        flops=2 * rows * base_width * all_cols, moved=10 * MIB,
    )

    def raise_up(ids_ref, based_ref, uq_ref, uv_ref, *refs):
        low_refs, out_refs, sum_ref = refs[:lane_count], refs[lane_count:-1], refs[-1]
        me = lax.axis_index("adapter")
        block = jnp.bitwise_xor(me, iota((slots, 1), 0) // capacity)
        seen = slot_map(
            ids_ref[...], jnp.full((slots, 1), me), block, capacity, block_rows, nearby
        )
        total = low_refs[0][...]
        for ref in low_refs[1:]:
            total = total + ref[...]
        column = lax.rem(iota((slots, 2 * low_cols), 1) // rank, nearby)
        picked = jnp.zeros_like(total)
        for near in range(nearby):
            uses = jnp.where(ids_ref[...] == me * nearby + near, seen, 0.0)
            uses = jnp.sum(uses, axis=1, keepdims=True) > 0.5
            picked = jnp.where(uses & (column == near), total, picked)
        lowered = lax.dot_general(
            seen.astype(BF16), picked.astype(BF16), (((0,), (0,)), ((), ())),
            preferred_element_type=F32,
        ).astype(BF16)
        for at in range(0, query_cols, 1024):
            stop = min(at + 1024, query_cols)
            sum_ref[:, at:stop] = based_ref[:, at:stop] + ADAPTER_SCALE * jnp.dot(
                lowered[:, :low_cols], uq_ref[:, at:stop], preferred_element_type=F32
            )
        middle = slice(query_cols, query_cols + kv_cols)
        last = slice(query_cols + kv_cols, all_cols)
        sum_ref[:, middle] = based_ref[:, middle]
        sum_ref[:, last] = based_ref[:, last] + ADAPTER_SCALE * jnp.dot(
            lowered[:, low_cols:], uv_ref[...], preferred_element_type=F32
        )
        for step in range(owners_count):
            start = pl.multiple_of(jnp.bitwise_xor(me, step) * block_rows, block_rows)
            out_refs[step][...] = sum_ref[pl.ds(start, block_rows), :].astype(out_refs[step].dtype)

    parts = call(
        raise_up, "raise_up",
        [
            jax.ShapeDtypeStruct((block_rows, all_cols), BF16 if step else F32)
            for step in range(owners_count)
        ],
        [VMEM] * (4 + lane_count), [VMEM] * owners_count,
        (ids, based, w_query_up, w_value_up, *lows),
        scratch=[pltpu.VMEM((rows, all_cols), F32)],
    )
    parts = [parts[0]] + [
        partner(parts[step], "adapter", step) for step in range(1, owners_count)
    ]

    def finish(length_ref, scale_ref, k_ref, v_ref, *refs):
        part_refs = refs[:owners_count]
        out_ref, fresh_ref, sum_ref, q_ref, s_ref, o_ref = refs[owners_count:]
        summed = part_refs[0][...]
        for ref in part_refs[1:]:
            summed = summed + ref[...].astype(F32)
        summed = (summed * scale_ref[:, :1]).astype(BF16)
        key_new = summed[:, query_cols : query_cols + kv_cols]
        value_new = summed[:, query_cols + kv_cols :]
        fresh_ref[:, :kv_cols] = key_new
        fresh_ref[:, kv_cols:] = value_new
        sum_ref[...] = summed.astype(F32)
        for head in range(heads):
            q_ref[:, head, :] = sum_ref[:, head * head_dim : (head + 1) * head_dim]
        scale = head_dim ** (-0.5)
        spot = iota((group_size, context), 1)
        own = []
        for row in range(block_rows):
            for group in range(kv_local):
                asked = q_ref[row, group * group_size : (group + 1) * group_size, :]
                scores = lax.dot_general(
                    asked.astype(BF16), k_ref[row, group], (((1,), (1,)), ((), ())),
                    preferred_element_type=F32,
                )
                s_ref[row * kv_local + group] = jnp.where(
                    spot < length_ref[row], scores * scale, -jnp.inf
                )
                at = query_cols + group * head_dim
                new = sum_ref[row : row + 1, at : at + head_dim]
                own.append(jnp.sum(asked * new, axis=1, keepdims=True))
        own_score = jnp.stack(own) * scale
        scores = s_ref[...]
        peak = jnp.maximum(jnp.max(scores, axis=2, keepdims=True), own_score)
        lifted = jnp.exp(scores - peak)
        own_lift = jnp.exp(own_score - peak)
        inverse = 1.0 / (jnp.sum(lifted, axis=2, keepdims=True) + own_lift)
        s_ref[...] = lifted * inverse
        own_weight = (own_lift * inverse).astype(BF16).astype(F32)
        for row in range(block_rows):
            for group in range(kv_local):
                index = row * kv_local + group
                mixed = jnp.dot(
                    s_ref[index].astype(BF16), v_ref[row, group], preferred_element_type=F32
                )
                at = query_cols + kv_cols + group * head_dim
                new = sum_ref[row : row + 1, at : at + head_dim]
                o_ref[row, group * group_size : (group + 1) * group_size, :] = (
                    mixed + own_weight[index] * new
                )
        for head in range(heads):
            out_ref[:, head * head_dim : (head + 1) * head_dim] = o_ref[:, head, :].astype(BF16)

    attended, fresh = call(
        finish, "finish",
        [
            jax.ShapeDtypeStruct((block_rows, query_cols), BF16),
            jax.ShapeDtypeStruct((block_rows, 2 * kv_cols), BF16),
        ],
        [SMEM] + [VMEM] * (3 + owners_count), [VMEM] * 2,
        (cached_length, row_scale, keys, values, *parts),
        scratch=[
            pltpu.VMEM((block_rows, all_cols), F32),
            pltpu.VMEM((block_rows, heads, head_dim), F32),
            pltpu.VMEM((block_rows * kv_local, group_size, context), F32),
            pltpu.VMEM((block_rows, heads, head_dim), F32),
        ],
    )
    return (attended, fresh.reshape(block_rows, 2, kv_cols))


def solution(mesh):
    in_specs = (
        P(("groups", "adapter"), None),
        P(),
        P("adapter", "lane"),
        P("adapter", "lane"),
        P("adapter", "lane"),
        P("adapter", "lane", None),
        P("adapter", None, "lane"),
        P("adapter", "lane", None),
        P("adapter", None, "lane"),
        P(("groups", "adapter"), "lane", None, None),
        P(("groups", "adapter"), "lane", None, None),
        P("groups"),
        P(("groups", "adapter")),
    )
    out_specs = (P(("groups", "adapter"), "lane"), P(("groups", "adapter"), None, "lane"))
    return jax.shard_map(
        on_device, mesh=mesh, in_specs=in_specs, out_specs=out_specs, check_vma=False
    )
```

time: 79.8 us -> 35.9 us (0.45)
  between operations: 14.3 us -> 0.71 us
  matrix products: 12.3 us -> 0 us
  Pallas kernels: 0 us -> 11.9 us
  blocking collectives: 11.2 us -> 0 us
  waiting for transfers between devices: 15.5 us -> 8.96 us
  other arithmetic: 6.24 us -> 0 us
  local copies, waits for them, and re-layouts: 6.28 us -> 2.22 us
  starting transfers between devices: 13.1 us -> 12 us
    all_to_all x3 -> x0, waiting for transfers between devices: 15.5 us -> none  [the longest x1 6.74 us: on_device(): lax.all_to_all(going_back, 'adapter', split_axis=0, concat_axis=0, tiled=...]
    all_to_all x3 -> x0, starting transfers between devices: 13.1 us -> none  [the longest x1 6.32 us: on_device(): lax.all_to_all(outgoing, 'adapter', split_axis=0, concat_axis=0, tiled=True)]
    dot_general x14 -> x0, matrix products: 12.3 us -> none  [the longest x1 5.09 us: on_device(): jnp.dot(full_rows, query_weight, preferred_element_type=jnp.float32)]
    ppermute x0 -> x9, starting transfers between devices: none -> 12 us  [partner(): return lax.ppermute(array, axis, [(i, i ^ step) for i in range(count)])]
    pallas_call x0 -> x6, Pallas kernels: none -> 11.9 us  [call(): pl.pallas_call(body, name=name, out_shape=outs, in_specs=in_specs, out_sp...]
    psum x1 -> x0, blocking collectives: 11.2 us -> none  [on_device(): rank_total = lax.psum((down_q_part, down_v_part), 'lane')]
    ppermute x0 -> x9, waiting for transfers between devices: none -> 8.96 us  [partner(): return lax.ppermute(array, axis, [(i, i ^ step) for i in range(count)])]
    convert_element_type x4 -> x0, other arithmetic: 1.92 us -> none  [the longest x1 1.08 us: on_device(): normalized_input = (widened * lax.rsqrt(jnp.mean(widened * widened, axis=...]
  transfers between devices with their start and end apart: 4 -> 9, of which waited for: 3 -> 4; matrix products, arithmetic and copies ran while one was open for 9% -> 0% of each run, Pallas kernels for 0% -> 22%
where the time goes in v2:
time: 35.9 us; the launch traced here: 35.7 us
  starting transfers between devices  12 us (33%)
  Pallas kernels  11.9 us (33%)
  waiting for transfers between devices  8.96 us (25%)
  local copies, waits for them, and re-layouts  2.22 us (6%)
  between operations  0.71 us (2%)
    ppermute x9, starting transfers between devices, partner(): return lax.ppermute(array, axis, [(i, i ^ step) for i in range(count)])  12 us
    pallas_call x6, Pallas kernels, call(): pl.pallas_call(body, name=name, out_shape=outs, in_specs=in_specs, out_sp...  11.9 us
    ppermute x9, waiting for transfers between devices, partner(): return lax.ppermute(array, axis, [(i, i ^ step) for i in range(count)])  8.96 us
    unnamed x10, local copies, waits for them, and re-layouts  1.61 us
  transfers between devices with their start and end apart: 9, of which 4 were waited for; matrix products, arithmetic and copies ran while one was open for 0% of the time, Pallas kernels for 22%

profile of v2, /device:TPU:0, one launch (start us, length us, event | category | flops | bytes accessed | tf_op | source)
XLA Modules:
  0.0 35.7 jit_solution(5161357317986867186)
XLA Ops:
  0.6 0.0 copy-start
  0.6 0.9 %copy-done = bf16[16,8192]{1,0:T(8,128)(2,1)S(1)} copy-done((bf16[16,8192]{1,0:T(8,128)(2,1)S(1)}, bf16[16,8192]{1,0:T(8,128)(2,1)}, u32[]{:S(2)}) %copy-start) | copy-done | bytes 262168
  1.6 0.0 copy-start.2
  1.6 0.7 %copy-done.2 = s32[64]{0:T(128)S(1)} copy-done((s32[64]{0:T(128)S(1)}, s32[64]{0:T(128)}, u32[]{:S(2)}) %copy-start.2) | copy-done | bytes 280
  2.2 0.4 %prepare.1 = (bf16[24,2048]{1,0:T(8,128)(2,1)S(1)}, bf16[24,2048]{1,0:T(8,128)(2,1)S(1)}, bf16[24,2048]{1,0:T(8,128)(2,1)S(1)}, bf16[24,2048]{1,0:T(8,128)(2,1)S(1)}) custom-call(s32[1,64]{1,0:T(1,128)S(1)} %bitcast.12, bf16[16,8192]{1,0:T(8,128)(2,1)S(1)} %copy-done), custom_call_target="tpu_custom_call" | custom-call | bytes 524288 | tf_op jit(solution)/shard_map/prepare/pallas_call | solution.py:24
  2.7 3.1 %collective-permute-start = (bf16[24,2048]{1,0:T(8,128)(2,1)S(1)}, bf16[24,2048]{1,0:T(8,128)(2,1)S(1)}, u32[]{:S(2)}, u32[]{:S(2)}) collective-permute-start(bf16[24,2048]{1,0:T(8,128)(2,1)S(1)} %get-tuple-element.29), channel_id=1, source_target_pairs={{0,4},{4,0},{8,12},{12,8},{1,5},{5,1},{9,13},{13,9},{2,6},{6,2},{1... | collective-permute-start | bytes 294920 | tf_op jit(solution)/shard_map/ppermute | solution.py:20
  5.7 2.6 %collective-permute-start.1 = (bf16[24,2048]{1,0:T(8,128)(2,1)S(1)}, bf16[24,2048]{1,0:T(8,128)(2,1)S(1)}, u32[]{:S(2)}, u32[]{:S(2)}) collective-permute-start(bf16[24,2048]{1,0:T(8,128)(2,1)S(1)} %get-tuple-element.30), channel_id=1, source_target_pairs={{0,8},{4,12},{8,0},{12,4},{1,9},{5,13},{9,1},{13,5},{2,10},{6,14},... | collective-permute-start | bytes 294920 | tf_op jit(solution)/shard_map/ppermute | solution.py:20
  8.3 0.0 collective-permute-start.2
  8.3 0.0 copy-start.1
  8.3 5.8 %fetch.1 = (bf16[2048,2048]{1,0:T(8,128)(2,1)S(1)}, bf16[2048,256]{1,0:T(8,128)(2,1)S(1)}, bf16[2048,256]{1,0:T(8,128)(2,1)S(1)}, bf16[128,2048]{1,0:T(8,128)(2,...) custom-call(bf16[16,8192]{1,0:T(8,128)(2,1)S(1)} %copy-done, ...), custom_call_target="tpu_custom_call" | custom-call | bytes 16777216 | tf_op jit(solution)/shard_map/fetch/pallas_call | solution.py:24
  14.1 0.0 collective-permute-done.refs_1_
  14.1 2.0 %collective-permute-done.1.refs_2_ = bf16[24,2048]{1,0:T(8,128)(2,1)S(1)} collective-permute-done((bf16[24,2048]{1,0:T(8,128)(2,1)S(1)}, bf16[24,2048]{1,0:T(8,128)(2,1)S(1)}, u32[]{:S(2)}, u32[]{:S(2)}) %collective-permute-start.1) | collective-permute-done | bytes 98336 | tf_op jit(solution)/shard_map/ppermute | solution.py:20
  16.2 0.0 collective-permute-done.2.refs_3_
  16.2 0.0 copy-done.1
  16.2 0.4 %lower.1.refs_0_ = f32[32,256]{1,0:T(8,128)S(1)} custom-call(f32[1,8192]{1,0:T(1,128)S(1)} %bitcast.10, bf16[128,2048]{1,0:T(8,128)(2,1)S(1)} %get-tuple-element.34.dq_ref, bf16[128,2048]{1,0:T(8,128)(2,1)S(1)} %get-tuple-element.35.dv_ref, bf16[24,2048]{1,0:T(8,128)(2,1)S(1)} %get-tuple-element.28.refs_0_, ...), custom_call_target="tpu_custom_call" | custom-call | bytes 1048576 | tf_op jit(solution)/shard_map/lower/pallas_call | solution.py:24
  16.6 0.0 collective-permute-start.5
  16.6 1.6 %collective-permute-start.4 = (f32[32,256]{1,0:T(8,128)S(1)}, f32[32,256]{1,0:T(8,128)S(1)}, u32[]{:S(2)}, u32[]{:S(2)}) collective-permute-start(f32[32,256]{1,0:T(8,128)S(1)} %lower.1.refs_0_), channel_id=1, source_target_pairs={{0,2},{1,3},{2,0},{3,1},{4,6},{5,7},{6,4},{7,5},{8,10},{9,11},{10,... | collective-permute-start | bytes 98312 | tf_op jit(solution)/shard_map/ppermute | solution.py:20
  18.2 0.3 collective-permute-start.3
  18.5 0.0 copy-start.3
  18.5 0.0 copy-start.4
  18.5 2.0 %project.1.based_ref = f32[64,2560]{1,0:T(8,128)S(1)} custom-call(f32[1,8192]{1,0:T(1,128)S(1)} %bitcast.11, bf16[2048,2048]{1,0:T(8,128)(2,1)S(1)} %get-tuple-element.25.wq_ref, bf16[2048,256]{1,0:T(8,128)(2,1)S(1)} %get-tuple-element.26.wk_ref, bf16[2048,256]{1,0:T(8,128)(2,1)S(1)} %get-tuple-element.27.wv_ref, ...), custom_call_target="tpu_custom_call" | custom-call | flops 671088640 | bytes 10485760 | tf_op jit(solution)/shard_map/project/pallas_call | solution.py:24
  20.5 0.0 collective-permute-done.5.refs_3_
  20.5 0.2 collective-permute-done.4.refs_2_
  20.7 0.0 collective-permute-done.3.refs_1_
  20.7 0.0 copy-done.3
  20.7 0.6 %raise_up.1 = (f32[16,2560]{1,0:T(8,128)S(1)}, bf16[16,2560]{1,0:T(8,128)(2,1)S(1)}, bf16[16,2560]{1,0:T(8,128)(2,1)S(1)}, bf16[16,2560]{1,0:T(8,128)(2,1)S(1)}) custom-call(s32[1,64]{1,0:T(1,128)S(1)} %bitcast.13, f32[64,2560]{1,0:T(8,128)S(1)} %project.1.based_ref, bf16[128,2048]{1,0:T(8,128)(2,1)S(1)} %get-tuple-element.32.uq_ref, ...), custom_call_target="tpu_custom_call" | custom-call | tf_op jit(solution)/shard_map/raise_up/pallas_call | solution.py:24
  21.3 1.7 %collective-permute-start.6 = (bf16[16,2560]{1,0:T(8,128)(2,1)S(1)}, bf16[16,2560]{1,0:T(8,128)(2,1)S(1)}, u32[]{:S(2)}, u32[]{:S(2)}) collective-permute-start(bf16[16,2560]{1,0:T(8,128)(2,1)S(1)} %get-tuple-element.37), channel_id=1, source_target_pairs={{0,4},{4,0},{8,12},{12,8},{1,5},{5,1},{9,13},{13,9},{2,6},{6,2},{1... | collective-permute-start | bytes 245768 | tf_op jit(solution)/shard_map/ppermute | solution.py:20
  23.0 1.4 %collective-permute-start.7 = (bf16[16,2560]{1,0:T(8,128)(2,1)S(1)}, bf16[16,2560]{1,0:T(8,128)(2,1)S(1)}, u32[]{:S(2)}, u32[]{:S(2)}) collective-permute-start(bf16[16,2560]{1,0:T(8,128)(2,1)S(1)} %get-tuple-element.38), channel_id=1, source_target_pairs={{0,8},{4,12},{8,0},{12,4},{1,9},{5,13},{9,1},{13,5},{2,10},{6,14},... | collective-permute-start | bytes 245768 | tf_op jit(solution)/shard_map/ppermute | solution.py:20
  24.4 1.3 %collective-permute-start.8 = (bf16[16,2560]{1,0:T(8,128)(2,1)S(1)}, bf16[16,2560]{1,0:T(8,128)(2,1)S(1)}, u32[]{:S(2)}, u32[]{:S(2)}) collective-permute-start(bf16[16,2560]{1,0:T(8,128)(2,1)S(1)} %get-tuple-element.39), channel_id=1, source_target_pairs={{0,12},{4,8},{8,4},{12,0},{1,13},{5,9},{9,5},{13,1},{2,14},{6,10},... | collective-permute-start | bytes 245768 | tf_op jit(solution)/shard_map/ppermute | solution.py:20
  25.7 0.3 collective-permute-done.6.refs_1_
  26.0 6.4 %collective-permute-done.7.refs_2_ = bf16[16,2560]{1,0:T(8,128)(2,1)S(1)} collective-permute-done((bf16[16,2560]{1,0:T(8,128)(2,1)S(1)}, bf16[16,2560]{1,0:T(8,128)(2,1)S(1)}, u32[]{:S(2)}, u32[]{:S(2)}) %collective-permute-start.7) | collective-permute-done | bytes 81952 | tf_op jit(solution)/shard_map/ppermute | solution.py:20
  32.5 0.0 collective-permute-done.8.refs_3_
  32.5 0.0 copy-done.4
  32.5 2.6 %finish.1 = (bf16[16,2048]{1,0:T(8,128)(2,1)}, bf16[16,512]{1,0:T(8,128)(2,1)S(1)}) custom-call(s32[16]{0:T(128)S(1)} %copy-done.4, f32[16,128]{1,0:T(8,128)S(1)} %get-tuple-element.22.scale_ref, bf16[16,2,256,128]{3,2,1,0:T(8,128)(2,1)S(1)} %get-tuple-element.23.k_ref, bf16[16,2,256,128]{3,2,1,0:T(8,128)(2,1)S(1)} %get-tuple-element.24.v_ref, ...), custom_call_target="tpu_custom_call" | custom-call | tf_op jit(solution)/shard_map/finish/pallas_call | solution.py:24
  35.1 0.6 %reshape.31 = bf16[16,2,256]{2,1,0:T(2,128)(2,1)} reshape(bf16[16,512]{1,0:T(8,128)(2,1)S(1)} %get-tuple-element.41) | data formatting | bytes 32768 | tf_op jit(solution)/shard_map/reshape | solution.py:339
Async XLA Ops:
  0.6 1.0 %copy-start = (bf16[16,8192]{1,0:T(8,128)(2,1)S(1)}, bf16[16,8192]{1,0:T(8,128)(2,1)}, u32[]{:S(2)}) copy-start(bf16[16,8192]{1,0:T(8,128)(2,1)} %x_ref.3) | copy-start | bytes 786436
  1.6 0.7 %copy-start.2 = (s32[64]{0:T(128)S(1)}, s32[64]{0:T(128)}, u32[]{:S(2)}) copy-start(s32[64]{0:T(128)} %param.24) | copy-start | bytes 772
  2.7 11.5 %collective-permute-start = (bf16[24,2048]{1,0:T(8,128)(2,1)S(1)}, bf16[24,2048]{1,0:T(8,128)(2,1)S(1)}, u32[]{:S(2)}, u32[]{:S(2)}) collective-permute-start(bf16[24,2048]{1,0:T(8,128)(2,1)S(1)} %get-tuple-element.29), channel_id=1, source_target_pairs={{0,4},{4,0},{8,12},{12,8},{1,5},{5,1},{9,13},{13,9},{2,6},{6,2},{1... | collective-permute-start | bytes 294920 | tf_op jit(solution)/shard_map/ppermute | solution.py:20
  5.7 10.4 %collective-permute-start.1 = (bf16[24,2048]{1,0:T(8,128)(2,1)S(1)}, bf16[24,2048]{1,0:T(8,128)(2,1)S(1)}, u32[]{:S(2)}, u32[]{:S(2)}) collective-permute-start(bf16[24,2048]{1,0:T(8,128)(2,1)S(1)} %get-tuple-element.30), channel_id=1, source_target_pairs={{0,8},{4,12},{8,0},{12,4},{1,9},{5,13},{9,1},{13,5},{2,10},{6,14},... | collective-permute-start | bytes 294920 | tf_op jit(solution)/shard_map/ppermute | solution.py:20
  8.3 7.8 %collective-permute-start.2 = (bf16[24,2048]{1,0:T(8,128)(2,1)S(1)}, bf16[24,2048]{1,0:T(8,128)(2,1)S(1)}, u32[]{:S(2)}, u32[]{:S(2)}) collective-permute-start(bf16[24,2048]{1,0:T(8,128)(2,1)S(1)} %get-tuple-element.31), channel_id=1, source_target_pairs={{0,12},{4,8},{8,4},{12,0},{1,13},{5,9},{9,5},{13,1},{2,14},{6,10},... | collective-permute-start | bytes 294920 | tf_op jit(solution)/shard_map/ppermute | solution.py:20
  8.3 7.8 %copy-start.1 = (f32[8192]{0:T(1024)S(1)}, f32[8192]{0:T(1024)}, u32[]{:S(2)}) copy-start(f32[8192]{0:T(1024)} %param.14) | copy-start | bytes 98308
  16.6 3.9 %collective-permute-start.5 = (f32[32,256]{1,0:T(8,128)S(1)}, f32[32,256]{1,0:T(8,128)S(1)}, u32[]{:S(2)}, u32[]{:S(2)}) collective-permute-start(f32[32,256]{1,0:T(8,128)S(1)} %lower.1.refs_0_), channel_id=1, source_target_pairs={{0,3},{1,2},{2,1},{3,0},{4,7},{5,6},{6,5},{7,4},{8,11},{9,10},{10,... | collective-permute-start | bytes 98312 | tf_op jit(solution)/shard_map/ppermute | solution.py:20
  16.6 4.0 %collective-permute-start.4 = (f32[32,256]{1,0:T(8,128)S(1)}, f32[32,256]{1,0:T(8,128)S(1)}, u32[]{:S(2)}, u32[]{:S(2)}) collective-permute-start(f32[32,256]{1,0:T(8,128)S(1)} %lower.1.refs_0_), channel_id=1, source_target_pairs={{0,2},{1,3},{2,0},{3,1},{4,6},{5,7},{6,4},{7,5},{8,10},{9,11},{10,... | collective-permute-start | bytes 98312 | tf_op jit(solution)/shard_map/ppermute | solution.py:20
  18.2 2.5 %collective-permute-start.3 = (f32[32,256]{1,0:T(8,128)S(1)}, f32[32,256]{1,0:T(8,128)S(1)}, u32[]{:S(2)}, u32[]{:S(2)}) collective-permute-start(f32[32,256]{1,0:T(8,128)S(1)} %lower.1.refs_0_), channel_id=1, source_target_pairs={{0,1},{1,0},{2,3},{3,2},{4,5},{5,4},{6,7},{7,6},{8,9},{9,8},{10,11... | collective-permute-start | bytes 98312 | tf_op jit(solution)/shard_map/ppermute | solution.py:20
  18.5 2.2 %copy-start.3 = (s32[64]{0:T(128)S(1)}, s32[64]{0:T(128)}, u32[]{:S(2)}) copy-start(s32[64]{0:T(128)} %param.24) | copy-start | bytes 772
  18.5 14.0 %copy-start.4 = (s32[16]{0:T(128)S(1)}, s32[16]{0:T(128)}, u32[]{:S(2)}) copy-start(s32[16]{0:T(128)} %length_ref.1) | copy-start | bytes 196
  21.3 4.7 %collective-permute-start.6 = (bf16[16,2560]{1,0:T(8,128)(2,1)S(1)}, bf16[16,2560]{1,0:T(8,128)(2,1)S(1)}, u32[]{:S(2)}, u32[]{:S(2)}) collective-permute-start(bf16[16,2560]{1,0:T(8,128)(2,1)S(1)} %get-tuple-element.37), channel_id=1, source_target_pairs={{0,4},{4,0},{8,12},{12,8},{1,5},{5,1},{9,13},{13,9},{2,6},{6,2},{1... | collective-permute-start | bytes 245768 | tf_op jit(solution)/shard_map/ppermute | solution.py:20
  23.0 9.5 %collective-permute-start.7 = (bf16[16,2560]{1,0:T(8,128)(2,1)S(1)}, bf16[16,2560]{1,0:T(8,128)(2,1)S(1)}, u32[]{:S(2)}, u32[]{:S(2)}) collective-permute-start(bf16[16,2560]{1,0:T(8,128)(2,1)S(1)} %get-tuple-element.38), channel_id=1, source_target_pairs={{0,8},{4,12},{8,0},{12,4},{1,9},{5,13},{9,1},{13,5},{2,10},{6,14},... | collective-permute-start | bytes 245768 | tf_op jit(solution)/shard_map/ppermute | solution.py:20
  24.4 8.1 %collective-permute-start.8 = (bf16[16,2560]{1,0:T(8,128)(2,1)S(1)}, bf16[16,2560]{1,0:T(8,128)(2,1)S(1)}, u32[]{:S(2)}, u32[]{:S(2)}) collective-permute-start(bf16[16,2560]{1,0:T(8,128)(2,1)S(1)} %get-tuple-element.39), channel_id=1, source_target_pairs={{0,12},{4,8},{8,4},{12,0},{1,13},{5,9},{9,5},{13,1},{2,14},{6,10},... | collective-permute-start | bytes 245768 | tf_op jit(solution)/shard_map/ppermute | solution.py:20

commit v3 on v2

--- a/solution.py
+++ b/solution.py
@@ -31,6 +31,10 @@
         compiler_params=pltpu.CompilerParams(vmem_limit_bytes=limit * MIB),
         cost_estimate=pl.CostEstimate(flops=flops, bytes_accessed=moved, transcendentals=0),
     )(*args)
+
+
+def in_hbm(array):
+    return pltpu.with_memory_space_constraint(array, pltpu.HBM)
 
 
 def iota(shape, axis):
@@ -91,28 +95,41 @@
     query_up = query_up_weight.reshape(low_cols, query_cols)
     value_up = value_up_weight.reshape(low_cols, kv_cols)
 
-    def prepare(ids_ref, x_ref, *out_refs):
+    def prepare(ids_ref, x_ref, *refs):
+        out_refs, chosen_ids, part, sems = refs[:-3], refs[-3], refs[-2], refs[-1]
         me = lax.axis_index("adapter")
         lane = lax.axis_index("lane")
+        lane_at = pl.ds(pl.multiple_of(lane * lane_width, lane_width), lane_width)
+        copies = [
+            pltpu.make_async_copy(ids_ref, chosen_ids, sems.at[owners_count]),
+            pltpu.make_async_copy(x_ref.at[:, lane_at], part, sems.at[owners_count + 1]),
+        ]
+        for step in range(owners_count):
+            other = jnp.bitwise_xor(me, step)
+            at = pl.ds(pl.multiple_of(other * base_width, base_width), base_width)
+            target = out_refs[step].at[:block_rows, :] if joined else out_refs[2 * step]
+            copies.append(pltpu.make_async_copy(x_ref.at[:, at], target, sems.at[step]))
+        for copy in copies:
+            copy.start()
+        copies[0].wait()
         owner = jnp.bitwise_xor(me, iota((slots, 1), 0) // capacity)
         chosen = slot_map(
-            ids_ref[...], owner, jnp.full((slots, 1), me), capacity, block_rows, nearby
+            chosen_ids[...], owner, jnp.full((slots, 1), me), capacity, block_rows, nearby
         )
         fold = lax.rem(iota((rows, block_rows), 0), block_rows) == iota((rows, block_rows), 1)
         chosen = jnp.dot(
             chosen.astype(BF16), jnp.where(fold, 1.0, 0.0).astype(BF16), preferred_element_type=F32
         )
-        part = x_ref[:, pl.ds(pl.multiple_of(lane * lane_width, lane_width), lane_width)]
-        placed = jnp.dot(chosen.astype(BF16), part, preferred_element_type=F32)
+        copies[1].wait()
+        placed = jnp.dot(chosen.astype(BF16), part[...], preferred_element_type=F32)
         for step in range(owners_count):
-            other = jnp.bitwise_xor(me, step)
-            base = x_ref[:, pl.ds(pl.multiple_of(other * base_width, base_width), base_width)]
             mine = placed[step * capacity : (step + 1) * capacity].astype(BF16)
             if joined:
-                out_refs[step][...] = jnp.concatenate([base, mine], axis=0)
+                out_refs[step][block_rows:, :] = mine
             else:
-                out_refs[2 * step][...] = base
                 out_refs[2 * step + 1][...] = mine
+        for copy in copies[2:]:
+            copy.wait()
 
     if joined:
         shapes = [jax.ShapeDtypeStruct((block_rows + capacity, base_width), BF16)] * owners_count
@@ -122,53 +139,69 @@
             jax.ShapeDtypeStruct((capacity, lane_width), BF16),
         ] * owners_count
     sent = call(
-        prepare, "prepare", shapes, [VMEM] * 2, [VMEM] * len(shapes), (ids, residual_input),
+        prepare, "prepare", shapes, [HBM] * 2, [VMEM] * len(shapes),
+        (in_hbm(ids), in_hbm(residual_input)),
+        scratch=[
+            pltpu.VMEM((1, rows), jnp.int32),
+            pltpu.VMEM((block_rows, lane_width), BF16),
+            pltpu.SemaphoreType.DMA((owners_count + 2,)),
+        ],
         moved=2**19,
     )
     per = len(sent) // owners_count
-    arrived = list(sent[:per])
-    for step in range(1, owners_count):
-        for piece in sent[per * step : per * (step + 1)]:
-            arrived.append(partner(piece, "adapter", step))
-
-    held = (
-        query_weight, key_weight, value_weight, query_down, value_down, query_up, value_up,
-        cached_key_rows, cached_value_rows,
-    )
-
-    def fetch(x_ref, *refs):
-        sources, targets, rms_ref, sems = refs[: len(held)], refs[len(held) : -2], refs[-2], refs[-1]
-        copies = [
-            pltpu.make_async_copy(source, target, sems.at[i])
-            for i, (source, target) in enumerate(zip(sources, targets))
+    arrived = [list(sent[:per])] + [None] * (owners_count - 1)
+    for step in reversed(range(1, owners_count)):
+        arrived[step] = [
+            partner(piece, "adapter", step) for piece in sent[per * step : per * (step + 1)]
         ]
-        for copy in copies:
-            copy.start()
-        x = x_ref[...].astype(F32)
-        mean = jnp.sum(x * x, axis=1, keepdims=True) * (1.0 / width)
-        rms_ref[...] = jnp.broadcast_to(lax.rsqrt(mean + EPS), rms_ref.shape)
-        for copy in copies:
-            copy.wait()
-
-    fetched = call(
-        fetch,
-        "fetch",
-        [pltpu.VMEM(a.shape, a.dtype) for a in held]
-        + [jax.ShapeDtypeStruct((block_rows, 128), F32)],
-        [VMEM] + [HBM] * len(held),
-        [VMEM] * (len(held) + 1),
-        (residual_input, *(pltpu.with_memory_space_constraint(a, pltpu.HBM) for a in held)),
-        scratch=[pltpu.SemaphoreType.DMA((len(held),))],
-        moved=16 * MIB,
-    )
-    (w_query, w_key, w_value, w_query_down, w_value_down, w_query_up, w_value_up,
-     keys, values, row_scale) = fetched
+    arrived = sum(reversed(arrived), [])
+
+    def fetch(arrays, name, after=None):
+        def body(x_ref, *refs):
+            refs = refs if after is None else refs[1:]
+            sources, targets = refs[: len(arrays)], refs[len(arrays) : 2 * len(arrays)]
+            sems = refs[-1]
+            copies = [
+                pltpu.make_async_copy(source, target, sems.at[i])
+                for i, (source, target) in enumerate(zip(sources, targets))
+            ]
+            for copy in copies:
+                copy.start()
+            if after is not None:
+                x = x_ref[...].astype(F32)
+                mean = jnp.sum(x * x, axis=1, keepdims=True) * (1.0 / width)
+                refs[-2][...] = jnp.broadcast_to(lax.rsqrt(mean + EPS), refs[-2].shape)
+            for copy in copies:
+                copy.wait()
+
+        extra = [] if after is None else [jax.ShapeDtypeStruct((block_rows, 128), F32)]
+        lead = [VMEM] if after is not None else [HBM]
+        return call(
+            body, name,
+            [pltpu.VMEM(a.shape, a.dtype) for a in arrays] + extra,
+            lead + ([] if after is None else [HBM]) + [HBM] * len(arrays),
+            [VMEM] * (len(arrays) + len(extra)),
+            (
+                residual_input if after is not None else in_hbm(residual_input),
+                *([] if after is None else [after]),
+                *(in_hbm(a) for a in arrays),
+            ),
+            scratch=[pltpu.SemaphoreType.DMA((len(arrays),))],
+            moved=sum(a.size * a.dtype.itemsize for a in arrays),
+        )
+
+    (w_query, w_key, w_value, w_query_down, w_value_down, w_query_up, w_value_up) = fetch(
+        (query_weight, key_weight, value_weight, query_down, value_down, query_up, value_up),
+        "fetch_weights",
+    )
 
     def base_of(refs, step):
-        return refs[step][:block_rows, :] if joined else refs[2 * step][...]
+        at = owners_count - 1 - step
+        return refs[at][:block_rows, :] if joined else refs[2 * at][...]
 
     def slots_of(refs, step):
-        return refs[step][block_rows:, :] if joined else refs[2 * step + 1][...]
+        at = owners_count - 1 - step
+        return refs[at][block_rows:, :] if joined else refs[2 * at + 1][...]
 
     def lower(gain_ref, dq_ref, dv_ref, *refs):
         part_refs, out_ref = refs[:-1], refs[-1]
@@ -265,21 +298,21 @@
         (ids, based, w_query_up, w_value_up, *lows),
         scratch=[pltpu.VMEM((rows, all_cols), F32)],
     )
-    parts = [parts[0]] + [
-        partner(parts[step], "adapter", step) for step in range(1, owners_count)
-    ]
+    keys, values, row_scale = fetch((cached_key_rows, cached_value_rows), "fetch_cache", parts[0])
+    parts = [
+        partner(parts[step], "adapter", step) for step in reversed(range(1, owners_count))
+    ] + [parts[0]]
 
     def finish(length_ref, scale_ref, k_ref, v_ref, *refs):
         part_refs = refs[:owners_count]
         out_ref, fresh_ref, sum_ref, q_ref, s_ref, o_ref = refs[owners_count:]
-        summed = part_refs[0][...]
-        for ref in part_refs[1:]:
+        summed = part_refs[-1][...]
+        for ref in part_refs[:-1]:
             summed = summed + ref[...].astype(F32)
         summed = (summed * scale_ref[:, :1]).astype(BF16)
         key_new = summed[:, query_cols : query_cols + kv_cols]
         value_new = summed[:, query_cols + kv_cols :]
-        fresh_ref[:, :kv_cols] = key_new
-        fresh_ref[:, kv_cols:] = value_new
+        fresh_ref[...] = jnp.stack([key_new, value_new], axis=1)
         sum_ref[...] = summed.astype(F32)
         for head in range(heads):
             q_ref[:, head, :] = sum_ref[:, head * head_dim : (head + 1) * head_dim]
@@ -325,7 +358,7 @@
         finish, "finish",
         [
             jax.ShapeDtypeStruct((block_rows, query_cols), BF16),
-            jax.ShapeDtypeStruct((block_rows, 2 * kv_cols), BF16),
+            jax.ShapeDtypeStruct((block_rows, 2, kv_cols), BF16),
         ],
         [SMEM] + [VMEM] * (3 + owners_count), [VMEM] * 2,
         (cached_length, row_scale, keys, values, *parts),
@@ -336,7 +369,7 @@
             pltpu.VMEM((block_rows, heads, head_dim), F32),
         ],
     )
-    return (attended, fresh.reshape(block_rows, 2, kv_cols))
+    return (attended, fresh)
 
 
 def solution(mesh):

time: 35.9 us -> 33.1 us (0.922)
  waiting for transfers between devices: 8.96 us -> 6.7 us
  local copies, waits for them, and re-layouts: 2.22 us -> 0.01 us
  Pallas kernels: 11.9 us -> 13.5 us
    ppermute x9, waiting for transfers between devices: 8.96 us -> 6.7 us  [partner(): return lax.ppermute(array, axis, [(i, i ^ step) for i in range(count)])]
    pallas_call x6 -> x7, Pallas kernels: 11.9 us -> 13.5 us  [call(): pl.pallas_call(body, name=name, out_shape=outs, in_specs=in_specs, out_sp...]
    unnamed x10 -> x8, local copies, waits for them, and re-layouts: 1.61 us -> 0.01 us
    reshape x1 -> x0, local copies, waits for them, and re-layouts: 0.62 us -> none  [on_device(): return (attended, fresh.reshape(block_rows, 2, kv_cols))]
  transfers between devices with their start and end apart: 9 -> 9, of which waited for: 4 -> 4; matrix products, arithmetic and copies ran while one was open for 0% -> 0% of each run, Pallas kernels for 22% -> 26%
where the time goes in v3:
time: 33.1 us; the launch traced here: 33 us
  Pallas kernels  13.5 us (41%)
  starting transfers between devices  12.1 us (37%)
  waiting for transfers between devices  6.7 us (20%)
  between operations  0.7 us (2%)
    pallas_call x7, Pallas kernels, call(): pl.pallas_call(body, name=name, out_shape=outs, in_specs=in_specs, out_sp...  13.5 us
    ppermute x9, starting transfers between devices, partner(): return lax.ppermute(array, axis, [(i, i ^ step) for i in range(count)])  12.1 us
    ppermute x9, waiting for transfers between devices, partner(): return lax.ppermute(array, axis, [(i, i ^ step) for i in range(count)])  6.7 us
  transfers between devices with their start and end apart: 9, of which 4 were waited for; matrix products, arithmetic and copies ran while one was open for 0% of the time, Pallas kernels for 26%

profile of v3, /device:TPU:0, one launch (start us, length us, event | category | flops | bytes accessed | tf_op | source)
XLA Modules:
  0.0 33.0 jit_solution(16001243047525402687)
XLA Ops:
  0.6 1.1 %prepare.1 = (bf16[24,2048]{1,0:T(8,128)(2,1)S(1)}, bf16[24,2048]{1,0:T(8,128)(2,1)S(1)}, bf16[24,2048]{1,0:T(8,128)(2,1)S(1)}, bf16[24,2048]{1,0:T(8,128)(2,1)S(1)}) custom-call(s32[1,64]{1,0:T(1,128)} %bitcast.12, bf16[16,8192]{1,0:T(8,128)(2,1)} %x_ref.5), custom_call_target="tpu_custom_call" | custom-call | bytes 524288 | tf_op jit(solution)/shard_map/prepare/pallas_call | solution.py:24
  1.8 5.1 %collective-permute-start = (bf16[24,2048]{1,0:T(8,128)(2,1)S(1)}, bf16[24,2048]{1,0:T(8,128)(2,1)S(1)}, u32[]{:S(2)}, u32[]{:S(2)}) collective-permute-start(bf16[24,2048]{1,0:T(8,128)(2,1)S(1)} %get-tuple-element.23), channel_id=1, source_target_pairs={{0,12},{4,8},{8,4},{12,0},{1,13},{5,9},{9,5},{13,1},{2,14},{6,10},... | collective-permute-start | bytes 294920 | tf_op jit(solution)/shard_map/ppermute | solution.py:20
  6.9 0.0 collective-permute-start.1
  6.9 0.6 %collective-permute-start.2 = (bf16[24,2048]{1,0:T(8,128)(2,1)S(1)}, bf16[24,2048]{1,0:T(8,128)(2,1)S(1)}, u32[]{:S(2)}, u32[]{:S(2)}) collective-permute-start(bf16[24,2048]{1,0:T(8,128)(2,1)S(1)} %get-tuple-element.25), channel_id=1, source_target_pairs={{0,4},{4,0},{8,12},{12,8},{1,5},{5,1},{9,13},{13,9},{2,6},{6,2},{1... | collective-permute-start | bytes 294920 | tf_op jit(solution)/shard_map/ppermute | solution.py:20
  7.5 0.0 copy-start.1
  7.5 4.4 %fetch_weights.1 = (bf16[2048,2048]{1,0:T(8,128)(2,1)S(1)}, bf16[2048,256]{1,0:T(8,128)(2,1)S(1)}, bf16[2048,256]{1,0:T(8,128)(2,1)S(1)}, bf16[128,2048]{1,0:T(8...) custom-call(bf16[16,8192]{1,0:T(8,128)(2,1)} %x_ref.5, ...), custom_call_target="tpu_custom_call" | custom-call | bytes 12124160 | tf_op jit(solution)/shard_map/fetch_weights/pallas_call | solution.py:24
  11.9 0.0 collective-permute-done.refs_0_
  11.9 3.2 %collective-permute-done.1.refs_1_ = bf16[24,2048]{1,0:T(8,128)(2,1)S(1)} collective-permute-done((bf16[24,2048]{1,0:T(8,128)(2,1)S(1)}, bf16[24,2048]{1,0:T(8,128)(2,1)S(1)}, u32[]{:S(2)}, u32[]{:S(2)}) %collective-permute-start.1) | collective-permute-done | bytes 98336 | tf_op jit(solution)/shard_map/ppermute | solution.py:20
  15.1 0.0 collective-permute-done.2.refs_2_
  15.1 0.0 copy-done.1
  15.2 0.4 %lower.1.refs_0_ = f32[32,256]{1,0:T(8,128)S(1)} custom-call(f32[1,8192]{1,0:T(1,128)S(1)} %bitcast.10, bf16[128,2048]{1,0:T(8,128)(2,1)S(1)} %get-tuple-element.29.dq_ref, bf16[128,2048]{1,0:T(8,128)(2,1)S(1)} %get-tuple-element.30.dv_ref, bf16[24,2048]{1,0:T(8,128)(2,1)S(1)} %collective-permute-done.refs_0_, ...), custom_call_target="tpu_custom_call" | custom-call | bytes 1048576 | tf_op jit(solution)/shard_map/lower/pallas_call | solution.py:24
  15.6 0.3 collective-permute-start.5
  15.9 1.3 %collective-permute-start.4 = (f32[32,256]{1,0:T(8,128)S(1)}, f32[32,256]{1,0:T(8,128)S(1)}, u32[]{:S(2)}, u32[]{:S(2)}) collective-permute-start(f32[32,256]{1,0:T(8,128)S(1)} %lower.1.refs_0_), channel_id=1, source_target_pairs={{0,2},{1,3},{2,0},{3,1},{4,6},{5,7},{6,4},{7,5},{8,10},{9,11},{10,... | collective-permute-start | bytes 98312 | tf_op jit(solution)/shard_map/ppermute | solution.py:20
  17.2 0.3 collective-permute-start.3
  17.5 0.0 copy-start.2
  17.5 0.0 copy-start
  17.5 2.0 %project.1.based_ref = f32[64,2560]{1,0:T(8,128)S(1)} custom-call(f32[1,8192]{1,0:T(1,128)S(1)} %bitcast.11, bf16[2048,2048]{1,0:T(8,128)(2,1)S(1)} %get-tuple-element.20.wq_ref, bf16[2048,256]{1,0:T(8,128)(2,1)S(1)} %get-tuple-element.21.wk_ref, bf16[2048,256]{1,0:T(8,128)(2,1)S(1)} %get-tuple-element.22.wv_ref, ...), custom_call_target="tpu_custom_call" | custom-call | flops 671088640 | bytes 10485760 | tf_op jit(solution)/shard_map/project/pallas_call | solution.py:24
  19.4 0.0 collective-permute-done.5.refs_3_
  19.5 0.3 collective-permute-done.4.refs_2_
  19.8 0.0 collective-permute-done.3.refs_1_
  19.8 0.0 copy-done.2
  19.8 0.6 %raise_up.1 = (f32[16,2560]{1,0:T(8,128)S(1)}, bf16[16,2560]{1,0:T(8,128)(2,1)S(1)}, bf16[16,2560]{1,0:T(8,128)(2,1)S(1)}, bf16[16,2560]{1,0:T(8,128)(2,1)S(1)}) custom-call(s32[1,64]{1,0:T(1,128)S(1)} %bitcast.13, f32[64,2560]{1,0:T(8,128)S(1)} %project.1.based_ref, bf16[128,2048]{1,0:T(8,128)(2,1)S(1)} %get-tuple-element.27.uq_ref, ...), custom_call_target="tpu_custom_call" | custom-call | tf_op jit(solution)/shard_map/raise_up/pallas_call | solution.py:24
  20.4 2.5 %collective-permute-start.6 = (bf16[16,2560]{1,0:T(8,128)(2,1)S(1)}, bf16[16,2560]{1,0:T(8,128)(2,1)S(1)}, u32[]{:S(2)}, u32[]{:S(2)}) collective-permute-start(bf16[16,2560]{1,0:T(8,128)(2,1)S(1)} %get-tuple-element.35), channel_id=1, source_target_pairs={{0,12},{4,8},{8,4},{12,0},{1,13},{5,9},{9,5},{13,1},{2,14},{6,10},... | collective-permute-start | bytes 245768 | tf_op jit(solution)/shard_map/ppermute | solution.py:20
  22.9 0.0 collective-permute-start.7
  22.9 2.0 %collective-permute-start.8 = (bf16[16,2560]{1,0:T(8,128)(2,1)S(1)}, bf16[16,2560]{1,0:T(8,128)(2,1)S(1)}, u32[]{:S(2)}, u32[]{:S(2)}) collective-permute-start(bf16[16,2560]{1,0:T(8,128)(2,1)S(1)} %get-tuple-element.37), channel_id=1, source_target_pairs={{0,4},{4,0},{8,12},{12,8},{1,5},{5,1},{9,13},{13,9},{2,6},{6,2},{1... | collective-permute-start | bytes 245768 | tf_op jit(solution)/shard_map/ppermute | solution.py:20
  24.8 0.0 copy-done
  24.8 0.0 copy-start.3
  24.8 2.3 %fetch_cache.1 = (bf16[16,2,256,128]{3,2,1,0:T(8,128)(2,1)S(1)}, bf16[16,2,256,128]{3,2,1,0:T(8,128)(2,1)S(1)}, f32[16,128]{1,0:T(8,128)S(1)}) custom-call(bf16[16,8192]{1,0:T(8,128)(2,1)S(1)} %copy-done, f32[16,2560]{1,0:T(8,128)S(1)} %get-tuple-element.31.refs_0_.refs_3_, bf16[16,2,256,128]{3,2,1,0:T(8,128)(2,1)} %refs_1_.3, bf16[16,2,256,128]{3,2,1,0:T(8,128)(2,1)} %refs_2_.3), custom_call_target="tpu_custom_call" | custom-call | bytes 4194304 | tf_op jit(solution)/shard_map/fetch_cache/pallas_call | solution.py:24
  27.1 0.5 %collective-permute-done.6.refs_0_ = bf16[16,2560]{1,0:T(8,128)(2,1)S(1)} collective-permute-done((bf16[16,2560]{1,0:T(8,128)(2,1)S(1)}, bf16[16,2560]{1,0:T(8,128)(2,1)S(1)}, u32[]{:S(2)}, u32[]{:S(2)}) %collective-permute-start.6) | collective-permute-done | bytes 81952 | tf_op jit(solution)/shard_map/ppermute | solution.py:20
  27.6 2.7 %collective-permute-done.7.refs_1_ = bf16[16,2560]{1,0:T(8,128)(2,1)S(1)} collective-permute-done((bf16[16,2560]{1,0:T(8,128)(2,1)S(1)}, bf16[16,2560]{1,0:T(8,128)(2,1)S(1)}, u32[]{:S(2)}, u32[]{:S(2)}) %collective-permute-start.7) | collective-permute-done | bytes 81952 | tf_op jit(solution)/shard_map/ppermute | solution.py:20
  30.3 0.0 collective-permute-done.8.refs_2_
  30.3 0.0 copy-done.3
  30.3 2.6 %finish.1 = (bf16[16,2048]{1,0:T(8,128)(2,1)}, bf16[16,2,256]{2,1,0:T(2,128)(2,1)}) custom-call(s32[16]{0:T(128)S(1)} %copy-done.3, f32[16,128]{1,0:T(8,128)S(1)} %get-tuple-element.32.scale_ref, bf16[16,2,256,128]{3,2,1,0:T(8,128)(2,1)S(1)} %get-tuple-element.33.k_ref, bf16[16,2,256,128]{3,2,1,0:T(8,128)(2,1)S(1)} %get-tuple-element.34.v_ref, ...), custom_call_target="tpu_custom_call" | custom-call | tf_op jit(solution)/shard_map/finish/pallas_call | solution.py:24
Async XLA Ops:
  1.8 10.2 %collective-permute-start = (bf16[24,2048]{1,0:T(8,128)(2,1)S(1)}, bf16[24,2048]{1,0:T(8,128)(2,1)S(1)}, u32[]{:S(2)}, u32[]{:S(2)}) collective-permute-start(bf16[24,2048]{1,0:T(8,128)(2,1)S(1)} %get-tuple-element.23), channel_id=1, source_target_pairs={{0,12},{4,8},{8,4},{12,0},{1,13},{5,9},{9,5},{13,1},{2,14},{6,10},... | collective-permute-start | bytes 294920 | tf_op jit(solution)/shard_map/ppermute | solution.py:20
  6.9 8.3 %collective-permute-start.1 = (bf16[24,2048]{1,0:T(8,128)(2,1)S(1)}, bf16[24,2048]{1,0:T(8,128)(2,1)S(1)}, u32[]{:S(2)}, u32[]{:S(2)}) collective-permute-start(bf16[24,2048]{1,0:T(8,128)(2,1)S(1)} %get-tuple-element.24), channel_id=1, source_target_pairs={{0,8},{4,12},{8,0},{12,4},{1,9},{5,13},{9,1},{13,5},{2,10},{6,14},... | collective-permute-start | bytes 294920 | tf_op jit(solution)/shard_map/ppermute | solution.py:20
  6.9 8.3 %collective-permute-start.2 = (bf16[24,2048]{1,0:T(8,128)(2,1)S(1)}, bf16[24,2048]{1,0:T(8,128)(2,1)S(1)}, u32[]{:S(2)}, u32[]{:S(2)}) collective-permute-start(bf16[24,2048]{1,0:T(8,128)(2,1)S(1)} %get-tuple-element.25), channel_id=1, source_target_pairs={{0,4},{4,0},{8,12},{12,8},{1,5},{5,1},{9,13},{13,9},{2,6},{6,2},{1... | collective-permute-start | bytes 294920 | tf_op jit(solution)/shard_map/ppermute | solution.py:20
  7.5 7.6 %copy-start.1 = (f32[8192]{0:T(1024)S(1)}, f32[8192]{0:T(1024)}, u32[]{:S(2)}) copy-start(f32[8192]{0:T(1024)} %param.14) | copy-start | bytes 98308
  15.6 3.9 %collective-permute-start.5 = (f32[32,256]{1,0:T(8,128)S(1)}, f32[32,256]{1,0:T(8,128)S(1)}, u32[]{:S(2)}, u32[]{:S(2)}) collective-permute-start(f32[32,256]{1,0:T(8,128)S(1)} %lower.1.refs_0_), channel_id=1, source_target_pairs={{0,3},{1,2},{2,1},{3,0},{4,7},{5,6},{6,5},{7,4},{8,11},{9,10},{10,... | collective-permute-start | bytes 98312 | tf_op jit(solution)/shard_map/ppermute | solution.py:20
  15.9 3.9 %collective-permute-start.4 = (f32[32,256]{1,0:T(8,128)S(1)}, f32[32,256]{1,0:T(8,128)S(1)}, u32[]{:S(2)}, u32[]{:S(2)}) collective-permute-start(f32[32,256]{1,0:T(8,128)S(1)} %lower.1.refs_0_), channel_id=1, source_target_pairs={{0,2},{1,3},{2,0},{3,1},{4,6},{5,7},{6,4},{7,5},{8,10},{9,11},{10,... | collective-permute-start | bytes 98312 | tf_op jit(solution)/shard_map/ppermute | solution.py:20
  17.2 2.6 %collective-permute-start.3 = (f32[32,256]{1,0:T(8,128)S(1)}, f32[32,256]{1,0:T(8,128)S(1)}, u32[]{:S(2)}, u32[]{:S(2)}) collective-permute-start(f32[32,256]{1,0:T(8,128)S(1)} %lower.1.refs_0_), channel_id=1, source_target_pairs={{0,1},{1,0},{2,3},{3,2},{4,5},{5,4},{6,7},{7,6},{8,9},{9,8},{10,11... | collective-permute-start | bytes 98312 | tf_op jit(solution)/shard_map/ppermute | solution.py:20
  17.5 2.3 %copy-start.2 = (s32[64]{0:T(128)S(1)}, s32[64]{0:T(128)}, u32[]{:S(2)}) copy-start(s32[64]{0:T(128)} %param.24) | copy-start | bytes 772
  17.5 7.4 %copy-start = (bf16[16,8192]{1,0:T(8,128)(2,1)S(1)}, bf16[16,8192]{1,0:T(8,128)(2,1)}, u32[]{:S(2)}) copy-start(bf16[16,8192]{1,0:T(8,128)(2,1)} %x_ref.5) | copy-start | bytes 786436
  20.4 7.2 %collective-permute-start.6 = (bf16[16,2560]{1,0:T(8,128)(2,1)S(1)}, bf16[16,2560]{1,0:T(8,128)(2,1)S(1)}, u32[]{:S(2)}, u32[]{:S(2)}) collective-permute-start(bf16[16,2560]{1,0:T(8,128)(2,1)S(1)} %get-tuple-element.35), channel_id=1, source_target_pairs={{0,12},{4,8},{8,4},{12,0},{1,13},{5,9},{9,5},{13,1},{2,14},{6,10},... | collective-permute-start | bytes 245768 | tf_op jit(solution)/shard_map/ppermute | solution.py:20
  22.9 7.5 %collective-permute-start.7 = (bf16[16,2560]{1,0:T(8,128)(2,1)S(1)}, bf16[16,2560]{1,0:T(8,128)(2,1)S(1)}, u32[]{:S(2)}, u32[]{:S(2)}) collective-permute-start(bf16[16,2560]{1,0:T(8,128)(2,1)S(1)} %get-tuple-element.36), channel_id=1, source_target_pairs={{0,8},{4,12},{8,0},{12,4},{1,9},{5,13},{9,1},{13,5},{2,10},{6,14},... | collective-permute-start | bytes 245768 | tf_op jit(solution)/shard_map/ppermute | solution.py:20
  22.9 7.5 %collective-permute-start.8 = (bf16[16,2560]{1,0:T(8,128)(2,1)S(1)}, bf16[16,2560]{1,0:T(8,128)(2,1)S(1)}, u32[]{:S(2)}, u32[]{:S(2)}) collective-permute-start(bf16[16,2560]{1,0:T(8,128)(2,1)S(1)} %get-tuple-element.37), channel_id=1, source_target_pairs={{0,4},{4,0},{8,12},{12,8},{1,5},{5,1},{9,13},{13,9},{2,6},{6,2},{1... | collective-permute-start | bytes 245768 | tf_op jit(solution)/shard_map/ppermute | solution.py:20
  24.8 5.5 %copy-start.3 = (s32[16]{0:T(128)S(1)}, s32[16]{0:T(128)}, u32[]{:S(2)}) copy-start(s32[16]{0:T(128)} %length_ref.1) | copy-start | bytes 196

commit v4 on v3

--- a/solution.py
+++ b/solution.py
@@ -83,7 +83,8 @@
     slots = owners_count * capacity
     rows = owners_count * block_rows
     low_cols = nearby * rank
-    joined = base_width == lane_width
+    half = base_width // 2
+    joined = 2 * half == lane_width
     kv_local, context, head_dim = cached_key_rows.shape[1:]
     group_size = query_cols // head_dim // kv_local
     heads = kv_local * group_size
@@ -106,7 +107,7 @@
         ]
         for step in range(owners_count):
             other = jnp.bitwise_xor(me, step)
-            at = pl.ds(pl.multiple_of(other * base_width, base_width), base_width)
+            at = pl.ds(pl.multiple_of(other * base_width + lax.rem(lane, 2) * half, half), half)
             target = out_refs[step].at[:block_rows, :] if joined else out_refs[2 * step]
             copies.append(pltpu.make_async_copy(x_ref.at[:, at], target, sems.at[step]))
         for copy in copies:
@@ -123,19 +124,21 @@
         copies[1].wait()
         placed = jnp.dot(chosen.astype(BF16), part[...], preferred_element_type=F32)
         for step in range(owners_count):
-            mine = placed[step * capacity : (step + 1) * capacity].astype(BF16)
+            mine = placed[step * capacity : (step + 1) * capacity]
             if joined:
-                out_refs[step][block_rows:, :] = mine
+                out_refs[step][block_rows:, :] = jnp.concatenate(
+                    [mine[:, :half], mine[:, half:]], axis=0
+                ).astype(BF16)
             else:
-                out_refs[2 * step + 1][...] = mine
+                out_refs[2 * step + 1][...] = mine.astype(BF16)
         for copy in copies[2:]:
             copy.wait()
 
     if joined:
-        shapes = [jax.ShapeDtypeStruct((block_rows + capacity, base_width), BF16)] * owners_count
+        shapes = [jax.ShapeDtypeStruct((block_rows + 2 * capacity, half), BF16)] * owners_count
     else:
         shapes = [
-            jax.ShapeDtypeStruct((block_rows, base_width), BF16),
+            jax.ShapeDtypeStruct((block_rows, half), BF16),
             jax.ShapeDtypeStruct((capacity, lane_width), BF16),
         ] * owners_count
     sent = call(
@@ -156,43 +159,35 @@
         ]
     arrived = sum(reversed(arrived), [])
 
-    def fetch(arrays, name, after=None):
-        def body(x_ref, *refs):
-            refs = refs if after is None else refs[1:]
-            sources, targets = refs[: len(arrays)], refs[len(arrays) : 2 * len(arrays)]
-            sems = refs[-1]
-            copies = [
-                pltpu.make_async_copy(source, target, sems.at[i])
-                for i, (source, target) in enumerate(zip(sources, targets))
-            ]
-            for copy in copies:
-                copy.start()
-            if after is not None:
-                x = x_ref[...].astype(F32)
-                mean = jnp.sum(x * x, axis=1, keepdims=True) * (1.0 / width)
-                refs[-2][...] = jnp.broadcast_to(lax.rsqrt(mean + EPS), refs[-2].shape)
-            for copy in copies:
-                copy.wait()
-
-        extra = [] if after is None else [jax.ShapeDtypeStruct((block_rows, 128), F32)]
-        lead = [VMEM] if after is not None else [HBM]
-        return call(
-            body, name,
-            [pltpu.VMEM(a.shape, a.dtype) for a in arrays] + extra,
-            lead + ([] if after is None else [HBM]) + [HBM] * len(arrays),
-            [VMEM] * (len(arrays) + len(extra)),
-            (
-                residual_input if after is not None else in_hbm(residual_input),
-                *([] if after is None else [after]),
-                *(in_hbm(a) for a in arrays),
-            ),
-            scratch=[pltpu.SemaphoreType.DMA((len(arrays),))],
-            moved=sum(a.size * a.dtype.itemsize for a in arrays),
-        )
-
-    (w_query, w_key, w_value, w_query_down, w_value_down, w_query_up, w_value_up) = fetch(
-        (query_weight, key_weight, value_weight, query_down, value_down, query_up, value_up),
-        "fetch_weights",
+    held = (query_weight, key_weight, value_weight, query_down, value_down, query_up, value_up)
+
+    def fetch(x_ref, *refs):
+        count = len(held)
+        rms_ref, x_copy, sems = refs[2 * count :]
+        copies = [pltpu.make_async_copy(x_ref, x_copy, sems.at[count])] + [
+            pltpu.make_async_copy(refs[i], refs[count + i], sems.at[i]) for i in range(count)
+        ]
+        for copy in copies:
+            copy.start()
+        copies[0].wait()
+        x = x_copy[...].astype(F32)
+        mean = jnp.sum(x * x, axis=1, keepdims=True) * (1.0 / width)
+        rms_ref[...] = jnp.broadcast_to(lax.rsqrt(mean + EPS), rms_ref.shape)
+        for copy in copies[1:]:
+            copy.wait()
+
+    (w_query, w_key, w_value, w_query_down, w_value_down, w_query_up, w_value_up,
+     row_scale) = call(
+        fetch, "fetch",
+        [pltpu.VMEM(a.shape, a.dtype) for a in held]
+        + [jax.ShapeDtypeStruct((block_rows, 128), F32)],
+        [HBM] * (1 + len(held)), [VMEM] * (1 + len(held)),
+        (in_hbm(residual_input), *(in_hbm(a) for a in held)),
+        scratch=[
+            pltpu.VMEM((block_rows, width), BF16),
+            pltpu.SemaphoreType.DMA((len(held) + 1,)),
+        ],
+        moved=sum(a.size * a.dtype.itemsize for a in held),
     )
 
     def base_of(refs, step):
@@ -201,14 +196,17 @@
 
     def slots_of(refs, step):
         at = owners_count - 1 - step
-        return refs[at][block_rows:, :] if joined else refs[2 * at + 1][...]
+        if not joined:
+            return refs[2 * at + 1][...].astype(F32)
+        both = refs[at][block_rows:, :].astype(F32)
+        return jnp.concatenate([both[:capacity], both[capacity:]], axis=1)
 
     def lower(gain_ref, dq_ref, dv_ref, *refs):
-        part_refs, out_ref = refs[:-1], refs[-1]
+        part_refs, out_ref, half_ref = refs[:-2], refs[-2], refs[-1]
         lane = lax.axis_index("lane")
         scaled = gain_ref[:, pl.ds(pl.multiple_of(lane * lane_width, lane_width), lane_width)]
         taken = jnp.concatenate(
-            [slots_of(part_refs, step).astype(F32) for step in range(owners_count)], axis=0
+            [slots_of(part_refs, step) for step in range(owners_count)], axis=0
         )
         taken = (taken * scaled).astype(BF16)
         contract = (((1,), (1,)), ((), ()))
@@ -218,22 +216,33 @@
         out_ref[:, low_cols:] = lax.dot_general(
             taken, dv_ref[...], contract, preferred_element_type=F32
         )
-
-    low = call(
-        lower, "lower", jax.ShapeDtypeStruct((slots, 2 * low_cols), F32),
-        [VMEM] * (3 + len(arrived)), VMEM, (gain, w_query_down, w_value_down, *arrived), moved=MIB,
-    )
-    lows = [low] + [partner(low, "lane", step) for step in range(1, lane_count)]
-
-    def project(gain_ref, wq_ref, wk_ref, wv_ref, *refs):
-        part_refs, out_ref, x_ref = refs[:-2], refs[-2], refs[-1]
         me = lax.axis_index("adapter")
-        scaled = gain_ref[:, pl.ds(pl.multiple_of(me * base_width, base_width), base_width)]
+        first = me * base_width + lax.rem(lane, 2) * half
+        scaled = gain_ref[:, pl.ds(pl.multiple_of(first, half), half)]
         for step in range(owners_count):
             start = pl.multiple_of(jnp.bitwise_xor(me, step) * block_rows, block_rows)
-            x_ref[pl.ds(start, block_rows), :] = (
+            half_ref[pl.ds(start, block_rows), :] = (
                 base_of(part_refs, step).astype(F32) * scaled
             ).astype(BF16)
+
+    low, near_half = call(
+        lower, "lower",
+        [
+            jax.ShapeDtypeStruct((slots, 2 * low_cols), F32),
+            jax.ShapeDtypeStruct((rows, half), BF16),
+        ],
+        [VMEM] * (3 + len(arrived)), [VMEM] * 2, (gain, w_query_down, w_value_down, *arrived),
+        moved=MIB,
+    )
+    far_half = partner(near_half, "lane", 1)
+    lows = [
+        partner(low, "lane", step) for step in reversed(range(1, lane_count))
+    ] + [low]
+
+    def project(near_ref, far_ref, wq_ref, wk_ref, wv_ref, out_ref, x_ref):
+        side = lax.rem(lax.axis_index("lane"), 2)
+        x_ref[:, pl.ds(pl.multiple_of(side * half, half), half)] = near_ref[...]
+        x_ref[:, pl.ds(pl.multiple_of((1 - side) * half, half), half)] = far_ref[...]
         tile = min(1024, query_cols)
         for at in range(0, query_cols, tile):
             out_ref[:, at : at + tile] = jnp.dot(
@@ -248,7 +257,7 @@
 
     based = call(
         project, "project", jax.ShapeDtypeStruct((rows, all_cols), F32),
-        [VMEM] * (4 + len(arrived)), VMEM, (gain, w_query, w_key, w_value, *arrived),
+        [VMEM] * 5, VMEM, (near_half, far_half, w_query, w_key, w_value),
         scratch=[pltpu.VMEM((rows, base_width), BF16)],
         flops=2 * rows * base_width * all_cols, moved=10 * MIB,
     )
@@ -298,7 +307,6 @@
         (ids, based, w_query_up, w_value_up, *lows),
         scratch=[pltpu.VMEM((rows, all_cols), F32)],
     )
-    keys, values, row_scale = fetch((cached_key_rows, cached_value_rows), "fetch_cache", parts[0])
     parts = [
         partner(parts[step], "adapter", step) for step in reversed(range(1, owners_count))
     ] + [parts[0]]
@@ -361,7 +369,7 @@
             jax.ShapeDtypeStruct((block_rows, 2, kv_cols), BF16),
         ],
         [SMEM] + [VMEM] * (3 + owners_count), [VMEM] * 2,
-        (cached_length, row_scale, keys, values, *parts),
+        (cached_length, row_scale, cached_key_rows, cached_value_rows, *parts),
         scratch=[
             pltpu.VMEM((block_rows, all_cols), F32),
             pltpu.VMEM((block_rows, heads, head_dim), F32),

time: 33.1 us -> 32.3 us (0.976)
  Pallas kernels: 13.5 us -> 11.2 us
  waiting for transfers between devices: 6.7 us -> 7.92 us
    pallas_call x7 -> x6, Pallas kernels: 13.5 us -> 11.2 us  [call(): pl.pallas_call(body, name=name, out_shape=outs, in_specs=in_specs, out_sp...]
    ppermute x9 -> x10, waiting for transfers between devices: 6.7 us -> 7.92 us  [partner(): return lax.ppermute(array, axis, [(i, i ^ step) for i in range(count)])]
    ppermute x9 -> x10, starting transfers between devices: 12.1 us -> 12.2 us  [partner(): return lax.ppermute(array, axis, [(i, i ^ step) for i in range(count)])]
  transfers between devices with their start and end apart: 9 -> 10, of which waited for: 4 -> 5; matrix products, arithmetic and copies ran while one was open for 0% -> 0% of each run, Pallas kernels for 26% -> 20%
where the time goes in v4:
time: 32.3 us; the launch traced here: 32.2 us
  starting transfers between devices  12.2 us (38%)
  Pallas kernels  11.2 us (35%)
  waiting for transfers between devices  7.92 us (25%)
  between operations  0.74 us (2%)
    ppermute x10, starting transfers between devices, partner(): return lax.ppermute(array, axis, [(i, i ^ step) for i in range(count)])  12.2 us
    pallas_call x6, Pallas kernels, call(): pl.pallas_call(body, name=name, out_shape=outs, in_specs=in_specs, out_sp...  11.2 us
    ppermute x10, waiting for transfers between devices, partner(): return lax.ppermute(array, axis, [(i, i ^ step) for i in range(count)])  7.92 us
  transfers between devices with their start and end apart: 10, of which 5 were waited for; matrix products, arithmetic and copies ran while one was open for 0% of the time, Pallas kernels for 20%

profile of v4, /device:TPU:0, one launch (start us, length us, event | category | flops | bytes accessed | tf_op | source)
XLA Modules:
  0.0 32.2 jit_solution(2268195051797883248)
XLA Ops:
  0.6 0.0 copy-start.2
  0.6 1.1 %prepare.1 = (bf16[32,1024]{1,0:T(8,128)(2,1)S(1)}, bf16[32,1024]{1,0:T(8,128)(2,1)S(1)}, bf16[32,1024]{1,0:T(8,128)(2,1)S(1)}, bf16[32,1024]{1,0:T(8,128)(2,1)S(1)}) custom-call(s32[1,64]{1,0:T(1,128)} %bitcast.11, bf16[16,8192]{1,0:T(8,128)(2,1)} %x_ref.3), custom_call_target="tpu_custom_call" | custom-call | bytes 524288 | tf_op jit(solution)/shard_map/prepare/pallas_call | solution.py:24
  1.8 5.1 %collective-permute-start = (bf16[32,1024]{1,0:T(8,128)(2,1)S(1)}, bf16[32,1024]{1,0:T(8,128)(2,1)S(1)}, u32[]{:S(2)}, u32[]{:S(2)}) collective-permute-start(bf16[32,1024]{1,0:T(8,128)(2,1)S(1)} %get-tuple-element.23), channel_id=1, source_target_pairs={{0,12},{4,8},{8,4},{12,0},{1,13},{5,9},{9,5},{13,1},{2,14},{6,10},... | collective-permute-start | bytes 196616 | tf_op jit(solution)/shard_map/ppermute | solution.py:20
  6.9 0.0 collective-permute-start.1
  6.9 0.6 %collective-permute-start.2 = (bf16[32,1024]{1,0:T(8,128)(2,1)S(1)}, bf16[32,1024]{1,0:T(8,128)(2,1)S(1)}, u32[]{:S(2)}, u32[]{:S(2)}) collective-permute-start(bf16[32,1024]{1,0:T(8,128)(2,1)S(1)} %get-tuple-element.25), channel_id=1, source_target_pairs={{0,4},{4,0},{8,12},{12,8},{1,5},{5,1},{9,13},{13,9},{2,6},{6,2},{1... | collective-permute-start | bytes 196616 | tf_op jit(solution)/shard_map/ppermute | solution.py:20
  7.5 4.5 %fetch.1 = (bf16[2048,2048]{1,0:T(8,128)(2,1)S(1)}, bf16[2048,256]{1,0:T(8,128)(2,1)S(1)}, bf16[2048,256]{1,0:T(8,128)(2,1)S(1)}, bf16[128,2048]{1,0:T(8,128)(2,...) custom-call(bf16[16,8192]{1,0:T(8,128)(2,1)} %x_ref.3, ...), custom_call_target="tpu_custom_call" | custom-call | bytes 12124160 | tf_op jit(solution)/shard_map/fetch/pallas_call | solution.py:24
  12.0 0.0 copy-start.3
  12.0 0.0 copy-start
  12.0 0.0 copy-start.1
  12.1 0.0 copy-start.4
  12.1 0.0 collective-permute-done.refs_0_
  12.1 0.4 %collective-permute-done.1.refs_1_ = bf16[32,1024]{1,0:T(8,128)(2,1)S(1)} collective-permute-done((bf16[32,1024]{1,0:T(8,128)(2,1)S(1)}, bf16[32,1024]{1,0:T(8,128)(2,1)S(1)}, u32[]{:S(2)}, u32[]{:S(2)}) %collective-permute-start.1) | collective-permute-done | bytes 65568 | tf_op jit(solution)/shard_map/ppermute | solution.py:20
  12.5 0.0 collective-permute-done.2.refs_2_
  12.5 0.0 copy-done.2
  12.5 0.4 %lower.1 = (f32[32,256]{1,0:T(8,128)S(1)}, bf16[64,1024]{1,0:T(8,128)(2,1)S(1)}) custom-call(f32[1,8192]{1,0:T(1,128)S(1)} %bitcast.10, bf16[128,2048]{1,0:T(8,128)(2,1)S(1)} %get-tuple-element.21.dq_ref, bf16[128,2048]{1,0:T(8,128)(2,1)S(1)} %get-tuple-element.22.dv_ref, bf16[32,1024]{1,0:T(8,128)(2,1)S(1)} %collective-permute-done.refs_0_, ...), custom_call_target="tpu_custom_call" | custom-call | bytes 1048576 | tf_op jit(solution)/shard_map/lower/pallas_call | solution.py:24
  12.9 0.0 collective-permute-start.3
  12.9 0.5 %collective-permute-start.6 = (f32[32,256]{1,0:T(8,128)S(1)}, f32[32,256]{1,0:T(8,128)S(1)}, u32[]{:S(2)}, u32[]{:S(2)}) collective-permute-start(f32[32,256]{1,0:T(8,128)S(1)} %get-tuple-element.33.refs_3_), channel_id=1, source_target_pairs={{0,1},{1,0},{2,3},{3,2},{4,5},{5,4},{6,7},{7,6},{8,9},{9,8},{10,11... | collective-permute-start | bytes 98312 | tf_op jit(solution)/shard_map/ppermute | solution.py:20
  13.5 1.5 %collective-permute-start.5 = (f32[32,256]{1,0:T(8,128)S(1)}, f32[32,256]{1,0:T(8,128)S(1)}, u32[]{:S(2)}, u32[]{:S(2)}) collective-permute-start(f32[32,256]{1,0:T(8,128)S(1)} %get-tuple-element.33.refs_3_), channel_id=1, source_target_pairs={{0,2},{1,3},{2,0},{3,1},{4,6},{5,7},{6,4},{7,5},{8,10},{9,11},{10,... | collective-permute-start | bytes 98312 | tf_op jit(solution)/shard_map/ppermute | solution.py:20
  15.0 0.0 collective-permute-start.4
  15.0 0.0 collective-permute-done.3.far_ref
  15.0 2.0 %project.1.based_ref = f32[64,2560]{1,0:T(8,128)S(1)} custom-call(bf16[64,1024]{1,0:T(8,128)(2,1)S(1)} %get-tuple-element.27.near_ref, bf16[64,1024]{1,0:T(8,128)(2,1)S(1)} %collective-permute-done.3.far_ref, bf16[2048,2048]{1,0:T(8,128)(2,1)S(1)} %get-tuple-element.28.wq_ref, bf16[2048,256]{1,0:T(8,128)(2,1)S(1)} %get-tuple-element.29.wk_ref, ...), custom_call_target="tpu_custom_call" | custom-call | flops 671088640 | bytes 10485760 | tf_op jit(solution)/shard_map/project/pallas_call | solution.py:24
  16.9 0.0 collective-permute-done.6.refs_2_
  16.9 0.4 %collective-permute-done.5.refs_1_ = f32[32,256]{1,0:T(8,128)S(1)} collective-permute-done((f32[32,256]{1,0:T(8,128)S(1)}, f32[32,256]{1,0:T(8,128)S(1)}, u32[]{:S(2)}, u32[]{:S(2)}) %collective-permute-start.5) | collective-permute-done | bytes 32800 | tf_op jit(solution)/shard_map/ppermute | solution.py:20
  17.4 1.2 %collective-permute-done.4.refs_0_ = f32[32,256]{1,0:T(8,128)S(1)} collective-permute-done((f32[32,256]{1,0:T(8,128)S(1)}, f32[32,256]{1,0:T(8,128)S(1)}, u32[]{:S(2)}, u32[]{:S(2)}) %collective-permute-start.4) | collective-permute-done | bytes 32800 | tf_op jit(solution)/shard_map/ppermute | solution.py:20
  18.6 0.0 copy-done.3
  18.6 0.6 %raise_up.1 = (f32[16,2560]{1,0:T(8,128)S(1)}, bf16[16,2560]{1,0:T(8,128)(2,1)S(1)}, bf16[16,2560]{1,0:T(8,128)(2,1)S(1)}, bf16[16,2560]{1,0:T(8,128)(2,1)S(1)}) custom-call(s32[1,64]{1,0:T(1,128)S(1)} %bitcast.12, f32[64,2560]{1,0:T(8,128)S(1)} %project.1.based_ref, bf16[128,2048]{1,0:T(8,128)(2,1)S(1)} %get-tuple-element.31.uq_ref, ...), custom_call_target="tpu_custom_call" | custom-call | tf_op jit(solution)/shard_map/raise_up/pallas_call | solution.py:24
  19.2 3.4 %collective-permute-start.7 = (bf16[16,2560]{1,0:T(8,128)(2,1)S(1)}, bf16[16,2560]{1,0:T(8,128)(2,1)S(1)}, u32[]{:S(2)}, u32[]{:S(2)}) collective-permute-start(bf16[16,2560]{1,0:T(8,128)(2,1)S(1)} %get-tuple-element.34), channel_id=1, source_target_pairs={{0,12},{4,8},{8,4},{12,0},{1,13},{5,9},{9,5},{13,1},{2,14},{6,10},... | collective-permute-start | bytes 245768 | tf_op jit(solution)/shard_map/ppermute | solution.py:20
  22.6 0.0 collective-permute-start.8
  22.6 1.0 %collective-permute-start.9 = (bf16[16,2560]{1,0:T(8,128)(2,1)S(1)}, bf16[16,2560]{1,0:T(8,128)(2,1)S(1)}, u32[]{:S(2)}, u32[]{:S(2)}) collective-permute-start(bf16[16,2560]{1,0:T(8,128)(2,1)S(1)} %get-tuple-element.36), channel_id=1, source_target_pairs={{0,4},{4,0},{8,12},{12,8},{1,5},{5,1},{9,13},{13,9},{2,6},{6,2},{1... | collective-permute-start | bytes 245768 | tf_op jit(solution)/shard_map/ppermute | solution.py:20
  23.7 2.9 %collective-permute-done.7.refs_0_ = bf16[16,2560]{1,0:T(8,128)(2,1)S(1)} collective-permute-done((bf16[16,2560]{1,0:T(8,128)(2,1)S(1)}, bf16[16,2560]{1,0:T(8,128)(2,1)S(1)}, u32[]{:S(2)}, u32[]{:S(2)}) %collective-permute-start.7) | collective-permute-done | bytes 81952 | tf_op jit(solution)/shard_map/ppermute | solution.py:20
  26.6 2.9 %collective-permute-done.8.refs_1_ = bf16[16,2560]{1,0:T(8,128)(2,1)S(1)} collective-permute-done((bf16[16,2560]{1,0:T(8,128)(2,1)S(1)}, bf16[16,2560]{1,0:T(8,128)(2,1)S(1)}, u32[]{:S(2)}, u32[]{:S(2)}) %collective-permute-start.8) | collective-permute-done | bytes 81952 | tf_op jit(solution)/shard_map/ppermute | solution.py:20
  29.5 0.0 collective-permute-done.9.refs_2_
  29.5 0.0 copy-done
  29.5 0.0 copy-done.1
  29.5 0.0 copy-done.4
  29.5 2.6 %finish.1 = (bf16[16,2048]{1,0:T(8,128)(2,1)}, bf16[16,2,256]{2,1,0:T(2,128)(2,1)}) custom-call(s32[16]{0:T(128)S(1)} %copy-done.4, f32[16,128]{1,0:T(8,128)S(1)} %get-tuple-element.20.scale_ref, bf16[16,2,256,128]{3,2,1,0:T(8,128)(2,1)S(1)} %copy-done, bf16[16,2,256,128]{3,2,1,0:T(8,128)(2,1)S(1)} %copy-done.1, ...), custom_call_target="tpu_custom_call" | custom-call | tf_op jit(solution)/shard_map/finish/pallas_call | solution.py:24
Async XLA Ops:
  0.6 11.9 %copy-start.2 = (f32[8192]{0:T(1024)S(1)}, f32[8192]{0:T(1024)}, u32[]{:S(2)}) copy-start(f32[8192]{0:T(1024)} %param.14) | copy-start | bytes 98308
  1.8 10.3 %collective-permute-start = (bf16[32,1024]{1,0:T(8,128)(2,1)S(1)}, bf16[32,1024]{1,0:T(8,128)(2,1)S(1)}, u32[]{:S(2)}, u32[]{:S(2)}) collective-permute-start(bf16[32,1024]{1,0:T(8,128)(2,1)S(1)} %get-tuple-element.23), channel_id=1, source_target_pairs={{0,12},{4,8},{8,4},{12,0},{1,13},{5,9},{9,5},{13,1},{2,14},{6,10},... | collective-permute-start | bytes 196616 | tf_op jit(solution)/shard_map/ppermute | solution.py:20
  6.9 5.6 %collective-permute-start.1 = (bf16[32,1024]{1,0:T(8,128)(2,1)S(1)}, bf16[32,1024]{1,0:T(8,128)(2,1)S(1)}, u32[]{:S(2)}, u32[]{:S(2)}) collective-permute-start(bf16[32,1024]{1,0:T(8,128)(2,1)S(1)} %get-tuple-element.24), channel_id=1, source_target_pairs={{0,8},{4,12},{8,0},{12,4},{1,9},{5,13},{9,1},{13,5},{2,10},{6,14},... | collective-permute-start | bytes 196616 | tf_op jit(solution)/shard_map/ppermute | solution.py:20
  6.9 5.6 %collective-permute-start.2 = (bf16[32,1024]{1,0:T(8,128)(2,1)S(1)}, bf16[32,1024]{1,0:T(8,128)(2,1)S(1)}, u32[]{:S(2)}, u32[]{:S(2)}) collective-permute-start(bf16[32,1024]{1,0:T(8,128)(2,1)S(1)} %get-tuple-element.25), channel_id=1, source_target_pairs={{0,4},{4,0},{8,12},{12,8},{1,5},{5,1},{9,13},{13,9},{2,6},{6,2},{1... | collective-permute-start | bytes 196616 | tf_op jit(solution)/shard_map/ppermute | solution.py:20
  12.0 6.6 %copy-start.3 = (s32[64]{0:T(128)S(1)}, s32[64]{0:T(128)}, u32[]{:S(2)}) copy-start(s32[64]{0:T(128)} %param.24) | copy-start | bytes 772
  12.0 17.5 %copy-start = (bf16[16,2,256,128]{3,2,1,0:T(8,128)(2,1)S(1)}, bf16[16,2,256,128]{3,2,1,0:T(8,128)(2,1)}, u32[]{:S(2)}) copy-start(bf16[16,2,256,128]{3,2,1,0:T(8,128)(2,1)} %k_ref.1) | copy-start | bytes 6291460
  12.0 17.5 %copy-start.1 = (bf16[16,2,256,128]{3,2,1,0:T(8,128)(2,1)S(1)}, bf16[16,2,256,128]{3,2,1,0:T(8,128)(2,1)}, u32[]{:S(2)}) copy-start(bf16[16,2,256,128]{3,2,1,0:T(8,128)(2,1)} %v_ref.1) | copy-start | bytes 6291460
  12.1 17.5 %copy-start.4 = (s32[16]{0:T(128)S(1)}, s32[16]{0:T(128)}, u32[]{:S(2)}) copy-start(s32[16]{0:T(128)} %length_ref.1) | copy-start | bytes 196
  12.9 2.0 %collective-permute-start.3 = (bf16[64,1024]{1,0:T(8,128)(2,1)S(1)}, bf16[64,1024]{1,0:T(8,128)(2,1)S(1)}, u32[]{:S(2)}, u32[]{:S(2)}) collective-permute-start(bf16[64,1024]{1,0:T(8,128)(2,1)S(1)} %get-tuple-element.27.near_ref), channel_id=1, source_target_pairs={{0,1},{1,0},{2,3},{3,2},{4,5},{5,4},{6,7},{7,6},{8,9},{9,8},{10,11... | collective-permute-start | bytes 393224 | tf_op jit(solution)/shard_map/ppermute | solution.py:20
  12.9 4.0 %collective-permute-start.6 = (f32[32,256]{1,0:T(8,128)S(1)}, f32[32,256]{1,0:T(8,128)S(1)}, u32[]{:S(2)}, u32[]{:S(2)}) collective-permute-start(f32[32,256]{1,0:T(8,128)S(1)} %get-tuple-element.33.refs_3_), channel_id=1, source_target_pairs={{0,1},{1,0},{2,3},{3,2},{4,5},{5,4},{6,7},{7,6},{8,9},{9,8},{10,11... | collective-permute-start | bytes 98312 | tf_op jit(solution)/shard_map/ppermute | solution.py:20
  13.5 3.9 %collective-permute-start.5 = (f32[32,256]{1,0:T(8,128)S(1)}, f32[32,256]{1,0:T(8,128)S(1)}, u32[]{:S(2)}, u32[]{:S(2)}) collective-permute-start(f32[32,256]{1,0:T(8,128)S(1)} %get-tuple-element.33.refs_3_), channel_id=1, source_target_pairs={{0,2},{1,3},{2,0},{3,1},{4,6},{5,7},{6,4},{7,5},{8,10},{9,11},{10,... | collective-permute-start | bytes 98312 | tf_op jit(solution)/shard_map/ppermute | solution.py:20
  15.0 3.6 %collective-permute-start.4 = (f32[32,256]{1,0:T(8,128)S(1)}, f32[32,256]{1,0:T(8,128)S(1)}, u32[]{:S(2)}, u32[]{:S(2)}) collective-permute-start(f32[32,256]{1,0:T(8,128)S(1)} %get-tuple-element.33.refs_3_), channel_id=1, source_target_pairs={{0,3},{1,2},{2,1},{3,0},{4,7},{5,6},{6,5},{7,4},{8,11},{9,10},{10,... | collective-permute-start | bytes 98312 | tf_op jit(solution)/shard_map/ppermute | solution.py:20
  19.2 7.3 %collective-permute-start.7 = (bf16[16,2560]{1,0:T(8,128)(2,1)S(1)}, bf16[16,2560]{1,0:T(8,128)(2,1)S(1)}, u32[]{:S(2)}, u32[]{:S(2)}) collective-permute-start(bf16[16,2560]{1,0:T(8,128)(2,1)S(1)} %get-tuple-element.34), channel_id=1, source_target_pairs={{0,12},{4,8},{8,4},{12,0},{1,13},{5,9},{9,5},{13,1},{2,14},{6,10},... | collective-permute-start | bytes 245768 | tf_op jit(solution)/shard_map/ppermute | solution.py:20
  22.6 6.9 %collective-permute-start.8 = (bf16[16,2560]{1,0:T(8,128)(2,1)S(1)}, bf16[16,2560]{1,0:T(8,128)(2,1)S(1)}, u32[]{:S(2)}, u32[]{:S(2)}) collective-permute-start(bf16[16,2560]{1,0:T(8,128)(2,1)S(1)} %get-tuple-element.35), channel_id=1, source_target_pairs={{0,8},{4,12},{8,0},{12,4},{1,9},{5,13},{9,1},{13,5},{2,10},{6,14},... | collective-permute-start | bytes 245768 | tf_op jit(solution)/shard_map/ppermute | solution.py:20
  22.6 6.9 %collective-permute-start.9 = (bf16[16,2560]{1,0:T(8,128)(2,1)S(1)}, bf16[16,2560]{1,0:T(8,128)(2,1)S(1)}, u32[]{:S(2)}, u32[]{:S(2)}) collective-permute-start(bf16[16,2560]{1,0:T(8,128)(2,1)S(1)} %get-tuple-element.36), channel_id=1, source_target_pairs={{0,4},{4,0},{8,12},{12,8},{1,5},{5,1},{9,13},{13,9},{2,6},{6,2},{1... | collective-permute-start | bytes 245768 | tf_op jit(solution)/shard_map/ppermute | solution.py:20

commit v5 on v4

--- a/solution.py
+++ b/solution.py
@@ -159,35 +159,56 @@
         ]
     arrived = sum(reversed(arrived), [])
 
-    held = (query_weight, key_weight, value_weight, query_down, value_down, query_up, value_up)
-
-    def fetch(x_ref, *refs):
+    held = (query_down, value_down, query_weight, key_weight, value_weight)
+
+    def survey(ids_ref, x_ref, *refs):
         count = len(held)
-        rms_ref, x_copy, sems = refs[2 * count :]
-        copies = [pltpu.make_async_copy(x_ref, x_copy, sems.at[count])] + [
-            pltpu.make_async_copy(refs[i], refs[count + i], sems.at[i]) for i in range(count)
+        rms_ref, seen_ref, mask_ref, ids_copy, x_copy, sems = refs[2 * count :]
+        copies = [
+            pltpu.make_async_copy(ids_ref, ids_copy, sems.at[0]),
+            pltpu.make_async_copy(x_ref, x_copy, sems.at[1]),
+        ] + [
+            pltpu.make_async_copy(refs[i], refs[count + i], sems.at[2 + i]) for i in range(count)
         ]
         for copy in copies:
             copy.start()
         copies[0].wait()
+        me = lax.axis_index("adapter")
+        block = jnp.bitwise_xor(me, iota((slots, 1), 0) // capacity)
+        seen = slot_map(
+            ids_copy[...], jnp.full((slots, 1), me), block, capacity, block_rows, nearby
+        )
+        seen_ref[...] = seen.astype(BF16)
+        column = lax.rem(iota((slots, 2 * low_cols), 1) // rank, nearby)
+        mask = jnp.zeros((slots, 2 * low_cols), F32)
+        for near in range(nearby):
+            uses = jnp.where(ids_copy[...] == me * nearby + near, seen, 0.0)
+            uses = jnp.sum(uses, axis=1, keepdims=True)
+            mask = jnp.where(column == near, uses, mask)
+        mask_ref[...] = mask
+        copies[1].wait()
         x = x_copy[...].astype(F32)
         mean = jnp.sum(x * x, axis=1, keepdims=True) * (1.0 / width)
         rms_ref[...] = jnp.broadcast_to(lax.rsqrt(mean + EPS), rms_ref.shape)
-        for copy in copies[1:]:
+        for copy in copies[2:]:
             copy.wait()
 
-    (w_query, w_key, w_value, w_query_down, w_value_down, w_query_up, w_value_up,
-     row_scale) = call(
-        fetch, "fetch",
+    (w_query_down, w_value_down, w_query, w_key, w_value, row_scale, seen, mask) = call(
+        survey, "survey",
         [pltpu.VMEM(a.shape, a.dtype) for a in held]
-        + [jax.ShapeDtypeStruct((block_rows, 128), F32)],
-        [HBM] * (1 + len(held)), [VMEM] * (1 + len(held)),
-        (in_hbm(residual_input), *(in_hbm(a) for a in held)),
+        + [
+            jax.ShapeDtypeStruct((block_rows, 128), F32),
+            jax.ShapeDtypeStruct((slots, rows), BF16),
+            jax.ShapeDtypeStruct((slots, 2 * low_cols), F32),
+        ],
+        [HBM] * (2 + len(held)), [VMEM] * (3 + len(held)),
+        (in_hbm(ids), in_hbm(residual_input), *(in_hbm(a) for a in held)),
         scratch=[
+            pltpu.VMEM((1, rows), jnp.int32),
             pltpu.VMEM((block_rows, width), BF16),
-            pltpu.SemaphoreType.DMA((len(held) + 1,)),
-        ],
-        moved=sum(a.size * a.dtype.itemsize for a in held),
+            pltpu.SemaphoreType.DMA((2 + len(held),)),
+        ],
+        moved=12 * MIB,
     )
 
     def base_of(refs, step):
@@ -201,7 +222,7 @@
         both = refs[at][block_rows:, :].astype(F32)
         return jnp.concatenate([both[:capacity], both[capacity:]], axis=1)
 
-    def lower(gain_ref, dq_ref, dv_ref, *refs):
+    def lower(gain_ref, mask_ref, dq_ref, dv_ref, *refs):
         part_refs, out_ref, half_ref = refs[:-2], refs[-2], refs[-1]
         lane = lax.axis_index("lane")
         scaled = gain_ref[:, pl.ds(pl.multiple_of(lane * lane_width, lane_width), lane_width)]
@@ -210,12 +231,14 @@
         )
         taken = (taken * scaled).astype(BF16)
         contract = (((1,), (1,)), ((), ()))
-        out_ref[:, :low_cols] = lax.dot_general(
-            taken, dq_ref[...], contract, preferred_element_type=F32
-        )
-        out_ref[:, low_cols:] = lax.dot_general(
-            taken, dv_ref[...], contract, preferred_element_type=F32
-        )
+        for at, ref in enumerate((dq_ref, dv_ref)):
+            every = mask_ref[:, at * low_cols : (at + 1) * low_cols] * lax.dot_general(
+                taken, ref[...], contract, preferred_element_type=F32
+            )
+            picked = every[:, :rank]
+            for near in range(1, nearby):
+                picked = picked + every[:, near * rank : (near + 1) * rank]
+            out_ref[:, at * rank : (at + 1) * rank] = picked
         me = lax.axis_index("adapter")
         first = me * base_width + lax.rem(lane, 2) * half
         scaled = gain_ref[:, pl.ds(pl.multiple_of(first, half), half)]
@@ -228,16 +251,15 @@
     low, near_half = call(
         lower, "lower",
         [
-            jax.ShapeDtypeStruct((slots, 2 * low_cols), F32),
+            jax.ShapeDtypeStruct((slots, 2 * rank), F32),
             jax.ShapeDtypeStruct((rows, half), BF16),
         ],
-        [VMEM] * (3 + len(arrived)), [VMEM] * 2, (gain, w_query_down, w_value_down, *arrived),
+        [VMEM] * (4 + len(arrived)), [VMEM] * 2,
+        (gain, mask, w_query_down, w_value_down, *arrived),
         moved=MIB,
     )
     far_half = partner(near_half, "lane", 1)
-    lows = [
-        partner(low, "lane", step) for step in reversed(range(1, lane_count))
-    ] + [low]
+    lows = [low] + [partner(low, "lane", step) for step in range(1, lane_count)]
 
     def project(near_ref, far_ref, wq_ref, wk_ref, wv_ref, out_ref, x_ref):
         side = lax.rem(lax.axis_index("lane"), 2)
@@ -262,24 +284,16 @@
         flops=2 * rows * base_width * all_cols, moved=10 * MIB,
     )
 
-    def raise_up(ids_ref, based_ref, uq_ref, uv_ref, *refs):
+    def raise_up(seen_ref, mask_ref, based_ref, uq_ref, uv_ref, *refs):
         low_refs, out_refs, sum_ref = refs[:lane_count], refs[lane_count:-1], refs[-1]
         me = lax.axis_index("adapter")
-        block = jnp.bitwise_xor(me, iota((slots, 1), 0) // capacity)
-        seen = slot_map(
-            ids_ref[...], jnp.full((slots, 1), me), block, capacity, block_rows, nearby
-        )
         total = low_refs[0][...]
         for ref in low_refs[1:]:
             total = total + ref[...]
-        column = lax.rem(iota((slots, 2 * low_cols), 1) // rank, nearby)
-        picked = jnp.zeros_like(total)
-        for near in range(nearby):
-            uses = jnp.where(ids_ref[...] == me * nearby + near, seen, 0.0)
-            uses = jnp.sum(uses, axis=1, keepdims=True) > 0.5
-            picked = jnp.where(uses & (column == near), total, picked)
+        spread = [total[:, :rank]] * nearby + [total[:, rank:]] * nearby
+        spread = jnp.concatenate(spread, axis=1) * mask_ref[...]
         lowered = lax.dot_general(
-            seen.astype(BF16), picked.astype(BF16), (((0,), (0,)), ((), ())),
+            seen_ref[...], spread.astype(BF16), (((0,), (0,)), ((), ())),
             preferred_element_type=F32,
         ).astype(BF16)
         for at in range(0, query_cols, 1024):
@@ -303,8 +317,8 @@
             jax.ShapeDtypeStruct((block_rows, all_cols), BF16 if step else F32)
             for step in range(owners_count)
         ],
-        [VMEM] * (4 + lane_count), [VMEM] * owners_count,
-        (ids, based, w_query_up, w_value_up, *lows),
+        [VMEM] * (5 + lane_count), [VMEM] * owners_count,
+        (seen, mask, based, query_up, value_up, *lows),
         scratch=[pltpu.VMEM((rows, all_cols), F32)],
     )
     parts = [

time: 32.3 us -> 31.7 us (0.981)
  waiting for transfers between devices: 7.92 us -> 7.19 us
    ppermute x10, waiting for transfers between devices: 7.92 us -> 7.19 us  [partner(): return lax.ppermute(array, axis, [(i, i ^ step) for i in range(count)])]
  transfers between devices with their start and end apart: 10 -> 10, of which waited for: 5 -> 4; matrix products, arithmetic and copies ran while one was open for 0% -> 0% of each run, Pallas kernels for 20% -> 20%
where the time goes in v5:
time: 31.7 us; the launch traced here: 31.5 us
  starting transfers between devices  12.4 us (39%)
  Pallas kernels  11.1 us (35%)
  waiting for transfers between devices  7.19 us (23%)
  between operations  0.76 us (2%)
    ppermute x10, starting transfers between devices, partner(): return lax.ppermute(array, axis, [(i, i ^ step) for i in range(count)])  12.4 us
    pallas_call x6, Pallas kernels, call(): pl.pallas_call(body, name=name, out_shape=outs, in_specs=in_specs, out_sp...  11.1 us
    ppermute x10, waiting for transfers between devices, partner(): return lax.ppermute(array, axis, [(i, i ^ step) for i in range(count)])  7.19 us
  transfers between devices with their start and end apart: 10, of which 4 were waited for; matrix products, arithmetic and copies ran while one was open for 0% of the time, Pallas kernels for 20%

profile of v5, /device:TPU:0, one launch (start us, length us, event | category | flops | bytes accessed | tf_op | source)
XLA Modules:
  0.0 31.5 jit_solution(16119112319279951110)
XLA Ops:
  0.6 0.0 copy-start.4
  0.6 1.1 %prepare.1 = (bf16[32,1024]{1,0:T(8,128)(2,1)S(1)}, bf16[32,1024]{1,0:T(8,128)(2,1)S(1)}, bf16[32,1024]{1,0:T(8,128)(2,1)S(1)}, bf16[32,1024]{1,0:T(8,128)(2,1)S(1)}) custom-call(s32[1,64]{1,0:T(1,128)} %bitcast.15, bf16[16,8192]{1,0:T(8,128)(2,1)} %x_ref.3), custom_call_target="tpu_custom_call" | custom-call | bytes 524288 | tf_op jit(solution)/shard_map/prepare/pallas_call | solution.py:24
  1.8 5.1 %collective-permute-start = (bf16[32,1024]{1,0:T(8,128)(2,1)S(1)}, bf16[32,1024]{1,0:T(8,128)(2,1)S(1)}, u32[]{:S(2)}, u32[]{:S(2)}) collective-permute-start(bf16[32,1024]{1,0:T(8,128)(2,1)S(1)} %get-tuple-element.25), channel_id=1, source_target_pairs={{0,12},{4,8},{8,4},{12,0},{1,13},{5,9},{9,5},{13,1},{2,14},{6,10},... | collective-permute-start | bytes 196616 | tf_op jit(solution)/shard_map/ppermute | solution.py:20
  6.9 0.0 collective-permute-start.1
  6.9 0.6 %collective-permute-start.2 = (bf16[32,1024]{1,0:T(8,128)(2,1)S(1)}, bf16[32,1024]{1,0:T(8,128)(2,1)S(1)}, u32[]{:S(2)}, u32[]{:S(2)}) collective-permute-start(bf16[32,1024]{1,0:T(8,128)(2,1)S(1)} %get-tuple-element.27), channel_id=1, source_target_pairs={{0,4},{4,0},{8,12},{12,8},{1,5},{5,1},{9,13},{13,9},{2,6},{6,2},{1... | collective-permute-start | bytes 196616 | tf_op jit(solution)/shard_map/ppermute | solution.py:20
  7.5 4.4 %survey.1 = (bf16[128,2048]{1,0:T(8,128)(2,1)S(1)}, bf16[128,2048]{1,0:T(8,128)(2,1)S(1)}, bf16[2048,2048]{1,0:T(8,128)(2,1)S(1)}, bf16[2048,256]{1,0:T(8,128)(2...) custom-call(s32[1,64]{1,0:T(1,128)} %bitcast.16, ...), custom_call_target="tpu_custom_call" | custom-call | bytes 12582912 | tf_op jit(solution)/shard_map/survey/pallas_call | solution.py:24
  11.9 0.0 copy-start.2
  11.9 0.0 copy-start.3
  12.0 0.0 copy-start
  12.0 0.0 copy-start.1
  12.0 0.0 copy-start.5
  12.0 0.0 collective-permute-done.refs_0_
  12.0 0.5 %collective-permute-done.1.refs_1_ = bf16[32,1024]{1,0:T(8,128)(2,1)S(1)} collective-permute-done((bf16[32,1024]{1,0:T(8,128)(2,1)S(1)}, bf16[32,1024]{1,0:T(8,128)(2,1)S(1)}, u32[]{:S(2)}, u32[]{:S(2)}) %collective-permute-start.1) | collective-permute-done | bytes 65568 | tf_op jit(solution)/shard_map/ppermute | solution.py:20
  12.5 0.0 collective-permute-done.2.refs_2_
  12.5 0.0 copy-done.4
  12.5 0.6 %lower.1 = (f32[32,128]{1,0:T(8,128)S(1)}, bf16[64,1024]{1,0:T(8,128)(2,1)S(1)}) custom-call(f32[1,8192]{1,0:T(1,128)S(1)} %bitcast.12, f32[32,256]{1,0:T(8,128)S(1)} %get-tuple-element.22.mask_ref, bf16[128,2048]{1,0:T(8,128)(2,1)S(1)} %get-tuple-element.23.dq_ref, bf16[128,2048]{1,0:T(8,128)(2,1)S(1)} %get-tuple-element.24.dv_ref, ...), custom_call_target="tpu_custom_call" | custom-call | bytes 1048576 | tf_op jit(solution)/shard_map/lower/pallas_call | solution.py:24
  13.1 0.0 collective-permute-start.3
  13.1 1.6 %collective-permute-start.6 = (f32[32,128]{1,0:T(8,128)S(1)}, f32[32,128]{1,0:T(8,128)S(1)}, u32[]{:S(2)}, u32[]{:S(2)}) collective-permute-start(f32[32,128]{1,0:T(8,128)S(1)} %get-tuple-element.33.refs_0_), channel_id=1, source_target_pairs={{0,3},{1,2},{2,1},{3,0},{4,7},{5,6},{6,5},{7,4},{8,11},{9,10},{10,... | collective-permute-start | bytes 49160 | tf_op jit(solution)/shard_map/ppermute | solution.py:20
  14.7 0.5 %collective-permute-start.5 = (f32[32,128]{1,0:T(8,128)S(1)}, f32[32,128]{1,0:T(8,128)S(1)}, u32[]{:S(2)}, u32[]{:S(2)}) collective-permute-start(f32[32,128]{1,0:T(8,128)S(1)} %get-tuple-element.33.refs_0_), channel_id=1, source_target_pairs={{0,2},{1,3},{2,0},{3,1},{4,6},{5,7},{6,4},{7,5},{8,10},{9,11},{10,... | collective-permute-start | bytes 49160 | tf_op jit(solution)/shard_map/ppermute | solution.py:20
  15.3 0.0 collective-permute-start.4
  15.3 0.0 collective-permute-done.3.far_ref
  15.3 1.9 %project.1.based_ref = f32[64,2560]{1,0:T(8,128)S(1)} custom-call(bf16[64,1024]{1,0:T(8,128)(2,1)S(1)} %get-tuple-element.29.near_ref, bf16[64,1024]{1,0:T(8,128)(2,1)S(1)} %collective-permute-done.3.far_ref, bf16[2048,2048]{1,0:T(8,128)(2,1)S(1)} %get-tuple-element.30.wq_ref, bf16[2048,256]{1,0:T(8,128)(2,1)S(1)} %get-tuple-element.31.wk_ref, ...), custom_call_target="tpu_custom_call" | custom-call | flops 671088640 | bytes 10485760 | tf_op jit(solution)/shard_map/project/pallas_call | solution.py:24
  17.2 0.0 collective-permute-done.6.refs_3_
  17.2 1.2 %collective-permute-done.5.refs_2_ = f32[32,128]{1,0:T(8,128)S(1)} collective-permute-done((f32[32,128]{1,0:T(8,128)S(1)}, f32[32,128]{1,0:T(8,128)S(1)}, u32[]{:S(2)}, u32[]{:S(2)}) %collective-permute-start.5) | collective-permute-done | bytes 16416 | tf_op jit(solution)/shard_map/ppermute | solution.py:20
  18.5 0.0 collective-permute-done.4.refs_1_
  18.5 0.0 copy-done.2
  18.5 0.0 copy-done.3
  18.5 0.5 %raise_up.1 = (f32[16,2560]{1,0:T(8,128)S(1)}, bf16[16,2560]{1,0:T(8,128)(2,1)S(1)}, bf16[16,2560]{1,0:T(8,128)(2,1)S(1)}, bf16[16,2560]{1,0:T(8,128)(2,1)S(1)}) custom-call(bf16[32,64]{1,0:T(8,128)(2,1)S(1)} %get-tuple-element.21.seen_ref, f32[32,256]{1,0:T(8,128)S(1)} %get-tuple-element.22.mask_ref, f32[64,2560]{1,0:T(8,128)S(1)} %project.1.based_ref, ...), custom_call_target="tpu_custom_call" | custom-call | tf_op jit(solution)/shard_map/raise_up/pallas_call | solution.py:24
  18.9 3.4 %collective-permute-start.7 = (bf16[16,2560]{1,0:T(8,128)(2,1)S(1)}, bf16[16,2560]{1,0:T(8,128)(2,1)S(1)}, u32[]{:S(2)}, u32[]{:S(2)}) collective-permute-start(bf16[16,2560]{1,0:T(8,128)(2,1)S(1)} %get-tuple-element.34), channel_id=1, source_target_pairs={{0,12},{4,8},{8,4},{12,0},{1,13},{5,9},{9,5},{13,1},{2,14},{6,10},... | collective-permute-start | bytes 245768 | tf_op jit(solution)/shard_map/ppermute | solution.py:20
  22.3 0.0 collective-permute-start.8
  22.3 1.1 %collective-permute-start.9 = (bf16[16,2560]{1,0:T(8,128)(2,1)S(1)}, bf16[16,2560]{1,0:T(8,128)(2,1)S(1)}, u32[]{:S(2)}, u32[]{:S(2)}) collective-permute-start(bf16[16,2560]{1,0:T(8,128)(2,1)S(1)} %get-tuple-element.36), channel_id=1, source_target_pairs={{0,4},{4,0},{8,12},{12,8},{1,5},{5,1},{9,13},{13,9},{2,6},{6,2},{1... | collective-permute-start | bytes 245768 | tf_op jit(solution)/shard_map/ppermute | solution.py:20
  23.4 2.1 %collective-permute-done.7.refs_0_ = bf16[16,2560]{1,0:T(8,128)(2,1)S(1)} collective-permute-done((bf16[16,2560]{1,0:T(8,128)(2,1)S(1)}, bf16[16,2560]{1,0:T(8,128)(2,1)S(1)}, u32[]{:S(2)}, u32[]{:S(2)}) %collective-permute-start.7) | collective-permute-done | bytes 81952 | tf_op jit(solution)/shard_map/ppermute | solution.py:20
  25.5 3.3 %collective-permute-done.8.refs_1_ = bf16[16,2560]{1,0:T(8,128)(2,1)S(1)} collective-permute-done((bf16[16,2560]{1,0:T(8,128)(2,1)S(1)}, bf16[16,2560]{1,0:T(8,128)(2,1)S(1)}, u32[]{:S(2)}, u32[]{:S(2)}) %collective-permute-start.8) | collective-permute-done | bytes 81952 | tf_op jit(solution)/shard_map/ppermute | solution.py:20
  28.8 0.0 collective-permute-done.9.refs_2_
  28.8 0.0 copy-done
  28.9 0.0 copy-done.1
  28.9 0.0 copy-done.5
  28.9 2.6 %finish.1 = (bf16[16,2048]{1,0:T(8,128)(2,1)}, bf16[16,2,256]{2,1,0:T(2,128)(2,1)}) custom-call(s32[16]{0:T(128)S(1)} %copy-done.5, f32[16,128]{1,0:T(8,128)S(1)} %get-tuple-element.20.scale_ref, bf16[16,2,256,128]{3,2,1,0:T(8,128)(2,1)S(1)} %copy-done, bf16[16,2,256,128]{3,2,1,0:T(8,128)(2,1)S(1)} %copy-done.1, ...), custom_call_target="tpu_custom_call" | custom-call | tf_op jit(solution)/shard_map/finish/pallas_call | solution.py:24
Async XLA Ops:
  0.6 11.9 %copy-start.4 = (f32[8192]{0:T(1024)S(1)}, f32[8192]{0:T(1024)}, u32[]{:S(2)}) copy-start(f32[8192]{0:T(1024)} %param.14) | copy-start | bytes 98308
  1.8 10.2 %collective-permute-start = (bf16[32,1024]{1,0:T(8,128)(2,1)S(1)}, bf16[32,1024]{1,0:T(8,128)(2,1)S(1)}, u32[]{:S(2)}, u32[]{:S(2)}) collective-permute-start(bf16[32,1024]{1,0:T(8,128)(2,1)S(1)} %get-tuple-element.25), channel_id=1, source_target_pairs={{0,12},{4,8},{8,4},{12,0},{1,13},{5,9},{9,5},{13,1},{2,14},{6,10},... | collective-permute-start | bytes 196616 | tf_op jit(solution)/shard_map/ppermute | solution.py:20
  6.9 5.6 %collective-permute-start.1 = (bf16[32,1024]{1,0:T(8,128)(2,1)S(1)}, bf16[32,1024]{1,0:T(8,128)(2,1)S(1)}, u32[]{:S(2)}, u32[]{:S(2)}) collective-permute-start(bf16[32,1024]{1,0:T(8,128)(2,1)S(1)} %get-tuple-element.26), channel_id=1, source_target_pairs={{0,8},{4,12},{8,0},{12,4},{1,9},{5,13},{9,1},{13,5},{2,10},{6,14},... | collective-permute-start | bytes 196616 | tf_op jit(solution)/shard_map/ppermute | solution.py:20
  6.9 5.6 %collective-permute-start.2 = (bf16[32,1024]{1,0:T(8,128)(2,1)S(1)}, bf16[32,1024]{1,0:T(8,128)(2,1)S(1)}, u32[]{:S(2)}, u32[]{:S(2)}) collective-permute-start(bf16[32,1024]{1,0:T(8,128)(2,1)S(1)} %get-tuple-element.27), channel_id=1, source_target_pairs={{0,4},{4,0},{8,12},{12,8},{1,5},{5,1},{9,13},{13,9},{2,6},{6,2},{1... | collective-permute-start | bytes 196616 | tf_op jit(solution)/shard_map/ppermute | solution.py:20
  11.9 6.5 %copy-start.2 = (bf16[2,64,2048]{2,1,0:T(8,128)(2,1)S(1)}, bf16[2,64,2048]{2,1,0:T(8,128)(2,1)}, u32[]{:S(2)}) copy-start(bf16[2,64,2048]{2,1,0:T(8,128)(2,1)} %param.19) | copy-start | bytes 1572868
  11.9 6.5 %copy-start.3 = (bf16[2,64,256]{2,1,0:T(8,128)(2,1)S(1)}, bf16[2,64,256]{2,1,0:T(8,128)(2,1)}, u32[]{:S(2)}) copy-start(bf16[2,64,256]{2,1,0:T(8,128)(2,1)} %param.21) | copy-start | bytes 196612
  12.0 16.9 %copy-start = (bf16[16,2,256,128]{3,2,1,0:T(8,128)(2,1)S(1)}, bf16[16,2,256,128]{3,2,1,0:T(8,128)(2,1)}, u32[]{:S(2)}) copy-start(bf16[16,2,256,128]{3,2,1,0:T(8,128)(2,1)} %k_ref.1) | copy-start | bytes 6291460
  12.0 16.9 %copy-start.1 = (bf16[16,2,256,128]{3,2,1,0:T(8,128)(2,1)S(1)}, bf16[16,2,256,128]{3,2,1,0:T(8,128)(2,1)}, u32[]{:S(2)}) copy-start(bf16[16,2,256,128]{3,2,1,0:T(8,128)(2,1)} %v_ref.1) | copy-start | bytes 6291460
  12.0 16.9 %copy-start.5 = (s32[16]{0:T(128)S(1)}, s32[16]{0:T(128)}, u32[]{:S(2)}) copy-start(s32[16]{0:T(128)} %length_ref.1) | copy-start | bytes 196
  13.1 2.2 %collective-permute-start.3 = (bf16[64,1024]{1,0:T(8,128)(2,1)S(1)}, bf16[64,1024]{1,0:T(8,128)(2,1)S(1)}, u32[]{:S(2)}, u32[]{:S(2)}) collective-permute-start(bf16[64,1024]{1,0:T(8,128)(2,1)S(1)} %get-tuple-element.29.near_ref), channel_id=1, source_target_pairs={{0,1},{1,0},{2,3},{3,2},{4,5},{5,4},{6,7},{7,6},{8,9},{9,8},{10,11... | collective-permute-start | bytes 393224 | tf_op jit(solution)/shard_map/ppermute | solution.py:20
  13.1 4.1 %collective-permute-start.6 = (f32[32,128]{1,0:T(8,128)S(1)}, f32[32,128]{1,0:T(8,128)S(1)}, u32[]{:S(2)}, u32[]{:S(2)}) collective-permute-start(f32[32,128]{1,0:T(8,128)S(1)} %get-tuple-element.33.refs_0_), channel_id=1, source_target_pairs={{0,3},{1,2},{2,1},{3,0},{4,7},{5,6},{6,5},{7,4},{8,11},{9,10},{10,... | collective-permute-start | bytes 49160 | tf_op jit(solution)/shard_map/ppermute | solution.py:20
  14.7 3.7 %collective-permute-start.5 = (f32[32,128]{1,0:T(8,128)S(1)}, f32[32,128]{1,0:T(8,128)S(1)}, u32[]{:S(2)}, u32[]{:S(2)}) collective-permute-start(f32[32,128]{1,0:T(8,128)S(1)} %get-tuple-element.33.refs_0_), channel_id=1, source_target_pairs={{0,2},{1,3},{2,0},{3,1},{4,6},{5,7},{6,4},{7,5},{8,10},{9,11},{10,... | collective-permute-start | bytes 49160 | tf_op jit(solution)/shard_map/ppermute | solution.py:20
  15.3 3.2 %collective-permute-start.4 = (f32[32,128]{1,0:T(8,128)S(1)}, f32[32,128]{1,0:T(8,128)S(1)}, u32[]{:S(2)}, u32[]{:S(2)}) collective-permute-start(f32[32,128]{1,0:T(8,128)S(1)} %get-tuple-element.33.refs_0_), channel_id=1, source_target_pairs={{0,1},{1,0},{2,3},{3,2},{4,5},{5,4},{6,7},{7,6},{8,9},{9,8},{10,11... | collective-permute-start | bytes 49160 | tf_op jit(solution)/shard_map/ppermute | solution.py:20
  18.9 6.6 %collective-permute-start.7 = (bf16[16,2560]{1,0:T(8,128)(2,1)S(1)}, bf16[16,2560]{1,0:T(8,128)(2,1)S(1)}, u32[]{:S(2)}, u32[]{:S(2)}) collective-permute-start(bf16[16,2560]{1,0:T(8,128)(2,1)S(1)} %get-tuple-element.34), channel_id=1, source_target_pairs={{0,12},{4,8},{8,4},{12,0},{1,13},{5,9},{9,5},{13,1},{2,14},{6,10},... | collective-permute-start | bytes 245768 | tf_op jit(solution)/shard_map/ppermute | solution.py:20
  22.3 6.5 %collective-permute-start.8 = (bf16[16,2560]{1,0:T(8,128)(2,1)S(1)}, bf16[16,2560]{1,0:T(8,128)(2,1)S(1)}, u32[]{:S(2)}, u32[]{:S(2)}) collective-permute-start(bf16[16,2560]{1,0:T(8,128)(2,1)S(1)} %get-tuple-element.35), channel_id=1, source_target_pairs={{0,8},{4,12},{8,0},{12,4},{1,9},{5,13},{9,1},{13,5},{2,10},{6,14},... | collective-permute-start | bytes 245768 | tf_op jit(solution)/shard_map/ppermute | solution.py:20
  22.3 6.5 %collective-permute-start.9 = (bf16[16,2560]{1,0:T(8,128)(2,1)S(1)}, bf16[16,2560]{1,0:T(8,128)(2,1)S(1)}, u32[]{:S(2)}, u32[]{:S(2)}) collective-permute-start(bf16[16,2560]{1,0:T(8,128)(2,1)S(1)} %get-tuple-element.36), channel_id=1, source_target_pairs={{0,4},{4,0},{8,12},{12,8},{1,5},{5,1},{9,13},{13,9},{2,6},{6,2},{1... | collective-permute-start | bytes 245768 | tf_op jit(solution)/shard_map/ppermute | solution.py:20

commit v6 on v5

--- a/solution.py
+++ b/solution.py
@@ -11,7 +11,6 @@
 F32 = jnp.float32
 BF16 = jnp.bfloat16
 VMEM = pl.BlockSpec(memory_space=pltpu.VMEM)
-SMEM = pl.BlockSpec(memory_space=pltpu.SMEM)
 HBM = pl.BlockSpec(memory_space=pltpu.HBM)
 
 
@@ -161,14 +160,15 @@
 
     held = (query_down, value_down, query_weight, key_weight, value_weight)
 
-    def survey(ids_ref, x_ref, *refs):
+    def survey(ids_ref, x_ref, length_ref, *refs):
         count = len(held)
-        rms_ref, seen_ref, mask_ref, ids_copy, x_copy, sems = refs[2 * count :]
+        rms_ref, seen_ref, mask_ref, many_ref, ids_copy, x_copy, length_copy, sems = refs[2 * count :]
         copies = [
             pltpu.make_async_copy(ids_ref, ids_copy, sems.at[0]),
             pltpu.make_async_copy(x_ref, x_copy, sems.at[1]),
+            pltpu.make_async_copy(length_ref, length_copy, sems.at[2]),
         ] + [
-            pltpu.make_async_copy(refs[i], refs[count + i], sems.at[2 + i]) for i in range(count)
+            pltpu.make_async_copy(refs[i], refs[count + i], sems.at[3 + i]) for i in range(count)
         ]
         for copy in copies:
             copy.start()
@@ -186,27 +186,37 @@
             uses = jnp.sum(uses, axis=1, keepdims=True)
             mask = jnp.where(column == near, uses, mask)
         mask_ref[...] = mask
+        copies[2].wait()
+        same = iota((block_rows, block_rows), 0) == iota((block_rows, block_rows), 1)
+        many = jnp.sum(
+            jnp.where(same, length_copy[...].astype(F32), 0.0), axis=1, keepdims=True
+        )
+        many_ref[...] = jnp.broadcast_to(many, many_ref.shape)
         copies[1].wait()
         x = x_copy[...].astype(F32)
         mean = jnp.sum(x * x, axis=1, keepdims=True) * (1.0 / width)
         rms_ref[...] = jnp.broadcast_to(lax.rsqrt(mean + EPS), rms_ref.shape)
-        for copy in copies[2:]:
+        for copy in copies[3:]:
             copy.wait()
 
-    (w_query_down, w_value_down, w_query, w_key, w_value, row_scale, seen, mask) = call(
+    (w_query_down, w_value_down, w_query, w_key, w_value, row_scale, seen, mask,
+     row_length) = call(
         survey, "survey",
         [pltpu.VMEM(a.shape, a.dtype) for a in held]
         + [
             jax.ShapeDtypeStruct((block_rows, 128), F32),
             jax.ShapeDtypeStruct((slots, rows), BF16),
             jax.ShapeDtypeStruct((slots, 2 * low_cols), F32),
-        ],
-        [HBM] * (2 + len(held)), [VMEM] * (3 + len(held)),
-        (in_hbm(ids), in_hbm(residual_input), *(in_hbm(a) for a in held)),
+            jax.ShapeDtypeStruct((block_rows, context), F32),
+        ],
+        [HBM] * (3 + len(held)), [VMEM] * (4 + len(held)),
+        (in_hbm(ids), in_hbm(residual_input), in_hbm(cached_length.reshape(1, block_rows)),
+         *(in_hbm(a) for a in held)),
         scratch=[
             pltpu.VMEM((1, rows), jnp.int32),
             pltpu.VMEM((block_rows, width), BF16),
-            pltpu.SemaphoreType.DMA((2 + len(held),)),
+            pltpu.VMEM((1, block_rows), jnp.int32),
+            pltpu.SemaphoreType.DMA((3 + len(held),)),
         ],
         moved=12 * MIB,
     )
@@ -339,21 +349,64 @@
         for head in range(heads):
             q_ref[:, head, :] = sum_ref[:, head * head_dim : (head + 1) * head_dim]
         scale = head_dim ** (-0.5)
-        spot = iota((group_size, context), 1)
+        twin = 2 * group_size
+        spot = iota((twin, context), 1).astype(F32)
+        top = iota((twin, 1), 0) < group_size
+        keep = jnp.where(top, 1.0, 0.0)
+
+        def pair_of(index):
+            return divmod(index, kv_local), divmod(index + 1, kv_local)
+
+        def stacked(index, start):
+            (row_a, group_a), (row_b, group_b) = pair_of(index)
+            at_a, at_b = start + group_a * head_dim, start + group_b * head_dim
+            return jnp.where(
+                top,
+                sum_ref[row_a : row_a + 1, at_a : at_a + head_dim],
+                sum_ref[row_b : row_b + 1, at_b : at_b + head_dim],
+            )
+
+        def asked_of(index):
+            (row_a, group_a), (row_b, group_b) = pair_of(index)
+            return jnp.concatenate(
+                [
+                    q_ref[row_a, group_a * group_size : (group_a + 1) * group_size, :],
+                    q_ref[row_b, group_b * group_size : (group_b + 1) * group_size, :],
+                ],
+                axis=0,
+            )
+
+        def scores_of(index, asked):
+            (row_a, group_a), (row_b, group_b) = pair_of(index)
+            wide = jnp.concatenate([asked * keep, asked * (1.0 - keep)], axis=1).astype(BF16)
+            both = jnp.concatenate([k_ref[row_a, group_a], k_ref[row_b, group_b]], axis=1)
+            scores = lax.dot_general(
+                wide, both, (((1,), (1,)), ((), ())), preferred_element_type=F32
+            )
+            length = jnp.where(
+                top, length_ref[row_a : row_a + 1, :], length_ref[row_b : row_b + 1, :]
+            )
+            return jnp.where(spot < length, scores * scale, -jnp.inf)
+
+        def mixed_of(index, weights):
+            (row_a, group_a), (row_b, group_b) = pair_of(index)
+            both = jnp.concatenate([v_ref[row_a, group_a], v_ref[row_b, group_b]], axis=1)
+            mixed = jnp.dot(weights.astype(BF16), both, preferred_element_type=F32)
+            return jnp.concatenate(
+                [mixed[:group_size, :head_dim], mixed[group_size:, head_dim:]], axis=0
+            )
+
+        def put(index, mixed):
+            (row_a, group_a), (row_b, group_b) = pair_of(index)
+            o_ref[row_a, group_a * group_size : (group_a + 1) * group_size, :] = mixed[:group_size]
+            o_ref[row_b, group_b * group_size : (group_b + 1) * group_size, :] = mixed[group_size:]
+
+        pairs = range(0, block_rows * kv_local, 2)
         own = []
-        for row in range(block_rows):
-            for group in range(kv_local):
-                asked = q_ref[row, group * group_size : (group + 1) * group_size, :]
-                scores = lax.dot_general(
-                    asked.astype(BF16), k_ref[row, group], (((1,), (1,)), ((), ())),
-                    preferred_element_type=F32,
-                )
-                s_ref[row * kv_local + group] = jnp.where(
-                    spot < length_ref[row], scores * scale, -jnp.inf
-                )
-                at = query_cols + group * head_dim
-                new = sum_ref[row : row + 1, at : at + head_dim]
-                own.append(jnp.sum(asked * new, axis=1, keepdims=True))
+        for index in pairs:
+            asked = asked_of(index)
+            s_ref[index // 2] = scores_of(index, asked)
+            own.append(jnp.sum(asked * stacked(index, query_cols), axis=1, keepdims=True))
         own_score = jnp.stack(own) * scale
         scores = s_ref[...]
         peak = jnp.maximum(jnp.max(scores, axis=2, keepdims=True), own_score)
@@ -362,17 +415,9 @@
         inverse = 1.0 / (jnp.sum(lifted, axis=2, keepdims=True) + own_lift)
         s_ref[...] = lifted * inverse
         own_weight = (own_lift * inverse).astype(BF16).astype(F32)
-        for row in range(block_rows):
-            for group in range(kv_local):
-                index = row * kv_local + group
-                mixed = jnp.dot(
-                    s_ref[index].astype(BF16), v_ref[row, group], preferred_element_type=F32
-                )
-                at = query_cols + kv_cols + group * head_dim
-                new = sum_ref[row : row + 1, at : at + head_dim]
-                o_ref[row, group * group_size : (group + 1) * group_size, :] = (
-                    mixed + own_weight[index] * new
-                )
+        for index in pairs:
+            mixed = mixed_of(index, s_ref[index // 2])
+            put(index, mixed + own_weight[index // 2] * stacked(index, query_cols + kv_cols))
         for head in range(heads):
             out_ref[:, head * head_dim : (head + 1) * head_dim] = o_ref[:, head, :].astype(BF16)
 
@@ -382,12 +427,12 @@
             jax.ShapeDtypeStruct((block_rows, query_cols), BF16),
             jax.ShapeDtypeStruct((block_rows, 2, kv_cols), BF16),
         ],
-        [SMEM] + [VMEM] * (3 + owners_count), [VMEM] * 2,
-        (cached_length, row_scale, cached_key_rows, cached_value_rows, *parts),
+        [VMEM] * (4 + owners_count), [VMEM] * 2,
+        (row_length, row_scale, cached_key_rows, cached_value_rows, *parts),
         scratch=[
             pltpu.VMEM((block_rows, all_cols), F32),
             pltpu.VMEM((block_rows, heads, head_dim), F32),
-            pltpu.VMEM((block_rows * kv_local, group_size, context), F32),
+            pltpu.VMEM((block_rows * kv_local // 2, 2 * group_size, context), F32),
             pltpu.VMEM((block_rows, heads, head_dim), F32),
         ],
     )

time: 31.7 us -> 30.9 us (0.975)
  Pallas kernels: 11.1 us -> 10.4 us
    pallas_call x6, Pallas kernels: 11.1 us -> 10.4 us  [call(): pl.pallas_call(body, name=name, out_shape=outs, in_specs=in_specs, out_sp...]
  transfers between devices with their start and end apart: 10 -> 10, of which waited for: 4 -> 4; matrix products, arithmetic and copies ran while one was open for 0% -> 0% of each run, Pallas kernels for 20% -> 21%
where the time goes in v6:
time: 30.9 us; the launch traced here: 30.7 us
  starting transfers between devices  12.4 us (40%)
  Pallas kernels  10.4 us (34%)
  waiting for transfers between devices  7.18 us (23%)
  between operations  0.74 us (2%)
    ppermute x10, starting transfers between devices, partner(): return lax.ppermute(array, axis, [(i, i ^ step) for i in range(count)])  12.4 us
    pallas_call x6, Pallas kernels, call(): pl.pallas_call(body, name=name, out_shape=outs, in_specs=in_specs, out_sp...  10.4 us
    ppermute x10, waiting for transfers between devices, partner(): return lax.ppermute(array, axis, [(i, i ^ step) for i in range(count)])  7.18 us
  transfers between devices with their start and end apart: 10, of which 4 were waited for; matrix products, arithmetic and copies ran while one was open for 0% of the time, Pallas kernels for 21%

profile of v6, /device:TPU:0, one launch (start us, length us, event | category | flops | bytes accessed | tf_op | source)
XLA Modules:
  0.0 30.7 jit_solution(5136912756956120281)
XLA Ops:
  0.6 0.0 copy-start.4
  0.6 1.1 %prepare.1 = (bf16[32,1024]{1,0:T(8,128)(2,1)S(1)}, bf16[32,1024]{1,0:T(8,128)(2,1)S(1)}, bf16[32,1024]{1,0:T(8,128)(2,1)S(1)}, bf16[32,1024]{1,0:T(8,128)(2,1)S(1)}) custom-call(s32[1,64]{1,0:T(1,128)} %bitcast.16, bf16[16,8192]{1,0:T(8,128)(2,1)} %x_ref.3), custom_call_target="tpu_custom_call" | custom-call | bytes 524288 | tf_op jit(solution)/shard_map/prepare/pallas_call | solution.py:23
  1.8 5.1 %collective-permute-start = (bf16[32,1024]{1,0:T(8,128)(2,1)S(1)}, bf16[32,1024]{1,0:T(8,128)(2,1)S(1)}, u32[]{:S(2)}, u32[]{:S(2)}) collective-permute-start(bf16[32,1024]{1,0:T(8,128)(2,1)S(1)} %get-tuple-element.27), channel_id=1, source_target_pairs={{0,12},{4,8},{8,4},{12,0},{1,13},{5,9},{9,5},{13,1},{2,14},{6,10},... | collective-permute-start | bytes 196616 | tf_op jit(solution)/shard_map/ppermute | solution.py:19
  6.9 0.0 collective-permute-start.1
  6.9 0.6 %collective-permute-start.2 = (bf16[32,1024]{1,0:T(8,128)(2,1)S(1)}, bf16[32,1024]{1,0:T(8,128)(2,1)S(1)}, u32[]{:S(2)}, u32[]{:S(2)}) collective-permute-start(bf16[32,1024]{1,0:T(8,128)(2,1)S(1)} %get-tuple-element.29), channel_id=1, source_target_pairs={{0,4},{4,0},{8,12},{12,8},{1,5},{5,1},{9,13},{13,9},{2,6},{6,2},{1... | collective-permute-start | bytes 196616 | tf_op jit(solution)/shard_map/ppermute | solution.py:19
  7.5 4.4 %survey.1 = (bf16[128,2048]{1,0:T(8,128)(2,1)S(1)}, bf16[128,2048]{1,0:T(8,128)(2,1)S(1)}, bf16[2048,2048]{1,0:T(8,128)(2,1)S(1)}, bf16[2048,256]{1,0:T(8,128)(2...) custom-call(s32[1,64]{1,0:T(1,128)} %bitcast.17, ...), custom_call_target="tpu_custom_call" | custom-call | bytes 12582912 | tf_op jit(solution)/shard_map/survey/pallas_call | solution.py:23
  12.0 0.0 copy-start.2
  12.0 0.0 copy-start.3
  12.0 0.0 copy-start
  12.0 0.0 copy-start.1
  12.0 0.0 collective-permute-done.refs_0_
  12.0 0.5 %collective-permute-done.1.refs_1_ = bf16[32,1024]{1,0:T(8,128)(2,1)S(1)} collective-permute-done((bf16[32,1024]{1,0:T(8,128)(2,1)S(1)}, bf16[32,1024]{1,0:T(8,128)(2,1)S(1)}, u32[]{:S(2)}, u32[]{:S(2)}) %collective-permute-start.1) | collective-permute-done | bytes 65568 | tf_op jit(solution)/shard_map/ppermute | solution.py:19
  12.5 0.0 collective-permute-done.2.refs_2_
  12.5 0.0 copy-done.4
  12.5 0.6 %lower.1 = (f32[32,128]{1,0:T(8,128)S(1)}, bf16[64,1024]{1,0:T(8,128)(2,1)S(1)}) custom-call(f32[1,8192]{1,0:T(1,128)S(1)} %bitcast.13, f32[32,256]{1,0:T(8,128)S(1)} %get-tuple-element.24.mask_ref, bf16[128,2048]{1,0:T(8,128)(2,1)S(1)} %get-tuple-element.25.dq_ref, bf16[128,2048]{1,0:T(8,128)(2,1)S(1)} %get-tuple-element.26.dv_ref, ...), custom_call_target="tpu_custom_call" | custom-call | bytes 1048576 | tf_op jit(solution)/shard_map/lower/pallas_call | solution.py:23
  13.1 0.0 collective-permute-start.3
  13.1 1.6 %collective-permute-start.6 = (f32[32,128]{1,0:T(8,128)S(1)}, f32[32,128]{1,0:T(8,128)S(1)}, u32[]{:S(2)}, u32[]{:S(2)}) collective-permute-start(f32[32,128]{1,0:T(8,128)S(1)} %get-tuple-element.35.refs_0_), channel_id=1, source_target_pairs={{0,3},{1,2},{2,1},{3,0},{4,7},{5,6},{6,5},{7,4},{8,11},{9,10},{10,... | collective-permute-start | bytes 49160 | tf_op jit(solution)/shard_map/ppermute | solution.py:19
  14.7 0.5 %collective-permute-start.5 = (f32[32,128]{1,0:T(8,128)S(1)}, f32[32,128]{1,0:T(8,128)S(1)}, u32[]{:S(2)}, u32[]{:S(2)}) collective-permute-start(f32[32,128]{1,0:T(8,128)S(1)} %get-tuple-element.35.refs_0_), channel_id=1, source_target_pairs={{0,2},{1,3},{2,0},{3,1},{4,6},{5,7},{6,4},{7,5},{8,10},{9,11},{10,... | collective-permute-start | bytes 49160 | tf_op jit(solution)/shard_map/ppermute | solution.py:19
  15.3 0.0 collective-permute-start.4
  15.3 0.0 collective-permute-done.3.far_ref
  15.3 1.9 %project.1.based_ref = f32[64,2560]{1,0:T(8,128)S(1)} custom-call(bf16[64,1024]{1,0:T(8,128)(2,1)S(1)} %get-tuple-element.31.near_ref, bf16[64,1024]{1,0:T(8,128)(2,1)S(1)} %collective-permute-done.3.far_ref, bf16[2048,2048]{1,0:T(8,128)(2,1)S(1)} %get-tuple-element.32.wq_ref, bf16[2048,256]{1,0:T(8,128)(2,1)S(1)} %get-tuple-element.33.wk_ref, ...), custom_call_target="tpu_custom_call" | custom-call | flops 671088640 | bytes 10485760 | tf_op jit(solution)/shard_map/project/pallas_call | solution.py:23
  17.2 0.0 collective-permute-done.6.refs_3_
  17.2 1.2 %collective-permute-done.5.refs_2_ = f32[32,128]{1,0:T(8,128)S(1)} collective-permute-done((f32[32,128]{1,0:T(8,128)S(1)}, f32[32,128]{1,0:T(8,128)S(1)}, u32[]{:S(2)}, u32[]{:S(2)}) %collective-permute-start.5) | collective-permute-done | bytes 16416 | tf_op jit(solution)/shard_map/ppermute | solution.py:19
  18.5 0.0 collective-permute-done.4.refs_1_
  18.5 0.0 copy-done.2
  18.5 0.0 copy-done.3
  18.5 0.5 %raise_up.1 = (f32[16,2560]{1,0:T(8,128)S(1)}, bf16[16,2560]{1,0:T(8,128)(2,1)S(1)}, bf16[16,2560]{1,0:T(8,128)(2,1)S(1)}, bf16[16,2560]{1,0:T(8,128)(2,1)S(1)}) custom-call(bf16[32,64]{1,0:T(8,128)(2,1)S(1)} %get-tuple-element.23.seen_ref, f32[32,256]{1,0:T(8,128)S(1)} %get-tuple-element.24.mask_ref, f32[64,2560]{1,0:T(8,128)S(1)} %project.1.based_ref, ...), custom_call_target="tpu_custom_call" | custom-call | tf_op jit(solution)/shard_map/raise_up/pallas_call | solution.py:23
  18.9 3.4 %collective-permute-start.7 = (bf16[16,2560]{1,0:T(8,128)(2,1)S(1)}, bf16[16,2560]{1,0:T(8,128)(2,1)S(1)}, u32[]{:S(2)}, u32[]{:S(2)}) collective-permute-start(bf16[16,2560]{1,0:T(8,128)(2,1)S(1)} %get-tuple-element.36), channel_id=1, source_target_pairs={{0,12},{4,8},{8,4},{12,0},{1,13},{5,9},{9,5},{13,1},{2,14},{6,10},... | collective-permute-start | bytes 245768 | tf_op jit(solution)/shard_map/ppermute | solution.py:19
  22.3 0.0 collective-permute-start.8
  22.3 1.1 %collective-permute-start.9 = (bf16[16,2560]{1,0:T(8,128)(2,1)S(1)}, bf16[16,2560]{1,0:T(8,128)(2,1)S(1)}, u32[]{:S(2)}, u32[]{:S(2)}) collective-permute-start(bf16[16,2560]{1,0:T(8,128)(2,1)S(1)} %get-tuple-element.38), channel_id=1, source_target_pairs={{0,4},{4,0},{8,12},{12,8},{1,5},{5,1},{9,13},{13,9},{2,6},{6,2},{1... | collective-permute-start | bytes 245768 | tf_op jit(solution)/shard_map/ppermute | solution.py:19
  23.4 2.1 %collective-permute-done.7.refs_0_ = bf16[16,2560]{1,0:T(8,128)(2,1)S(1)} collective-permute-done((bf16[16,2560]{1,0:T(8,128)(2,1)S(1)}, bf16[16,2560]{1,0:T(8,128)(2,1)S(1)}, u32[]{:S(2)}, u32[]{:S(2)}) %collective-permute-start.7) | collective-permute-done | bytes 81952 | tf_op jit(solution)/shard_map/ppermute | solution.py:19
  25.6 3.3 %collective-permute-done.8.refs_1_ = bf16[16,2560]{1,0:T(8,128)(2,1)S(1)} collective-permute-done((bf16[16,2560]{1,0:T(8,128)(2,1)S(1)}, bf16[16,2560]{1,0:T(8,128)(2,1)S(1)}, u32[]{:S(2)}, u32[]{:S(2)}) %collective-permute-start.8) | collective-permute-done | bytes 81952 | tf_op jit(solution)/shard_map/ppermute | solution.py:19
  28.9 0.0 collective-permute-done.9.refs_2_
  28.9 0.0 copy-done
  28.9 0.0 copy-done.1
  28.9 1.9 %finish.1 = (bf16[16,2048]{1,0:T(8,128)(2,1)}, bf16[16,2,256]{2,1,0:T(2,128)(2,1)}) custom-call(f32[16,256]{1,0:T(8,128)S(1)} %get-tuple-element.21.length_ref, f32[16,128]{1,0:T(8,128)S(1)} %get-tuple-element.22.scale_ref, bf16[16,2,256,128]{3,2,1,0:T(8,128)(2,1)S(1)} %copy-done, bf16[16,2,256,128]{3,2,1,0:T(8,128)(2,1)S(1)} %copy-done.1, ...), custom_call_target="tpu_custom_call" | custom-call | tf_op jit(solution)/shard_map/finish/pallas_call | solution.py:23
Async XLA Ops:
  0.6 11.9 %copy-start.4 = (f32[8192]{0:T(1024)S(1)}, f32[8192]{0:T(1024)}, u32[]{:S(2)}) copy-start(f32[8192]{0:T(1024)} %param.14) | copy-start | bytes 98308
  1.8 10.2 %collective-permute-start = (bf16[32,1024]{1,0:T(8,128)(2,1)S(1)}, bf16[32,1024]{1,0:T(8,128)(2,1)S(1)}, u32[]{:S(2)}, u32[]{:S(2)}) collective-permute-start(bf16[32,1024]{1,0:T(8,128)(2,1)S(1)} %get-tuple-element.27), channel_id=1, source_target_pairs={{0,12},{4,8},{8,4},{12,0},{1,13},{5,9},{9,5},{13,1},{2,14},{6,10},... | collective-permute-start | bytes 196616 | tf_op jit(solution)/shard_map/ppermute | solution.py:19
  6.9 5.6 %collective-permute-start.1 = (bf16[32,1024]{1,0:T(8,128)(2,1)S(1)}, bf16[32,1024]{1,0:T(8,128)(2,1)S(1)}, u32[]{:S(2)}, u32[]{:S(2)}) collective-permute-start(bf16[32,1024]{1,0:T(8,128)(2,1)S(1)} %get-tuple-element.28), channel_id=1, source_target_pairs={{0,8},{4,12},{8,0},{12,4},{1,9},{5,13},{9,1},{13,5},{2,10},{6,14},... | collective-permute-start | bytes 196616 | tf_op jit(solution)/shard_map/ppermute | solution.py:19
  6.9 5.6 %collective-permute-start.2 = (bf16[32,1024]{1,0:T(8,128)(2,1)S(1)}, bf16[32,1024]{1,0:T(8,128)(2,1)S(1)}, u32[]{:S(2)}, u32[]{:S(2)}) collective-permute-start(bf16[32,1024]{1,0:T(8,128)(2,1)S(1)} %get-tuple-element.29), channel_id=1, source_target_pairs={{0,4},{4,0},{8,12},{12,8},{1,5},{5,1},{9,13},{13,9},{2,6},{6,2},{1... | collective-permute-start | bytes 196616 | tf_op jit(solution)/shard_map/ppermute | solution.py:19
  12.0 6.5 %copy-start.2 = (bf16[2,64,2048]{2,1,0:T(8,128)(2,1)S(1)}, bf16[2,64,2048]{2,1,0:T(8,128)(2,1)}, u32[]{:S(2)}) copy-start(bf16[2,64,2048]{2,1,0:T(8,128)(2,1)} %param.19) | copy-start | bytes 1572868
  12.0 6.5 %copy-start.3 = (bf16[2,64,256]{2,1,0:T(8,128)(2,1)S(1)}, bf16[2,64,256]{2,1,0:T(8,128)(2,1)}, u32[]{:S(2)}) copy-start(bf16[2,64,256]{2,1,0:T(8,128)(2,1)} %param.21) | copy-start | bytes 196612
  12.0 16.9 %copy-start = (bf16[16,2,256,128]{3,2,1,0:T(8,128)(2,1)S(1)}, bf16[16,2,256,128]{3,2,1,0:T(8,128)(2,1)}, u32[]{:S(2)}) copy-start(bf16[16,2,256,128]{3,2,1,0:T(8,128)(2,1)} %k_ref.1) | copy-start | bytes 6291460
  12.0 16.9 %copy-start.1 = (bf16[16,2,256,128]{3,2,1,0:T(8,128)(2,1)S(1)}, bf16[16,2,256,128]{3,2,1,0:T(8,128)(2,1)}, u32[]{:S(2)}) copy-start(bf16[16,2,256,128]{3,2,1,0:T(8,128)(2,1)} %v_ref.1) | copy-start | bytes 6291460
  13.1 2.2 %collective-permute-start.3 = (bf16[64,1024]{1,0:T(8,128)(2,1)S(1)}, bf16[64,1024]{1,0:T(8,128)(2,1)S(1)}, u32[]{:S(2)}, u32[]{:S(2)}) collective-permute-start(bf16[64,1024]{1,0:T(8,128)(2,1)S(1)} %get-tuple-element.31.near_ref), channel_id=1, source_target_pairs={{0,1},{1,0},{2,3},{3,2},{4,5},{5,4},{6,7},{7,6},{8,9},{9,8},{10,11... | collective-permute-start | bytes 393224 | tf_op jit(solution)/shard_map/ppermute | solution.py:19
  13.1 4.1 %collective-permute-start.6 = (f32[32,128]{1,0:T(8,128)S(1)}, f32[32,128]{1,0:T(8,128)S(1)}, u32[]{:S(2)}, u32[]{:S(2)}) collective-permute-start(f32[32,128]{1,0:T(8,128)S(1)} %get-tuple-element.35.refs_0_), channel_id=1, source_target_pairs={{0,3},{1,2},{2,1},{3,0},{4,7},{5,6},{6,5},{7,4},{8,11},{9,10},{10,... | collective-permute-start | bytes 49160 | tf_op jit(solution)/shard_map/ppermute | solution.py:19
  14.7 3.7 %collective-permute-start.5 = (f32[32,128]{1,0:T(8,128)S(1)}, f32[32,128]{1,0:T(8,128)S(1)}, u32[]{:S(2)}, u32[]{:S(2)}) collective-permute-start(f32[32,128]{1,0:T(8,128)S(1)} %get-tuple-element.35.refs_0_), channel_id=1, source_target_pairs={{0,2},{1,3},{2,0},{3,1},{4,6},{5,7},{6,4},{7,5},{8,10},{9,11},{10,... | collective-permute-start | bytes 49160 | tf_op jit(solution)/shard_map/ppermute | solution.py:19
  15.3 3.2 %collective-permute-start.4 = (f32[32,128]{1,0:T(8,128)S(1)}, f32[32,128]{1,0:T(8,128)S(1)}, u32[]{:S(2)}, u32[]{:S(2)}) collective-permute-start(f32[32,128]{1,0:T(8,128)S(1)} %get-tuple-element.35.refs_0_), channel_id=1, source_target_pairs={{0,1},{1,0},{2,3},{3,2},{4,5},{5,4},{6,7},{7,6},{8,9},{9,8},{10,11... | collective-permute-start | bytes 49160 | tf_op jit(solution)/shard_map/ppermute | solution.py:19
  18.9 6.6 %collective-permute-start.7 = (bf16[16,2560]{1,0:T(8,128)(2,1)S(1)}, bf16[16,2560]{1,0:T(8,128)(2,1)S(1)}, u32[]{:S(2)}, u32[]{:S(2)}) collective-permute-start(bf16[16,2560]{1,0:T(8,128)(2,1)S(1)} %get-tuple-element.36), channel_id=1, source_target_pairs={{0,12},{4,8},{8,4},{12,0},{1,13},{5,9},{9,5},{13,1},{2,14},{6,10},... | collective-permute-start | bytes 245768 | tf_op jit(solution)/shard_map/ppermute | solution.py:19
  22.3 6.5 %collective-permute-start.8 = (bf16[16,2560]{1,0:T(8,128)(2,1)S(1)}, bf16[16,2560]{1,0:T(8,128)(2,1)S(1)}, u32[]{:S(2)}, u32[]{:S(2)}) collective-permute-start(bf16[16,2560]{1,0:T(8,128)(2,1)S(1)} %get-tuple-element.37), channel_id=1, source_target_pairs={{0,8},{4,12},{8,0},{12,4},{1,9},{5,13},{9,1},{13,5},{2,10},{6,14},... | collective-permute-start | bytes 245768 | tf_op jit(solution)/shard_map/ppermute | solution.py:19
  22.3 6.5 %collective-permute-start.9 = (bf16[16,2560]{1,0:T(8,128)(2,1)S(1)}, bf16[16,2560]{1,0:T(8,128)(2,1)S(1)}, u32[]{:S(2)}, u32[]{:S(2)}) collective-permute-start(bf16[16,2560]{1,0:T(8,128)(2,1)S(1)} %get-tuple-element.38), channel_id=1, source_target_pairs={{0,4},{4,0},{8,12},{12,8},{1,5},{5,1},{9,13},{13,9},{2,6},{6,2},{1... | collective-permute-start | bytes 245768 | tf_op jit(solution)/shard_map/ppermute | solution.py:19

commit v7 on v6

--- a/solution.py
+++ b/solution.py
@@ -151,12 +151,15 @@
         moved=2**19,
     )
     per = len(sent) // owners_count
-    arrived = [list(sent[:per])] + [None] * (owners_count - 1)
-    for step in reversed(range(1, owners_count)):
-        arrived[step] = [
-            partner(piece, "adapter", step) for piece in sent[per * step : per * (step + 1)]
-        ]
-    arrived = sum(reversed(arrived), [])
+    first_order = list(reversed(range(1, owners_count)))
+    arrived = [
+        partner(piece, "adapter", step)
+        for step in first_order
+        for piece in sent[per * step : per * (step + 1)]
+    ] + list(sent[:per])
+
+    def place_of(step):
+        return first_order.index(step) if step else owners_count - 1
 
     held = (query_down, value_down, query_weight, key_weight, value_weight)
 
@@ -222,11 +225,11 @@
     )
 
     def base_of(refs, step):
-        at = owners_count - 1 - step
+        at = place_of(step)
         return refs[at][:block_rows, :] if joined else refs[2 * at][...]
 
     def slots_of(refs, step):
-        at = owners_count - 1 - step
+        at = place_of(step)
         if not joined:
             return refs[2 * at + 1][...].astype(F32)
         both = refs[at][block_rows:, :].astype(F32)
@@ -332,7 +335,7 @@
         scratch=[pltpu.VMEM((rows, all_cols), F32)],
     )
     parts = [
-        partner(parts[step], "adapter", step) for step in reversed(range(1, owners_count))
+        partner(parts[step], "adapter", step) for step in [*range(2, owners_count), 1]
     ] + [parts[0]]
 
     def finish(length_ref, scale_ref, k_ref, v_ref, *refs):

time: 30.9 us -> 30.2 us (0.977)
  starting transfers between devices: 12.4 us -> 11.9 us
    ppermute x10, starting transfers between devices: 12.4 us -> 11.9 us  [partner(): return lax.ppermute(array, axis, [(i, i ^ step) for i in range(count)])]
where the time goes in v7:
time: 30.2 us; the launch traced here: 30 us
  starting transfers between devices  11.9 us (39%)
  Pallas kernels  10.4 us (34%)
  waiting for transfers between devices  7 us (23%)
  between operations  0.74 us (2%)
    ppermute x10, starting transfers between devices, partner(): return lax.ppermute(array, axis, [(i, i ^ step) for i in range(count)])  11.9 us
    pallas_call x6, Pallas kernels, call(): pl.pallas_call(body, name=name, out_shape=outs, in_specs=in_specs, out_sp...  10.4 us
    ppermute x10, waiting for transfers between devices, partner(): return lax.ppermute(array, axis, [(i, i ^ step) for i in range(count)])  7 us
  transfers between devices with their start and end apart: 10, of which 4 were waited for; matrix products, arithmetic and copies ran while one was open for 0% of the time, Pallas kernels for 21%

profile of v7, /device:TPU:0, one launch (start us, length us, event | category | flops | bytes accessed | tf_op | source)
XLA Modules:
  0.0 30.0 jit_solution(18076993887832571598)
XLA Ops:
  0.6 0.0 copy-start.4
  0.6 1.1 %prepare.1 = (bf16[32,1024]{1,0:T(8,128)(2,1)S(1)}, bf16[32,1024]{1,0:T(8,128)(2,1)S(1)}, bf16[32,1024]{1,0:T(8,128)(2,1)S(1)}, bf16[32,1024]{1,0:T(8,128)(2,1)S(1)}) custom-call(s32[1,64]{1,0:T(1,128)} %bitcast.16, bf16[16,8192]{1,0:T(8,128)(2,1)} %x_ref.3), custom_call_target="tpu_custom_call" | custom-call | bytes 524288 | tf_op jit(solution)/shard_map/prepare/pallas_call | solution.py:23
  1.8 5.1 %collective-permute-start = (bf16[32,1024]{1,0:T(8,128)(2,1)S(1)}, bf16[32,1024]{1,0:T(8,128)(2,1)S(1)}, u32[]{:S(2)}, u32[]{:S(2)}) collective-permute-start(bf16[32,1024]{1,0:T(8,128)(2,1)S(1)} %get-tuple-element.27), channel_id=1, source_target_pairs={{0,12},{4,8},{8,4},{12,0},{1,13},{5,9},{9,5},{13,1},{2,14},{6,10},... | collective-permute-start | bytes 196616 | tf_op jit(solution)/shard_map/ppermute | solution.py:19
  6.9 0.0 collective-permute-start.1
  6.9 0.6 %collective-permute-start.2 = (bf16[32,1024]{1,0:T(8,128)(2,1)S(1)}, bf16[32,1024]{1,0:T(8,128)(2,1)S(1)}, u32[]{:S(2)}, u32[]{:S(2)}) collective-permute-start(bf16[32,1024]{1,0:T(8,128)(2,1)S(1)} %get-tuple-element.29), channel_id=1, source_target_pairs={{0,4},{4,0},{8,12},{12,8},{1,5},{5,1},{9,13},{13,9},{2,6},{6,2},{1... | collective-permute-start | bytes 196616 | tf_op jit(solution)/shard_map/ppermute | solution.py:19
  7.5 4.4 %survey.1 = (bf16[128,2048]{1,0:T(8,128)(2,1)S(1)}, bf16[128,2048]{1,0:T(8,128)(2,1)S(1)}, bf16[2048,2048]{1,0:T(8,128)(2,1)S(1)}, bf16[2048,256]{1,0:T(8,128)(2...) custom-call(s32[1,64]{1,0:T(1,128)} %bitcast.17, ...), custom_call_target="tpu_custom_call" | custom-call | bytes 12582912 | tf_op jit(solution)/shard_map/survey/pallas_call | solution.py:23
  12.0 0.0 copy-start.2
  12.0 0.0 copy-start.3
  12.0 0.0 copy-start
  12.0 0.0 copy-start.1
  12.0 0.0 collective-permute-done.refs_0_
  12.0 0.5 %collective-permute-done.1.refs_1_ = bf16[32,1024]{1,0:T(8,128)(2,1)S(1)} collective-permute-done((bf16[32,1024]{1,0:T(8,128)(2,1)S(1)}, bf16[32,1024]{1,0:T(8,128)(2,1)S(1)}, u32[]{:S(2)}, u32[]{:S(2)}) %collective-permute-start.1) | collective-permute-done | bytes 65568 | tf_op jit(solution)/shard_map/ppermute | solution.py:19
  12.5 0.0 collective-permute-done.2.refs_2_
  12.5 0.0 copy-done.4
  12.5 0.6 %lower.1 = (f32[32,128]{1,0:T(8,128)S(1)}, bf16[64,1024]{1,0:T(8,128)(2,1)S(1)}) custom-call(f32[1,8192]{1,0:T(1,128)S(1)} %bitcast.13, f32[32,256]{1,0:T(8,128)S(1)} %get-tuple-element.24.mask_ref, bf16[128,2048]{1,0:T(8,128)(2,1)S(1)} %get-tuple-element.25.dq_ref, bf16[128,2048]{1,0:T(8,128)(2,1)S(1)} %get-tuple-element.26.dv_ref, ...), custom_call_target="tpu_custom_call" | custom-call | bytes 1048576 | tf_op jit(solution)/shard_map/lower/pallas_call | solution.py:23
  13.1 0.0 collective-permute-start.3
  13.1 1.6 %collective-permute-start.6 = (f32[32,128]{1,0:T(8,128)S(1)}, f32[32,128]{1,0:T(8,128)S(1)}, u32[]{:S(2)}, u32[]{:S(2)}) collective-permute-start(f32[32,128]{1,0:T(8,128)S(1)} %get-tuple-element.35.refs_0_), channel_id=1, source_target_pairs={{0,3},{1,2},{2,1},{3,0},{4,7},{5,6},{6,5},{7,4},{8,11},{9,10},{10,... | collective-permute-start | bytes 49160 | tf_op jit(solution)/shard_map/ppermute | solution.py:19
  14.7 0.5 %collective-permute-start.5 = (f32[32,128]{1,0:T(8,128)S(1)}, f32[32,128]{1,0:T(8,128)S(1)}, u32[]{:S(2)}, u32[]{:S(2)}) collective-permute-start(f32[32,128]{1,0:T(8,128)S(1)} %get-tuple-element.35.refs_0_), channel_id=1, source_target_pairs={{0,2},{1,3},{2,0},{3,1},{4,6},{5,7},{6,4},{7,5},{8,10},{9,11},{10,... | collective-permute-start | bytes 49160 | tf_op jit(solution)/shard_map/ppermute | solution.py:19
  15.3 0.0 collective-permute-start.4
  15.3 0.0 collective-permute-done.3.far_ref
  15.3 1.9 %project.1.based_ref = f32[64,2560]{1,0:T(8,128)S(1)} custom-call(bf16[64,1024]{1,0:T(8,128)(2,1)S(1)} %get-tuple-element.31.near_ref, bf16[64,1024]{1,0:T(8,128)(2,1)S(1)} %collective-permute-done.3.far_ref, bf16[2048,2048]{1,0:T(8,128)(2,1)S(1)} %get-tuple-element.32.wq_ref, bf16[2048,256]{1,0:T(8,128)(2,1)S(1)} %get-tuple-element.33.wk_ref, ...), custom_call_target="tpu_custom_call" | custom-call | flops 671088640 | bytes 10485760 | tf_op jit(solution)/shard_map/project/pallas_call | solution.py:23
  17.2 0.0 collective-permute-done.6.refs_3_
  17.2 1.2 %collective-permute-done.5.refs_2_ = f32[32,128]{1,0:T(8,128)S(1)} collective-permute-done((f32[32,128]{1,0:T(8,128)S(1)}, f32[32,128]{1,0:T(8,128)S(1)}, u32[]{:S(2)}, u32[]{:S(2)}) %collective-permute-start.5) | collective-permute-done | bytes 16416 | tf_op jit(solution)/shard_map/ppermute | solution.py:19
  18.5 0.0 collective-permute-done.4.refs_1_
  18.5 0.0 copy-done.2
  18.5 0.0 copy-done.3
  18.5 0.5 %raise_up.1 = (f32[16,2560]{1,0:T(8,128)S(1)}, bf16[16,2560]{1,0:T(8,128)(2,1)S(1)}, bf16[16,2560]{1,0:T(8,128)(2,1)S(1)}, bf16[16,2560]{1,0:T(8,128)(2,1)S(1)}) custom-call(bf16[32,64]{1,0:T(8,128)(2,1)S(1)} %get-tuple-element.23.seen_ref, f32[32,256]{1,0:T(8,128)S(1)} %get-tuple-element.24.mask_ref, f32[64,2560]{1,0:T(8,128)S(1)} %project.1.based_ref, ...), custom_call_target="tpu_custom_call" | custom-call | tf_op jit(solution)/shard_map/raise_up/pallas_call | solution.py:23
  18.9 1.9 %collective-permute-start.7 = (bf16[16,2560]{1,0:T(8,128)(2,1)S(1)}, bf16[16,2560]{1,0:T(8,128)(2,1)S(1)}, u32[]{:S(2)}, u32[]{:S(2)}) collective-permute-start(bf16[16,2560]{1,0:T(8,128)(2,1)S(1)} %get-tuple-element.36), channel_id=1, source_target_pairs={{0,8},{4,12},{8,0},{12,4},{1,9},{5,13},{9,1},{13,5},{2,10},{6,14},... | collective-permute-start | bytes 245768 | tf_op jit(solution)/shard_map/ppermute | solution.py:19
  20.9 1.6 %collective-permute-start.8 = (bf16[16,2560]{1,0:T(8,128)(2,1)S(1)}, bf16[16,2560]{1,0:T(8,128)(2,1)S(1)}, u32[]{:S(2)}, u32[]{:S(2)}) collective-permute-start(bf16[16,2560]{1,0:T(8,128)(2,1)S(1)} %get-tuple-element.37), channel_id=1, source_target_pairs={{0,12},{4,8},{8,4},{12,0},{1,13},{5,9},{9,5},{13,1},{2,14},{6,10},... | collective-permute-start | bytes 245768 | tf_op jit(solution)/shard_map/ppermute | solution.py:19
  22.5 0.4 %collective-permute-start.9 = (bf16[16,2560]{1,0:T(8,128)(2,1)S(1)}, bf16[16,2560]{1,0:T(8,128)(2,1)S(1)}, u32[]{:S(2)}, u32[]{:S(2)}) collective-permute-start(bf16[16,2560]{1,0:T(8,128)(2,1)S(1)} %get-tuple-element.38), channel_id=1, source_target_pairs={{0,4},{4,0},{8,12},{12,8},{1,5},{5,1},{9,13},{13,9},{2,6},{6,2},{1... | collective-permute-start | bytes 245768 | tf_op jit(solution)/shard_map/ppermute | solution.py:19
  22.9 4.8 %collective-permute-done.7.refs_0_ = bf16[16,2560]{1,0:T(8,128)(2,1)S(1)} collective-permute-done((bf16[16,2560]{1,0:T(8,128)(2,1)S(1)}, bf16[16,2560]{1,0:T(8,128)(2,1)S(1)}, u32[]{:S(2)}, u32[]{:S(2)}) %collective-permute-start.7) | collective-permute-done | bytes 81952 | tf_op jit(solution)/shard_map/ppermute | solution.py:19
  27.7 0.0 collective-permute-done.8.refs_1_
  27.7 0.5 %collective-permute-done.9.refs_2_ = bf16[16,2560]{1,0:T(8,128)(2,1)S(1)} collective-permute-done((bf16[16,2560]{1,0:T(8,128)(2,1)S(1)}, bf16[16,2560]{1,0:T(8,128)(2,1)S(1)}, u32[]{:S(2)}, u32[]{:S(2)}) %collective-permute-start.9) | collective-permute-done | bytes 81952 | tf_op jit(solution)/shard_map/ppermute | solution.py:19
  28.2 0.0 copy-done
  28.2 0.0 copy-done.1
  28.2 1.9 %finish.1 = (bf16[16,2048]{1,0:T(8,128)(2,1)}, bf16[16,2,256]{2,1,0:T(2,128)(2,1)}) custom-call(f32[16,256]{1,0:T(8,128)S(1)} %get-tuple-element.21.length_ref, f32[16,128]{1,0:T(8,128)S(1)} %get-tuple-element.22.scale_ref, bf16[16,2,256,128]{3,2,1,0:T(8,128)(2,1)S(1)} %copy-done, bf16[16,2,256,128]{3,2,1,0:T(8,128)(2,1)S(1)} %copy-done.1, ...), custom_call_target="tpu_custom_call" | custom-call | tf_op jit(solution)/shard_map/finish/pallas_call | solution.py:23
Async XLA Ops:
  0.6 11.9 %copy-start.4 = (f32[8192]{0:T(1024)S(1)}, f32[8192]{0:T(1024)}, u32[]{:S(2)}) copy-start(f32[8192]{0:T(1024)} %param.14) | copy-start | bytes 98308
  1.8 10.2 %collective-permute-start = (bf16[32,1024]{1,0:T(8,128)(2,1)S(1)}, bf16[32,1024]{1,0:T(8,128)(2,1)S(1)}, u32[]{:S(2)}, u32[]{:S(2)}) collective-permute-start(bf16[32,1024]{1,0:T(8,128)(2,1)S(1)} %get-tuple-element.27), channel_id=1, source_target_pairs={{0,12},{4,8},{8,4},{12,0},{1,13},{5,9},{9,5},{13,1},{2,14},{6,10},... | collective-permute-start | bytes 196616 | tf_op jit(solution)/shard_map/ppermute | solution.py:19
  6.9 5.6 %collective-permute-start.1 = (bf16[32,1024]{1,0:T(8,128)(2,1)S(1)}, bf16[32,1024]{1,0:T(8,128)(2,1)S(1)}, u32[]{:S(2)}, u32[]{:S(2)}) collective-permute-start(bf16[32,1024]{1,0:T(8,128)(2,1)S(1)} %get-tuple-element.28), channel_id=1, source_target_pairs={{0,8},{4,12},{8,0},{12,4},{1,9},{5,13},{9,1},{13,5},{2,10},{6,14},... | collective-permute-start | bytes 196616 | tf_op jit(solution)/shard_map/ppermute | solution.py:19
  6.9 5.6 %collective-permute-start.2 = (bf16[32,1024]{1,0:T(8,128)(2,1)S(1)}, bf16[32,1024]{1,0:T(8,128)(2,1)S(1)}, u32[]{:S(2)}, u32[]{:S(2)}) collective-permute-start(bf16[32,1024]{1,0:T(8,128)(2,1)S(1)} %get-tuple-element.29), channel_id=1, source_target_pairs={{0,4},{4,0},{8,12},{12,8},{1,5},{5,1},{9,13},{13,9},{2,6},{6,2},{1... | collective-permute-start | bytes 196616 | tf_op jit(solution)/shard_map/ppermute | solution.py:19
  12.0 6.5 %copy-start.2 = (bf16[2,64,2048]{2,1,0:T(8,128)(2,1)S(1)}, bf16[2,64,2048]{2,1,0:T(8,128)(2,1)}, u32[]{:S(2)}) copy-start(bf16[2,64,2048]{2,1,0:T(8,128)(2,1)} %param.19) | copy-start | bytes 1572868
  12.0 6.5 %copy-start.3 = (bf16[2,64,256]{2,1,0:T(8,128)(2,1)S(1)}, bf16[2,64,256]{2,1,0:T(8,128)(2,1)}, u32[]{:S(2)}) copy-start(bf16[2,64,256]{2,1,0:T(8,128)(2,1)} %param.21) | copy-start | bytes 196612
  12.0 16.2 %copy-start = (bf16[16,2,256,128]{3,2,1,0:T(8,128)(2,1)S(1)}, bf16[16,2,256,128]{3,2,1,0:T(8,128)(2,1)}, u32[]{:S(2)}) copy-start(bf16[16,2,256,128]{3,2,1,0:T(8,128)(2,1)} %k_ref.1) | copy-start | bytes 6291460
  12.0 16.2 %copy-start.1 = (bf16[16,2,256,128]{3,2,1,0:T(8,128)(2,1)S(1)}, bf16[16,2,256,128]{3,2,1,0:T(8,128)(2,1)}, u32[]{:S(2)}) copy-start(bf16[16,2,256,128]{3,2,1,0:T(8,128)(2,1)} %v_ref.1) | copy-start | bytes 6291460
  13.1 2.2 %collective-permute-start.3 = (bf16[64,1024]{1,0:T(8,128)(2,1)S(1)}, bf16[64,1024]{1,0:T(8,128)(2,1)S(1)}, u32[]{:S(2)}, u32[]{:S(2)}) collective-permute-start(bf16[64,1024]{1,0:T(8,128)(2,1)S(1)} %get-tuple-element.31.near_ref), channel_id=1, source_target_pairs={{0,1},{1,0},{2,3},{3,2},{4,5},{5,4},{6,7},{7,6},{8,9},{9,8},{10,11... | collective-permute-start | bytes 393224 | tf_op jit(solution)/shard_map/ppermute | solution.py:19
  13.1 4.1 %collective-permute-start.6 = (f32[32,128]{1,0:T(8,128)S(1)}, f32[32,128]{1,0:T(8,128)S(1)}, u32[]{:S(2)}, u32[]{:S(2)}) collective-permute-start(f32[32,128]{1,0:T(8,128)S(1)} %get-tuple-element.35.refs_0_), channel_id=1, source_target_pairs={{0,3},{1,2},{2,1},{3,0},{4,7},{5,6},{6,5},{7,4},{8,11},{9,10},{10,... | collective-permute-start | bytes 49160 | tf_op jit(solution)/shard_map/ppermute | solution.py:19
  14.7 3.7 %collective-permute-start.5 = (f32[32,128]{1,0:T(8,128)S(1)}, f32[32,128]{1,0:T(8,128)S(1)}, u32[]{:S(2)}, u32[]{:S(2)}) collective-permute-start(f32[32,128]{1,0:T(8,128)S(1)} %get-tuple-element.35.refs_0_), channel_id=1, source_target_pairs={{0,2},{1,3},{2,0},{3,1},{4,6},{5,7},{6,4},{7,5},{8,10},{9,11},{10,... | collective-permute-start | bytes 49160 | tf_op jit(solution)/shard_map/ppermute | solution.py:19
  15.3 3.2 %collective-permute-start.4 = (f32[32,128]{1,0:T(8,128)S(1)}, f32[32,128]{1,0:T(8,128)S(1)}, u32[]{:S(2)}, u32[]{:S(2)}) collective-permute-start(f32[32,128]{1,0:T(8,128)S(1)} %get-tuple-element.35.refs_0_), channel_id=1, source_target_pairs={{0,1},{1,0},{2,3},{3,2},{4,5},{5,4},{6,7},{7,6},{8,9},{9,8},{10,11... | collective-permute-start | bytes 49160 | tf_op jit(solution)/shard_map/ppermute | solution.py:19
  18.9 8.7 %collective-permute-start.7 = (bf16[16,2560]{1,0:T(8,128)(2,1)S(1)}, bf16[16,2560]{1,0:T(8,128)(2,1)S(1)}, u32[]{:S(2)}, u32[]{:S(2)}) collective-permute-start(bf16[16,2560]{1,0:T(8,128)(2,1)S(1)} %get-tuple-element.36), channel_id=1, source_target_pairs={{0,8},{4,12},{8,0},{12,4},{1,9},{5,13},{9,1},{13,5},{2,10},{6,14},... | collective-permute-start | bytes 245768 | tf_op jit(solution)/shard_map/ppermute | solution.py:19
  20.9 6.8 %collective-permute-start.8 = (bf16[16,2560]{1,0:T(8,128)(2,1)S(1)}, bf16[16,2560]{1,0:T(8,128)(2,1)S(1)}, u32[]{:S(2)}, u32[]{:S(2)}) collective-permute-start(bf16[16,2560]{1,0:T(8,128)(2,1)S(1)} %get-tuple-element.37), channel_id=1, source_target_pairs={{0,12},{4,8},{8,4},{12,0},{1,13},{5,9},{9,5},{13,1},{2,14},{6,10},... | collective-permute-start | bytes 245768 | tf_op jit(solution)/shard_map/ppermute | solution.py:19
  22.5 5.7 %collective-permute-start.9 = (bf16[16,2560]{1,0:T(8,128)(2,1)S(1)}, bf16[16,2560]{1,0:T(8,128)(2,1)S(1)}, u32[]{:S(2)}, u32[]{:S(2)}) collective-permute-start(bf16[16,2560]{1,0:T(8,128)(2,1)S(1)} %get-tuple-element.38), channel_id=1, source_target_pairs={{0,4},{4,0},{8,12},{12,8},{1,5},{5,1},{9,13},{13,9},{2,6},{6,2},{1... | collective-permute-start | bytes 245768 | tf_op jit(solution)/shard_map/ppermute | solution.py:19

commit v8 on v7

--- a/solution.py
+++ b/solution.py
@@ -111,15 +111,17 @@
             copies.append(pltpu.make_async_copy(x_ref.at[:, at], target, sems.at[step]))
         for copy in copies:
             copy.start()
+        owner = jnp.bitwise_xor(me, iota((slots, rows), 0) // capacity) * nearby
+        row, spot = iota((rows, block_rows), 0), iota((rows, block_rows), 1) + me * block_rows
+        fold = jnp.where(row == spot, 1.0, 0.0).astype(BF16)
+        before = jnp.where((row < spot) & (row >= me * block_rows), 1.0, 0.0).astype(BF16)
+        which = lax.rem(iota((slots, block_rows), 0), capacity).astype(F32)
         copies[0].wait()
-        owner = jnp.bitwise_xor(me, iota((slots, 1), 0) // capacity)
-        chosen = slot_map(
-            chosen_ids[...], owner, jnp.full((slots, 1), me), capacity, block_rows, nearby
-        )
-        fold = lax.rem(iota((rows, block_rows), 0), block_rows) == iota((rows, block_rows), 1)
-        chosen = jnp.dot(
-            chosen.astype(BF16), jnp.where(fold, 1.0, 0.0).astype(BF16), preferred_element_type=F32
-        )
+        taken = chosen_ids[...]
+        hit = jnp.where((taken >= owner) & (taken < owner + nearby), 1.0, 0.0).astype(BF16)
+        mine = jnp.dot(hit, fold, preferred_element_type=F32)
+        place = jnp.dot(hit, before, preferred_element_type=F32)
+        chosen = jnp.where((mine > 0.5) & (place == which), 1.0, 0.0)
         copies[1].wait()
         placed = jnp.dot(chosen.astype(BF16), part[...], preferred_element_type=F32)
         for step in range(owners_count):
@@ -162,16 +164,24 @@
         return first_order.index(step) if step else owners_count - 1
 
     held = (query_down, value_down, query_weight, key_weight, value_weight)
+    made = [
+        pltpu.VMEM((2 * low_cols, lane_width), BF16),
+        *(pltpu.VMEM(a.shape, a.dtype) for a in held[2:]),
+    ]
 
     def survey(ids_ref, x_ref, length_ref, *refs):
         count = len(held)
-        rms_ref, seen_ref, mask_ref, many_ref, ids_copy, x_copy, length_copy, sems = refs[2 * count :]
+        rms_ref, seen_ref, mask_ref, many_ref, ids_copy, x_copy, length_copy, sems = refs[2 * count - 1 :]
+        targets = [
+            refs[count].at[:low_cols, :], refs[count].at[low_cols:, :],
+            *refs[count + 1 : 2 * count - 1],
+        ]
         copies = [
             pltpu.make_async_copy(ids_ref, ids_copy, sems.at[0]),
             pltpu.make_async_copy(x_ref, x_copy, sems.at[1]),
             pltpu.make_async_copy(length_ref, length_copy, sems.at[2]),
         ] + [
-            pltpu.make_async_copy(refs[i], refs[count + i], sems.at[3 + i]) for i in range(count)
+            pltpu.make_async_copy(refs[i], targets[i], sems.at[3 + i]) for i in range(count)
         ]
         for copy in copies:
             copy.start()
@@ -181,7 +191,12 @@
         seen = slot_map(
             ids_copy[...], jnp.full((slots, 1), me), block, capacity, block_rows, nearby
         )
-        seen_ref[...] = seen.astype(BF16)
+        spot = iota((rows, rows), 1)
+        mirror = jnp.bitwise_xor(me, spot // block_rows) * block_rows + lax.rem(spot, block_rows)
+        mirror = jnp.where(iota((rows, rows), 0) == mirror, 1.0, 0.0).astype(BF16)
+        seen_ref[...] = jnp.dot(
+            seen.astype(BF16), mirror, preferred_element_type=F32
+        ).astype(BF16)
         column = lax.rem(iota((slots, 2 * low_cols), 1) // rank, nearby)
         mask = jnp.zeros((slots, 2 * low_cols), F32)
         for near in range(nearby):
@@ -202,17 +217,17 @@
         for copy in copies[3:]:
             copy.wait()
 
-    (w_query_down, w_value_down, w_query, w_key, w_value, row_scale, seen, mask,
+    (w_down, w_query, w_key, w_value, row_scale, seen, mask,
      row_length) = call(
         survey, "survey",
-        [pltpu.VMEM(a.shape, a.dtype) for a in held]
+        made
         + [
             jax.ShapeDtypeStruct((block_rows, 128), F32),
             jax.ShapeDtypeStruct((slots, rows), BF16),
             jax.ShapeDtypeStruct((slots, 2 * low_cols), F32),
             jax.ShapeDtypeStruct((block_rows, context), F32),
         ],
-        [HBM] * (3 + len(held)), [VMEM] * (4 + len(held)),
+        [HBM] * (3 + len(held)), [VMEM] * (4 + len(made)),
         (in_hbm(ids), in_hbm(residual_input), in_hbm(cached_length.reshape(1, block_rows)),
          *(in_hbm(a) for a in held)),
         scratch=[
@@ -235,7 +250,7 @@
         both = refs[at][block_rows:, :].astype(F32)
         return jnp.concatenate([both[:capacity], both[capacity:]], axis=1)
 
-    def lower(gain_ref, mask_ref, dq_ref, dv_ref, *refs):
+    def lower(gain_ref, mask_ref, down_ref, *refs):
         part_refs, out_ref, half_ref = refs[:-2], refs[-2], refs[-1]
         lane = lax.axis_index("lane")
         scaled = gain_ref[:, pl.ds(pl.multiple_of(lane * lane_width, lane_width), lane_width)]
@@ -244,20 +259,20 @@
         )
         taken = (taken * scaled).astype(BF16)
         contract = (((1,), (1,)), ((), ()))
-        for at, ref in enumerate((dq_ref, dv_ref)):
-            every = mask_ref[:, at * low_cols : (at + 1) * low_cols] * lax.dot_general(
-                taken, ref[...], contract, preferred_element_type=F32
-            )
-            picked = every[:, :rank]
+        every = mask_ref[...] * lax.dot_general(
+            taken, down_ref[...], contract, preferred_element_type=F32
+        )
+        for at in range(2):
+            first = at * low_cols
+            picked = every[:, first : first + rank]
             for near in range(1, nearby):
-                picked = picked + every[:, near * rank : (near + 1) * rank]
+                picked = picked + every[:, first + near * rank : first + (near + 1) * rank]
             out_ref[:, at * rank : (at + 1) * rank] = picked
         me = lax.axis_index("adapter")
         first = me * base_width + lax.rem(lane, 2) * half
         scaled = gain_ref[:, pl.ds(pl.multiple_of(first, half), half)]
         for step in range(owners_count):
-            start = pl.multiple_of(jnp.bitwise_xor(me, step) * block_rows, block_rows)
-            half_ref[pl.ds(start, block_rows), :] = (
+            half_ref[step * block_rows : (step + 1) * block_rows, :] = (
                 base_of(part_refs, step).astype(F32) * scaled
             ).astype(BF16)
 
@@ -267,8 +282,8 @@
             jax.ShapeDtypeStruct((slots, 2 * rank), F32),
             jax.ShapeDtypeStruct((rows, half), BF16),
         ],
-        [VMEM] * (4 + len(arrived)), [VMEM] * 2,
-        (gain, mask, w_query_down, w_value_down, *arrived),
+        [VMEM] * (3 + len(arrived)), [VMEM] * 2,
+        (gain, mask, w_down, *arrived),
         moved=MIB,
     )
     far_half = partner(near_half, "lane", 1)
@@ -298,8 +313,7 @@
     )
 
     def raise_up(seen_ref, mask_ref, based_ref, uq_ref, uv_ref, *refs):
-        low_refs, out_refs, sum_ref = refs[:lane_count], refs[lane_count:-1], refs[-1]
-        me = lax.axis_index("adapter")
+        low_refs, out_refs = refs[:lane_count], refs[lane_count:]
         total = low_refs[0][...]
         for ref in low_refs[1:]:
             total = total + ref[...]
@@ -309,20 +323,25 @@
             seen_ref[...], spread.astype(BF16), (((0,), (0,)), ((), ())),
             preferred_element_type=F32,
         ).astype(BF16)
-        for at in range(0, query_cols, 1024):
-            stop = min(at + 1024, query_cols)
-            sum_ref[:, at:stop] = based_ref[:, at:stop] + ADAPTER_SCALE * jnp.dot(
-                lowered[:, :low_cols], uq_ref[:, at:stop], preferred_element_type=F32
-            )
         middle = slice(query_cols, query_cols + kv_cols)
         last = slice(query_cols + kv_cols, all_cols)
-        sum_ref[:, middle] = based_ref[:, middle]
-        sum_ref[:, last] = based_ref[:, last] + ADAPTER_SCALE * jnp.dot(
-            lowered[:, low_cols:], uv_ref[...], preferred_element_type=F32
-        )
+        tile = min(1024, query_cols)
+        pieces = [(slice(at, at + tile), 0, uq_ref, at) for at in range(0, query_cols, tile)]
+        pieces.append((last, low_cols, uv_ref, 0))
+        for columns, first, weight_ref, at in pieces:
+            size = columns.stop - columns.start
+            raised = based_ref[:, columns] + ADAPTER_SCALE * jnp.dot(
+                lowered[:, first : first + low_cols], weight_ref[:, at : at + size],
+                preferred_element_type=F32,
+            )
+            for step in range(owners_count):
+                out_refs[step][:, columns] = raised[
+                    step * block_rows : (step + 1) * block_rows
+                ].astype(out_refs[step].dtype)
         for step in range(owners_count):
-            start = pl.multiple_of(jnp.bitwise_xor(me, step) * block_rows, block_rows)
-            out_refs[step][...] = sum_ref[pl.ds(start, block_rows), :].astype(out_refs[step].dtype)
+            out_refs[step][:, middle] = based_ref[
+                step * block_rows : (step + 1) * block_rows, middle
+            ].astype(out_refs[step].dtype)
 
     parts = call(
         raise_up, "raise_up",
@@ -332,7 +351,6 @@
         ],
         [VMEM] * (5 + lane_count), [VMEM] * owners_count,
         (seen, mask, based, query_up, value_up, *lows),
-        scratch=[pltpu.VMEM((rows, all_cols), F32)],
     )
     parts = [
         partner(parts[step], "adapter", step) for step in [*range(2, owners_count), 1]

time: 30.2 us -> 30.1 us (level)
  no operation moved by 1% of the time
where the time goes in v8:
time: 30.1 us; the launch traced here: 29.9 us
  starting transfers between devices  11.8 us (39%)
  Pallas kernels  10.3 us (34%)
  waiting for transfers between devices  7.01 us (23%)
  between operations  0.74 us (2%)
    ppermute x10, starting transfers between devices, partner(): return lax.ppermute(array, axis, [(i, i ^ step) for i in range(count)])  11.8 us
    pallas_call x6, Pallas kernels, call(): pl.pallas_call(body, name=name, out_shape=outs, in_specs=in_specs, out_sp...  10.3 us
    ppermute x10, waiting for transfers between devices, partner(): return lax.ppermute(array, axis, [(i, i ^ step) for i in range(count)])  7.01 us
  transfers between devices with their start and end apart: 10, of which 4 were waited for; matrix products, arithmetic and copies ran while one was open for 0% of the time, Pallas kernels for 21%

profile of v8, /device:TPU:0, one launch (start us, length us, event | category | flops | bytes accessed | tf_op | source)
XLA Modules:
  0.0 29.9 jit_solution(15722560445311269928)
XLA Ops:
  0.6 0.0 copy-start.4
  0.6 1.1 %prepare.1 = (bf16[32,1024]{1,0:T(8,128)(2,1)S(1)}, bf16[32,1024]{1,0:T(8,128)(2,1)S(1)}, bf16[32,1024]{1,0:T(8,128)(2,1)S(1)}, bf16[32,1024]{1,0:T(8,128)(2,1)S(1)}) custom-call(s32[1,64]{1,0:T(1,128)} %bitcast.16, bf16[16,8192]{1,0:T(8,128)(2,1)} %x_ref.3), custom_call_target="tpu_custom_call" | custom-call | bytes 524288 | tf_op jit(solution)/shard_map/prepare/pallas_call | solution.py:23
  1.7 5.1 %collective-permute-start = (bf16[32,1024]{1,0:T(8,128)(2,1)S(1)}, bf16[32,1024]{1,0:T(8,128)(2,1)S(1)}, u32[]{:S(2)}, u32[]{:S(2)}) collective-permute-start(bf16[32,1024]{1,0:T(8,128)(2,1)S(1)} %get-tuple-element.25), channel_id=1, source_target_pairs={{0,12},{4,8},{8,4},{12,0},{1,13},{5,9},{9,5},{13,1},{2,14},{6,10},... | collective-permute-start | bytes 196616 | tf_op jit(solution)/shard_map/ppermute | solution.py:19
  6.8 0.0 collective-permute-start.1
  6.8 0.6 %collective-permute-start.2 = (bf16[32,1024]{1,0:T(8,128)(2,1)S(1)}, bf16[32,1024]{1,0:T(8,128)(2,1)S(1)}, u32[]{:S(2)}, u32[]{:S(2)}) collective-permute-start(bf16[32,1024]{1,0:T(8,128)(2,1)S(1)} %get-tuple-element.27), channel_id=1, source_target_pairs={{0,4},{4,0},{8,12},{12,8},{1,5},{5,1},{9,13},{13,9},{2,6},{6,2},{1... | collective-permute-start | bytes 196616 | tf_op jit(solution)/shard_map/ppermute | solution.py:19
  7.5 4.4 %survey.1 = (bf16[256,2048]{1,0:T(8,128)(2,1)S(1)}, bf16[2048,2048]{1,0:T(8,128)(2,1)S(1)}, bf16[2048,256]{1,0:T(8,128)(2,1)S(1)}, bf16[2048,256]{1,0:T(8,128)(2...) custom-call(s32[1,64]{1,0:T(1,128)} %bitcast.17, ...), custom_call_target="tpu_custom_call" | custom-call | bytes 12582912 | tf_op jit(solution)/shard_map/survey/pallas_call | solution.py:23
  11.9 0.0 copy-start.2
  11.9 0.0 copy-start.3
  11.9 0.0 copy-start
  11.9 0.0 copy-start.1
  12.0 0.0 collective-permute-done.refs_0_
  12.0 0.5 %collective-permute-done.1.refs_1_ = bf16[32,1024]{1,0:T(8,128)(2,1)S(1)} collective-permute-done((bf16[32,1024]{1,0:T(8,128)(2,1)S(1)}, bf16[32,1024]{1,0:T(8,128)(2,1)S(1)}, u32[]{:S(2)}, u32[]{:S(2)}) %collective-permute-start.1) | collective-permute-done | bytes 65568 | tf_op jit(solution)/shard_map/ppermute | solution.py:19
  12.4 0.0 collective-permute-done.2.refs_2_
  12.4 0.0 copy-done.4
  12.4 0.6 %lower.1 = (f32[32,128]{1,0:T(8,128)S(1)}, bf16[64,1024]{1,0:T(8,128)(2,1)S(1)}) custom-call(f32[1,8192]{1,0:T(1,128)S(1)} %bitcast.13, f32[32,256]{1,0:T(8,128)S(1)} %get-tuple-element.23.mask_ref, bf16[256,2048]{1,0:T(8,128)(2,1)S(1)} %get-tuple-element.24.down_ref, bf16[32,1024]{1,0:T(8,128)(2,1)S(1)} %collective-permute-done.refs_0_, ...), custom_call_target="tpu_custom_call" | custom-call | bytes 1048576 | tf_op jit(solution)/shard_map/lower/pallas_call | solution.py:23
  13.0 0.0 collective-permute-start.3
  13.0 1.6 %collective-permute-start.6 = (f32[32,128]{1,0:T(8,128)S(1)}, f32[32,128]{1,0:T(8,128)S(1)}, u32[]{:S(2)}, u32[]{:S(2)}) collective-permute-start(f32[32,128]{1,0:T(8,128)S(1)} %get-tuple-element.33.refs_0_), channel_id=1, source_target_pairs={{0,3},{1,2},{2,1},{3,0},{4,7},{5,6},{6,5},{7,4},{8,11},{9,10},{10,... | collective-permute-start | bytes 49160 | tf_op jit(solution)/shard_map/ppermute | solution.py:19
  14.6 0.5 %collective-permute-start.5 = (f32[32,128]{1,0:T(8,128)S(1)}, f32[32,128]{1,0:T(8,128)S(1)}, u32[]{:S(2)}, u32[]{:S(2)}) collective-permute-start(f32[32,128]{1,0:T(8,128)S(1)} %get-tuple-element.33.refs_0_), channel_id=1, source_target_pairs={{0,2},{1,3},{2,0},{3,1},{4,6},{5,7},{6,4},{7,5},{8,10},{9,11},{10,... | collective-permute-start | bytes 49160 | tf_op jit(solution)/shard_map/ppermute | solution.py:19
  15.2 0.0 collective-permute-start.4
  15.2 0.0 collective-permute-done.3.far_ref
  15.2 1.9 %project.1.based_ref = f32[64,2560]{1,0:T(8,128)S(1)} custom-call(bf16[64,1024]{1,0:T(8,128)(2,1)S(1)} %get-tuple-element.29.near_ref, bf16[64,1024]{1,0:T(8,128)(2,1)S(1)} %collective-permute-done.3.far_ref, bf16[2048,2048]{1,0:T(8,128)(2,1)S(1)} %get-tuple-element.30.wq_ref, bf16[2048,256]{1,0:T(8,128)(2,1)S(1)} %get-tuple-element.31.wk_ref, ...), custom_call_target="tpu_custom_call" | custom-call | flops 671088640 | bytes 10485760 | tf_op jit(solution)/shard_map/project/pallas_call | solution.py:23
  17.1 0.0 collective-permute-done.6.refs_3_
  17.1 1.2 %collective-permute-done.5.refs_2_ = f32[32,128]{1,0:T(8,128)S(1)} collective-permute-done((f32[32,128]{1,0:T(8,128)S(1)}, f32[32,128]{1,0:T(8,128)S(1)}, u32[]{:S(2)}, u32[]{:S(2)}) %collective-permute-start.5) | collective-permute-done | bytes 16416 | tf_op jit(solution)/shard_map/ppermute | solution.py:19
  18.4 0.0 collective-permute-done.4.refs_1_
  18.4 0.0 copy-done.2
  18.4 0.0 copy-done.3
  18.4 0.4 %raise_up.1 = (f32[16,2560]{1,0:T(8,128)S(1)}, bf16[16,2560]{1,0:T(8,128)(2,1)S(1)}, bf16[16,2560]{1,0:T(8,128)(2,1)S(1)}, bf16[16,2560]{1,0:T(8,128)(2,1)S(1)}) custom-call(bf16[32,64]{1,0:T(8,128)(2,1)S(1)} %get-tuple-element.22.seen_ref, f32[32,256]{1,0:T(8,128)S(1)} %get-tuple-element.23.mask_ref, f32[64,2560]{1,0:T(8,128)S(1)} %project.1.based_ref, ...), custom_call_target="tpu_custom_call" | custom-call | tf_op jit(solution)/shard_map/raise_up/pallas_call | solution.py:23
  18.8 1.9 %collective-permute-start.7 = (bf16[16,2560]{1,0:T(8,128)(2,1)S(1)}, bf16[16,2560]{1,0:T(8,128)(2,1)S(1)}, u32[]{:S(2)}, u32[]{:S(2)}) collective-permute-start(bf16[16,2560]{1,0:T(8,128)(2,1)S(1)} %get-tuple-element.34), channel_id=1, source_target_pairs={{0,8},{4,12},{8,0},{12,4},{1,9},{5,13},{9,1},{13,5},{2,10},{6,14},... | collective-permute-start | bytes 245768 | tf_op jit(solution)/shard_map/ppermute | solution.py:19
  20.7 1.6 %collective-permute-start.8 = (bf16[16,2560]{1,0:T(8,128)(2,1)S(1)}, bf16[16,2560]{1,0:T(8,128)(2,1)S(1)}, u32[]{:S(2)}, u32[]{:S(2)}) collective-permute-start(bf16[16,2560]{1,0:T(8,128)(2,1)S(1)} %get-tuple-element.35), channel_id=1, source_target_pairs={{0,12},{4,8},{8,4},{12,0},{1,13},{5,9},{9,5},{13,1},{2,14},{6,10},... | collective-permute-start | bytes 245768 | tf_op jit(solution)/shard_map/ppermute | solution.py:19
  22.3 0.4 %collective-permute-start.9 = (bf16[16,2560]{1,0:T(8,128)(2,1)S(1)}, bf16[16,2560]{1,0:T(8,128)(2,1)S(1)}, u32[]{:S(2)}, u32[]{:S(2)}) collective-permute-start(bf16[16,2560]{1,0:T(8,128)(2,1)S(1)} %get-tuple-element.36), channel_id=1, source_target_pairs={{0,4},{4,0},{8,12},{12,8},{1,5},{5,1},{9,13},{13,9},{2,6},{6,2},{1... | collective-permute-start | bytes 245768 | tf_op jit(solution)/shard_map/ppermute | solution.py:19
  22.7 4.8 %collective-permute-done.7.refs_0_ = bf16[16,2560]{1,0:T(8,128)(2,1)S(1)} collective-permute-done((bf16[16,2560]{1,0:T(8,128)(2,1)S(1)}, bf16[16,2560]{1,0:T(8,128)(2,1)S(1)}, u32[]{:S(2)}, u32[]{:S(2)}) %collective-permute-start.7) | collective-permute-done | bytes 81952 | tf_op jit(solution)/shard_map/ppermute | solution.py:19
  27.5 0.0 collective-permute-done.8.refs_1_
  27.5 0.5 %collective-permute-done.9.refs_2_ = bf16[16,2560]{1,0:T(8,128)(2,1)S(1)} collective-permute-done((bf16[16,2560]{1,0:T(8,128)(2,1)S(1)}, bf16[16,2560]{1,0:T(8,128)(2,1)S(1)}, u32[]{:S(2)}, u32[]{:S(2)}) %collective-permute-start.9) | collective-permute-done | bytes 81952 | tf_op jit(solution)/shard_map/ppermute | solution.py:19
  28.0 0.0 copy-done
  28.0 0.0 copy-done.1
  28.0 1.9 %finish.1 = (bf16[16,2048]{1,0:T(8,128)(2,1)}, bf16[16,2,256]{2,1,0:T(2,128)(2,1)}) custom-call(f32[16,256]{1,0:T(8,128)S(1)} %get-tuple-element.20.length_ref, f32[16,128]{1,0:T(8,128)S(1)} %get-tuple-element.21.scale_ref, bf16[16,2,256,128]{3,2,1,0:T(8,128)(2,1)S(1)} %copy-done, bf16[16,2,256,128]{3,2,1,0:T(8,128)(2,1)S(1)} %copy-done.1, ...), custom_call_target="tpu_custom_call" | custom-call | tf_op jit(solution)/shard_map/finish/pallas_call | solution.py:23
Async XLA Ops:
  0.6 11.8 %copy-start.4 = (f32[8192]{0:T(1024)S(1)}, f32[8192]{0:T(1024)}, u32[]{:S(2)}) copy-start(f32[8192]{0:T(1024)} %param.14) | copy-start | bytes 98308
  1.7 10.2 %collective-permute-start = (bf16[32,1024]{1,0:T(8,128)(2,1)S(1)}, bf16[32,1024]{1,0:T(8,128)(2,1)S(1)}, u32[]{:S(2)}, u32[]{:S(2)}) collective-permute-start(bf16[32,1024]{1,0:T(8,128)(2,1)S(1)} %get-tuple-element.25), channel_id=1, source_target_pairs={{0,12},{4,8},{8,4},{12,0},{1,13},{5,9},{9,5},{13,1},{2,14},{6,10},... | collective-permute-start | bytes 196616 | tf_op jit(solution)/shard_map/ppermute | solution.py:19
  6.8 5.6 %collective-permute-start.1 = (bf16[32,1024]{1,0:T(8,128)(2,1)S(1)}, bf16[32,1024]{1,0:T(8,128)(2,1)S(1)}, u32[]{:S(2)}, u32[]{:S(2)}) collective-permute-start(bf16[32,1024]{1,0:T(8,128)(2,1)S(1)} %get-tuple-element.26), channel_id=1, source_target_pairs={{0,8},{4,12},{8,0},{12,4},{1,9},{5,13},{9,1},{13,5},{2,10},{6,14},... | collective-permute-start | bytes 196616 | tf_op jit(solution)/shard_map/ppermute | solution.py:19
  6.8 5.6 %collective-permute-start.2 = (bf16[32,1024]{1,0:T(8,128)(2,1)S(1)}, bf16[32,1024]{1,0:T(8,128)(2,1)S(1)}, u32[]{:S(2)}, u32[]{:S(2)}) collective-permute-start(bf16[32,1024]{1,0:T(8,128)(2,1)S(1)} %get-tuple-element.27), channel_id=1, source_target_pairs={{0,4},{4,0},{8,12},{12,8},{1,5},{5,1},{9,13},{13,9},{2,6},{6,2},{1... | collective-permute-start | bytes 196616 | tf_op jit(solution)/shard_map/ppermute | solution.py:19
  11.9 6.5 %copy-start.2 = (bf16[2,64,2048]{2,1,0:T(8,128)(2,1)S(1)}, bf16[2,64,2048]{2,1,0:T(8,128)(2,1)}, u32[]{:S(2)}) copy-start(bf16[2,64,2048]{2,1,0:T(8,128)(2,1)} %param.19) | copy-start | bytes 1572868
  11.9 6.5 %copy-start.3 = (bf16[2,64,256]{2,1,0:T(8,128)(2,1)S(1)}, bf16[2,64,256]{2,1,0:T(8,128)(2,1)}, u32[]{:S(2)}) copy-start(bf16[2,64,256]{2,1,0:T(8,128)(2,1)} %param.21) | copy-start | bytes 196612
  11.9 16.1 %copy-start = (bf16[16,2,256,128]{3,2,1,0:T(8,128)(2,1)S(1)}, bf16[16,2,256,128]{3,2,1,0:T(8,128)(2,1)}, u32[]{:S(2)}) copy-start(bf16[16,2,256,128]{3,2,1,0:T(8,128)(2,1)} %k_ref.1) | copy-start | bytes 6291460
  11.9 16.1 %copy-start.1 = (bf16[16,2,256,128]{3,2,1,0:T(8,128)(2,1)S(1)}, bf16[16,2,256,128]{3,2,1,0:T(8,128)(2,1)}, u32[]{:S(2)}) copy-start(bf16[16,2,256,128]{3,2,1,0:T(8,128)(2,1)} %v_ref.1) | copy-start | bytes 6291460
  13.0 2.2 %collective-permute-start.3 = (bf16[64,1024]{1,0:T(8,128)(2,1)S(1)}, bf16[64,1024]{1,0:T(8,128)(2,1)S(1)}, u32[]{:S(2)}, u32[]{:S(2)}) collective-permute-start(bf16[64,1024]{1,0:T(8,128)(2,1)S(1)} %get-tuple-element.29.near_ref), channel_id=1, source_target_pairs={{0,1},{1,0},{2,3},{3,2},{4,5},{5,4},{6,7},{7,6},{8,9},{9,8},{10,11... | collective-permute-start | bytes 393224 | tf_op jit(solution)/shard_map/ppermute | solution.py:19
  13.0 4.1 %collective-permute-start.6 = (f32[32,128]{1,0:T(8,128)S(1)}, f32[32,128]{1,0:T(8,128)S(1)}, u32[]{:S(2)}, u32[]{:S(2)}) collective-permute-start(f32[32,128]{1,0:T(8,128)S(1)} %get-tuple-element.33.refs_0_), channel_id=1, source_target_pairs={{0,3},{1,2},{2,1},{3,0},{4,7},{5,6},{6,5},{7,4},{8,11},{9,10},{10,... | collective-permute-start | bytes 49160 | tf_op jit(solution)/shard_map/ppermute | solution.py:19
  14.6 3.7 %collective-permute-start.5 = (f32[32,128]{1,0:T(8,128)S(1)}, f32[32,128]{1,0:T(8,128)S(1)}, u32[]{:S(2)}, u32[]{:S(2)}) collective-permute-start(f32[32,128]{1,0:T(8,128)S(1)} %get-tuple-element.33.refs_0_), channel_id=1, source_target_pairs={{0,2},{1,3},{2,0},{3,1},{4,6},{5,7},{6,4},{7,5},{8,10},{9,11},{10,... | collective-permute-start | bytes 49160 | tf_op jit(solution)/shard_map/ppermute | solution.py:19
  15.2 3.2 %collective-permute-start.4 = (f32[32,128]{1,0:T(8,128)S(1)}, f32[32,128]{1,0:T(8,128)S(1)}, u32[]{:S(2)}, u32[]{:S(2)}) collective-permute-start(f32[32,128]{1,0:T(8,128)S(1)} %get-tuple-element.33.refs_0_), channel_id=1, source_target_pairs={{0,1},{1,0},{2,3},{3,2},{4,5},{5,4},{6,7},{7,6},{8,9},{9,8},{10,11... | collective-permute-start | bytes 49160 | tf_op jit(solution)/shard_map/ppermute | solution.py:19
  18.8 8.7 %collective-permute-start.7 = (bf16[16,2560]{1,0:T(8,128)(2,1)S(1)}, bf16[16,2560]{1,0:T(8,128)(2,1)S(1)}, u32[]{:S(2)}, u32[]{:S(2)}) collective-permute-start(bf16[16,2560]{1,0:T(8,128)(2,1)S(1)} %get-tuple-element.34), channel_id=1, source_target_pairs={{0,8},{4,12},{8,0},{12,4},{1,9},{5,13},{9,1},{13,5},{2,10},{6,14},... | collective-permute-start | bytes 245768 | tf_op jit(solution)/shard_map/ppermute | solution.py:19
  20.7 6.8 %collective-permute-start.8 = (bf16[16,2560]{1,0:T(8,128)(2,1)S(1)}, bf16[16,2560]{1,0:T(8,128)(2,1)S(1)}, u32[]{:S(2)}, u32[]{:S(2)}) collective-permute-start(bf16[16,2560]{1,0:T(8,128)(2,1)S(1)} %get-tuple-element.35), channel_id=1, source_target_pairs={{0,12},{4,8},{8,4},{12,0},{1,13},{5,9},{9,5},{13,1},{2,14},{6,10},... | collective-permute-start | bytes 245768 | tf_op jit(solution)/shard_map/ppermute | solution.py:19
  22.3 5.7 %collective-permute-start.9 = (bf16[16,2560]{1,0:T(8,128)(2,1)S(1)}, bf16[16,2560]{1,0:T(8,128)(2,1)S(1)}, u32[]{:S(2)}, u32[]{:S(2)}) collective-permute-start(bf16[16,2560]{1,0:T(8,128)(2,1)S(1)} %get-tuple-element.36), channel_id=1, source_target_pairs={{0,4},{4,0},{8,12},{12,8},{1,5},{5,1},{9,13},{13,9},{2,6},{6,2},{1... | collective-permute-start | bytes 245768 | tf_op jit(solution)/shard_map/ppermute | solution.py:19

commit v9 on v8

--- a/solution.py
+++ b/solution.py
@@ -267,7 +267,7 @@
             picked = every[:, first : first + rank]
             for near in range(1, nearby):
                 picked = picked + every[:, first + near * rank : first + (near + 1) * rank]
-            out_ref[:, at * rank : (at + 1) * rank] = picked
+            out_ref[:, at * rank : (at + 1) * rank] = picked.astype(BF16)
         me = lax.axis_index("adapter")
         first = me * base_width + lax.rem(lane, 2) * half
         scaled = gain_ref[:, pl.ds(pl.multiple_of(first, half), half)]
@@ -279,7 +279,7 @@
     low, near_half = call(
         lower, "lower",
         [
-            jax.ShapeDtypeStruct((slots, 2 * rank), F32),
+            jax.ShapeDtypeStruct((slots, 2 * rank), BF16),
             jax.ShapeDtypeStruct((rows, half), BF16),
         ],
         [VMEM] * (3 + len(arrived)), [VMEM] * 2,
@@ -314,9 +314,9 @@
 
     def raise_up(seen_ref, mask_ref, based_ref, uq_ref, uv_ref, *refs):
         low_refs, out_refs = refs[:lane_count], refs[lane_count:]
-        total = low_refs[0][...]
+        total = low_refs[0][...].astype(F32)
         for ref in low_refs[1:]:
-            total = total + ref[...]
+            total = total + ref[...].astype(F32)
         spread = [total[:, :rank]] * nearby + [total[:, rank:]] * nearby
         spread = jnp.concatenate(spread, axis=1) * mask_ref[...]
         lowered = lax.dot_general(
@@ -367,8 +367,7 @@
         value_new = summed[:, query_cols + kv_cols :]
         fresh_ref[...] = jnp.stack([key_new, value_new], axis=1)
         sum_ref[...] = summed.astype(F32)
-        for head in range(heads):
-            q_ref[:, head, :] = sum_ref[:, head * head_dim : (head + 1) * head_dim]
+        q_ref[...] = sum_ref[:, :query_cols].reshape(block_rows, heads, head_dim)
         scale = head_dim ** (-0.5)
         twin = 2 * group_size
         spot = iota((twin, context), 1).astype(F32)
@@ -439,8 +438,7 @@
         for index in pairs:
             mixed = mixed_of(index, s_ref[index // 2])
             put(index, mixed + own_weight[index // 2] * stacked(index, query_cols + kv_cols))
-        for head in range(heads):
-            out_ref[:, head * head_dim : (head + 1) * head_dim] = o_ref[:, head, :].astype(BF16)
+        out_ref[...] = o_ref[...].reshape(block_rows, query_cols).astype(BF16)
 
     attended, fresh = call(
         finish, "finish",

time: 30.1 us -> 29.9 us (level)
  no operation moved by 1% of the time
where the time goes in v9:
time: 29.9 us; the launch traced here: 29.7 us
  starting transfers between devices  11.8 us (39%)
  Pallas kernels  10.2 us (34%)
  waiting for transfers between devices  6.93 us (23%)
  between operations  0.74 us (2%)
    ppermute x10, starting transfers between devices, partner(): return lax.ppermute(array, axis, [(i, i ^ step) for i in range(count)])  11.8 us
    pallas_call x6, Pallas kernels, call(): pl.pallas_call(body, name=name, out_shape=outs, in_specs=in_specs, out_sp...  10.2 us
    ppermute x10, waiting for transfers between devices, partner(): return lax.ppermute(array, axis, [(i, i ^ step) for i in range(count)])  6.93 us
  transfers between devices with their start and end apart: 10, of which 4 were waited for; matrix products, arithmetic and copies ran while one was open for 0% of the time, Pallas kernels for 21%

profile of v9, /device:TPU:0, one launch (start us, length us, event | category | flops | bytes accessed | tf_op | source)
XLA Modules:
  0.0 29.7 jit_solution(9252886657066989003)
XLA Ops:
  0.6 0.0 copy-start.4
  0.6 1.1 %prepare.1 = (bf16[32,1024]{1,0:T(8,128)(2,1)S(1)}, bf16[32,1024]{1,0:T(8,128)(2,1)S(1)}, bf16[32,1024]{1,0:T(8,128)(2,1)S(1)}, bf16[32,1024]{1,0:T(8,128)(2,1)S(1)}) custom-call(s32[1,64]{1,0:T(1,128)} %bitcast.16, bf16[16,8192]{1,0:T(8,128)(2,1)} %x_ref.3), custom_call_target="tpu_custom_call" | custom-call | bytes 524288 | tf_op jit(solution)/shard_map/prepare/pallas_call | solution.py:23
  1.7 5.1 %collective-permute-start = (bf16[32,1024]{1,0:T(8,128)(2,1)S(1)}, bf16[32,1024]{1,0:T(8,128)(2,1)S(1)}, u32[]{:S(2)}, u32[]{:S(2)}) collective-permute-start(bf16[32,1024]{1,0:T(8,128)(2,1)S(1)} %get-tuple-element.25), channel_id=1, source_target_pairs={{0,12},{4,8},{8,4},{12,0},{1,13},{5,9},{9,5},{13,1},{2,14},{6,10},... | collective-permute-start | bytes 196616 | tf_op jit(solution)/shard_map/ppermute | solution.py:19
  6.8 0.0 collective-permute-start.1
  6.8 0.6 %collective-permute-start.2 = (bf16[32,1024]{1,0:T(8,128)(2,1)S(1)}, bf16[32,1024]{1,0:T(8,128)(2,1)S(1)}, u32[]{:S(2)}, u32[]{:S(2)}) collective-permute-start(bf16[32,1024]{1,0:T(8,128)(2,1)S(1)} %get-tuple-element.27), channel_id=1, source_target_pairs={{0,4},{4,0},{8,12},{12,8},{1,5},{5,1},{9,13},{13,9},{2,6},{6,2},{1... | collective-permute-start | bytes 196616 | tf_op jit(solution)/shard_map/ppermute | solution.py:19
  7.5 4.4 %survey.1 = (bf16[256,2048]{1,0:T(8,128)(2,1)S(1)}, bf16[2048,2048]{1,0:T(8,128)(2,1)S(1)}, bf16[2048,256]{1,0:T(8,128)(2,1)S(1)}, bf16[2048,256]{1,0:T(8,128)(2...) custom-call(s32[1,64]{1,0:T(1,128)} %bitcast.17, ...), custom_call_target="tpu_custom_call" | custom-call | bytes 12582912 | tf_op jit(solution)/shard_map/survey/pallas_call | solution.py:23
  11.9 0.0 copy-start.2
  11.9 0.0 copy-start.3
  11.9 0.0 copy-start
  11.9 0.0 copy-start.1
  12.0 0.0 collective-permute-done.refs_0_
  12.0 0.5 %collective-permute-done.1.refs_1_ = bf16[32,1024]{1,0:T(8,128)(2,1)S(1)} collective-permute-done((bf16[32,1024]{1,0:T(8,128)(2,1)S(1)}, bf16[32,1024]{1,0:T(8,128)(2,1)S(1)}, u32[]{:S(2)}, u32[]{:S(2)}) %collective-permute-start.1) | collective-permute-done | bytes 65568 | tf_op jit(solution)/shard_map/ppermute | solution.py:19
  12.4 0.0 collective-permute-done.2.refs_2_
  12.4 0.0 copy-done.4
  12.4 0.6 %lower.1 = (bf16[32,128]{1,0:T(8,128)(2,1)S(1)}, bf16[64,1024]{1,0:T(8,128)(2,1)S(1)}) custom-call(f32[1,8192]{1,0:T(1,128)S(1)} %bitcast.13, f32[32,256]{1,0:T(8,128)S(1)} %get-tuple-element.23.mask_ref, bf16[256,2048]{1,0:T(8,128)(2,1)S(1)} %get-tuple-element.24.down_ref, bf16[32,1024]{1,0:T(8,128)(2,1)S(1)} %collective-permute-done.refs_0_, ...), custom_call_target="tpu_custom_call" | custom-call | bytes 1048576 | tf_op jit(solution)/shard_map/lower/pallas_call | solution.py:23
  13.0 0.0 collective-permute-start.3
  13.0 1.6 %collective-permute-start.6 = (bf16[32,128]{1,0:T(8,128)(2,1)S(1)}, bf16[32,128]{1,0:T(8,128)(2,1)S(1)}, u32[]{:S(2)}, u32[]{:S(2)}) collective-permute-start(bf16[32,128]{1,0:T(8,128)(2,1)S(1)} %get-tuple-element.33.refs_0_), channel_id=1, source_target_pairs={{0,3},{1,2},{2,1},{3,0},{4,7},{5,6},{6,5},{7,4},{8,11},{9,10},{10,... | collective-permute-start | bytes 24584 | tf_op jit(solution)/shard_map/ppermute | solution.py:19
  14.6 0.5 %collective-permute-start.5 = (bf16[32,128]{1,0:T(8,128)(2,1)S(1)}, bf16[32,128]{1,0:T(8,128)(2,1)S(1)}, u32[]{:S(2)}, u32[]{:S(2)}) collective-permute-start(bf16[32,128]{1,0:T(8,128)(2,1)S(1)} %get-tuple-element.33.refs_0_), channel_id=1, source_target_pairs={{0,2},{1,3},{2,0},{3,1},{4,6},{5,7},{6,4},{7,5},{8,10},{9,11},{10,... | collective-permute-start | bytes 24584 | tf_op jit(solution)/shard_map/ppermute | solution.py:19
  15.2 0.0 collective-permute-start.4
  15.2 0.0 collective-permute-done.3.far_ref
  15.2 1.9 %project.1.based_ref = f32[64,2560]{1,0:T(8,128)S(1)} custom-call(bf16[64,1024]{1,0:T(8,128)(2,1)S(1)} %get-tuple-element.29.near_ref, bf16[64,1024]{1,0:T(8,128)(2,1)S(1)} %collective-permute-done.3.far_ref, bf16[2048,2048]{1,0:T(8,128)(2,1)S(1)} %get-tuple-element.30.wq_ref, bf16[2048,256]{1,0:T(8,128)(2,1)S(1)} %get-tuple-element.31.wk_ref, ...), custom_call_target="tpu_custom_call" | custom-call | flops 671088640 | bytes 10485760 | tf_op jit(solution)/shard_map/project/pallas_call | solution.py:23
  17.1 0.0 collective-permute-done.6.refs_3_
  17.2 1.1 %collective-permute-done.5.refs_2_ = bf16[32,128]{1,0:T(8,128)(2,1)S(1)} collective-permute-done((bf16[32,128]{1,0:T(8,128)(2,1)S(1)}, bf16[32,128]{1,0:T(8,128)(2,1)S(1)}, u32[]{:S(2)}, u32[]{:S(2)}) %collective-permute-start.5) | collective-permute-done | bytes 8224 | tf_op jit(solution)/shard_map/ppermute | solution.py:19
  18.3 0.0 collective-permute-done.4.refs_1_
  18.3 0.0 copy-done.2
  18.3 0.0 copy-done.3
  18.3 0.4 %raise_up.1 = (f32[16,2560]{1,0:T(8,128)S(1)}, bf16[16,2560]{1,0:T(8,128)(2,1)S(1)}, bf16[16,2560]{1,0:T(8,128)(2,1)S(1)}, bf16[16,2560]{1,0:T(8,128)(2,1)S(1)}) custom-call(bf16[32,64]{1,0:T(8,128)(2,1)S(1)} %get-tuple-element.22.seen_ref, f32[32,256]{1,0:T(8,128)S(1)} %get-tuple-element.23.mask_ref, f32[64,2560]{1,0:T(8,128)S(1)} %project.1.based_ref, ...), custom_call_target="tpu_custom_call" | custom-call | tf_op jit(solution)/shard_map/raise_up/pallas_call | solution.py:23
  18.7 1.9 %collective-permute-start.7 = (bf16[16,2560]{1,0:T(8,128)(2,1)S(1)}, bf16[16,2560]{1,0:T(8,128)(2,1)S(1)}, u32[]{:S(2)}, u32[]{:S(2)}) collective-permute-start(bf16[16,2560]{1,0:T(8,128)(2,1)S(1)} %get-tuple-element.34), channel_id=1, source_target_pairs={{0,8},{4,12},{8,0},{12,4},{1,9},{5,13},{9,1},{13,5},{2,10},{6,14},... | collective-permute-start | bytes 245768 | tf_op jit(solution)/shard_map/ppermute | solution.py:19
  20.6 1.6 %collective-permute-start.8 = (bf16[16,2560]{1,0:T(8,128)(2,1)S(1)}, bf16[16,2560]{1,0:T(8,128)(2,1)S(1)}, u32[]{:S(2)}, u32[]{:S(2)}) collective-permute-start(bf16[16,2560]{1,0:T(8,128)(2,1)S(1)} %get-tuple-element.35), channel_id=1, source_target_pairs={{0,12},{4,8},{8,4},{12,0},{1,13},{5,9},{9,5},{13,1},{2,14},{6,10},... | collective-permute-start | bytes 245768 | tf_op jit(solution)/shard_map/ppermute | solution.py:19
  22.2 0.4 %collective-permute-start.9 = (bf16[16,2560]{1,0:T(8,128)(2,1)S(1)}, bf16[16,2560]{1,0:T(8,128)(2,1)S(1)}, u32[]{:S(2)}, u32[]{:S(2)}) collective-permute-start(bf16[16,2560]{1,0:T(8,128)(2,1)S(1)} %get-tuple-element.36), channel_id=1, source_target_pairs={{0,4},{4,0},{8,12},{12,8},{1,5},{5,1},{9,13},{13,9},{2,6},{6,2},{1... | collective-permute-start | bytes 245768 | tf_op jit(solution)/shard_map/ppermute | solution.py:19
  22.7 4.8 %collective-permute-done.7.refs_0_ = bf16[16,2560]{1,0:T(8,128)(2,1)S(1)} collective-permute-done((bf16[16,2560]{1,0:T(8,128)(2,1)S(1)}, bf16[16,2560]{1,0:T(8,128)(2,1)S(1)}, u32[]{:S(2)}, u32[]{:S(2)}) %collective-permute-start.7) | collective-permute-done | bytes 81952 | tf_op jit(solution)/shard_map/ppermute | solution.py:19
  27.5 0.0 collective-permute-done.8.refs_1_
  27.5 0.5 %collective-permute-done.9.refs_2_ = bf16[16,2560]{1,0:T(8,128)(2,1)S(1)} collective-permute-done((bf16[16,2560]{1,0:T(8,128)(2,1)S(1)}, bf16[16,2560]{1,0:T(8,128)(2,1)S(1)}, u32[]{:S(2)}, u32[]{:S(2)}) %collective-permute-start.9) | collective-permute-done | bytes 81952 | tf_op jit(solution)/shard_map/ppermute | solution.py:19
  28.0 0.0 copy-done
  28.0 0.0 copy-done.1
  28.0 1.8 %finish.1 = (bf16[16,2048]{1,0:T(8,128)(2,1)}, bf16[16,2,256]{2,1,0:T(2,128)(2,1)}) custom-call(f32[16,256]{1,0:T(8,128)S(1)} %get-tuple-element.20.length_ref, f32[16,128]{1,0:T(8,128)S(1)} %get-tuple-element.21.scale_ref, bf16[16,2,256,128]{3,2,1,0:T(8,128)(2,1)S(1)} %copy-done, bf16[16,2,256,128]{3,2,1,0:T(8,128)(2,1)S(1)} %copy-done.1, ...), custom_call_target="tpu_custom_call" | custom-call | tf_op jit(solution)/shard_map/finish/pallas_call | solution.py:23
Async XLA Ops:
  0.6 11.8 %copy-start.4 = (f32[8192]{0:T(1024)S(1)}, f32[8192]{0:T(1024)}, u32[]{:S(2)}) copy-start(f32[8192]{0:T(1024)} %param.14) | copy-start | bytes 98308
  1.7 10.2 %collective-permute-start = (bf16[32,1024]{1,0:T(8,128)(2,1)S(1)}, bf16[32,1024]{1,0:T(8,128)(2,1)S(1)}, u32[]{:S(2)}, u32[]{:S(2)}) collective-permute-start(bf16[32,1024]{1,0:T(8,128)(2,1)S(1)} %get-tuple-element.25), channel_id=1, source_target_pairs={{0,12},{4,8},{8,4},{12,0},{1,13},{5,9},{9,5},{13,1},{2,14},{6,10},... | collective-permute-start | bytes 196616 | tf_op jit(solution)/shard_map/ppermute | solution.py:19
  6.8 5.6 %collective-permute-start.1 = (bf16[32,1024]{1,0:T(8,128)(2,1)S(1)}, bf16[32,1024]{1,0:T(8,128)(2,1)S(1)}, u32[]{:S(2)}, u32[]{:S(2)}) collective-permute-start(bf16[32,1024]{1,0:T(8,128)(2,1)S(1)} %get-tuple-element.26), channel_id=1, source_target_pairs={{0,8},{4,12},{8,0},{12,4},{1,9},{5,13},{9,1},{13,5},{2,10},{6,14},... | collective-permute-start | bytes 196616 | tf_op jit(solution)/shard_map/ppermute | solution.py:19
  6.8 5.6 %collective-permute-start.2 = (bf16[32,1024]{1,0:T(8,128)(2,1)S(1)}, bf16[32,1024]{1,0:T(8,128)(2,1)S(1)}, u32[]{:S(2)}, u32[]{:S(2)}) collective-permute-start(bf16[32,1024]{1,0:T(8,128)(2,1)S(1)} %get-tuple-element.27), channel_id=1, source_target_pairs={{0,4},{4,0},{8,12},{12,8},{1,5},{5,1},{9,13},{13,9},{2,6},{6,2},{1... | collective-permute-start | bytes 196616 | tf_op jit(solution)/shard_map/ppermute | solution.py:19
  11.9 6.4 %copy-start.2 = (bf16[2,64,2048]{2,1,0:T(8,128)(2,1)S(1)}, bf16[2,64,2048]{2,1,0:T(8,128)(2,1)}, u32[]{:S(2)}) copy-start(bf16[2,64,2048]{2,1,0:T(8,128)(2,1)} %param.19) | copy-start | bytes 1572868
  11.9 6.4 %copy-start.3 = (bf16[2,64,256]{2,1,0:T(8,128)(2,1)S(1)}, bf16[2,64,256]{2,1,0:T(8,128)(2,1)}, u32[]{:S(2)}) copy-start(bf16[2,64,256]{2,1,0:T(8,128)(2,1)} %param.21) | copy-start | bytes 196612
  11.9 16.0 %copy-start = (bf16[16,2,256,128]{3,2,1,0:T(8,128)(2,1)S(1)}, bf16[16,2,256,128]{3,2,1,0:T(8,128)(2,1)}, u32[]{:S(2)}) copy-start(bf16[16,2,256,128]{3,2,1,0:T(8,128)(2,1)} %k_ref.1) | copy-start | bytes 6291460
  11.9 16.0 %copy-start.1 = (bf16[16,2,256,128]{3,2,1,0:T(8,128)(2,1)S(1)}, bf16[16,2,256,128]{3,2,1,0:T(8,128)(2,1)}, u32[]{:S(2)}) copy-start(bf16[16,2,256,128]{3,2,1,0:T(8,128)(2,1)} %v_ref.1) | copy-start | bytes 6291460
  13.0 2.2 %collective-permute-start.3 = (bf16[64,1024]{1,0:T(8,128)(2,1)S(1)}, bf16[64,1024]{1,0:T(8,128)(2,1)S(1)}, u32[]{:S(2)}, u32[]{:S(2)}) collective-permute-start(bf16[64,1024]{1,0:T(8,128)(2,1)S(1)} %get-tuple-element.29.near_ref), channel_id=1, source_target_pairs={{0,1},{1,0},{2,3},{3,2},{4,5},{5,4},{6,7},{7,6},{8,9},{9,8},{10,11... | collective-permute-start | bytes 393224 | tf_op jit(solution)/shard_map/ppermute | solution.py:19
  13.0 4.1 %collective-permute-start.6 = (bf16[32,128]{1,0:T(8,128)(2,1)S(1)}, bf16[32,128]{1,0:T(8,128)(2,1)S(1)}, u32[]{:S(2)}, u32[]{:S(2)}) collective-permute-start(bf16[32,128]{1,0:T(8,128)(2,1)S(1)} %get-tuple-element.33.refs_0_), channel_id=1, source_target_pairs={{0,3},{1,2},{2,1},{3,0},{4,7},{5,6},{6,5},{7,4},{8,11},{9,10},{10,... | collective-permute-start | bytes 24584 | tf_op jit(solution)/shard_map/ppermute | solution.py:19
  14.6 3.7 %collective-permute-start.5 = (bf16[32,128]{1,0:T(8,128)(2,1)S(1)}, bf16[32,128]{1,0:T(8,128)(2,1)S(1)}, u32[]{:S(2)}, u32[]{:S(2)}) collective-permute-start(bf16[32,128]{1,0:T(8,128)(2,1)S(1)} %get-tuple-element.33.refs_0_), channel_id=1, source_target_pairs={{0,2},{1,3},{2,0},{3,1},{4,6},{5,7},{6,4},{7,5},{8,10},{9,11},{10,... | collective-permute-start | bytes 24584 | tf_op jit(solution)/shard_map/ppermute | solution.py:19
  15.2 3.1 %collective-permute-start.4 = (bf16[32,128]{1,0:T(8,128)(2,1)S(1)}, bf16[32,128]{1,0:T(8,128)(2,1)S(1)}, u32[]{:S(2)}, u32[]{:S(2)}) collective-permute-start(bf16[32,128]{1,0:T(8,128)(2,1)S(1)} %get-tuple-element.33.refs_0_), channel_id=1, source_target_pairs={{0,1},{1,0},{2,3},{3,2},{4,5},{5,4},{6,7},{7,6},{8,9},{9,8},{10,11... | collective-permute-start | bytes 24584 | tf_op jit(solution)/shard_map/ppermute | solution.py:19
  18.7 8.8 %collective-permute-start.7 = (bf16[16,2560]{1,0:T(8,128)(2,1)S(1)}, bf16[16,2560]{1,0:T(8,128)(2,1)S(1)}, u32[]{:S(2)}, u32[]{:S(2)}) collective-permute-start(bf16[16,2560]{1,0:T(8,128)(2,1)S(1)} %get-tuple-element.34), channel_id=1, source_target_pairs={{0,8},{4,12},{8,0},{12,4},{1,9},{5,13},{9,1},{13,5},{2,10},{6,14},... | collective-permute-start | bytes 245768 | tf_op jit(solution)/shard_map/ppermute | solution.py:19
  20.6 6.9 %collective-permute-start.8 = (bf16[16,2560]{1,0:T(8,128)(2,1)S(1)}, bf16[16,2560]{1,0:T(8,128)(2,1)S(1)}, u32[]{:S(2)}, u32[]{:S(2)}) collective-permute-start(bf16[16,2560]{1,0:T(8,128)(2,1)S(1)} %get-tuple-element.35), channel_id=1, source_target_pairs={{0,12},{4,8},{8,4},{12,0},{1,13},{5,9},{9,5},{13,1},{2,14},{6,10},... | collective-permute-start | bytes 245768 | tf_op jit(solution)/shard_map/ppermute | solution.py:19
  22.2 5.7 %collective-permute-start.9 = (bf16[16,2560]{1,0:T(8,128)(2,1)S(1)}, bf16[16,2560]{1,0:T(8,128)(2,1)S(1)}, u32[]{:S(2)}, u32[]{:S(2)}) collective-permute-start(bf16[16,2560]{1,0:T(8,128)(2,1)S(1)} %get-tuple-element.36), channel_id=1, source_target_pairs={{0,4},{4,0},{8,12},{12,8},{1,5},{5,1},{9,13},{13,9},{2,6},{6,2},{1... | collective-permute-start | bytes 245768 | tf_op jit(solution)/shard_map/ppermute | solution.py:19

commit v10 on v9

--- a/solution.py
+++ b/solution.py
@@ -433,11 +433,12 @@
         lifted = jnp.exp(scores - peak)
         own_lift = jnp.exp(own_score - peak)
         inverse = 1.0 / (jnp.sum(lifted, axis=2, keepdims=True) + own_lift)
-        s_ref[...] = lifted * inverse
-        own_weight = (own_lift * inverse).astype(BF16).astype(F32)
+        s_ref[...] = lifted
+        own_weight = own_lift.astype(BF16).astype(F32)
         for index in pairs:
             mixed = mixed_of(index, s_ref[index // 2])
-            put(index, mixed + own_weight[index // 2] * stacked(index, query_cols + kv_cols))
+            mixed = mixed + own_weight[index // 2] * stacked(index, query_cols + kv_cols)
+            put(index, mixed * inverse[index // 2])
         out_ref[...] = o_ref[...].reshape(block_rows, query_cols).astype(BF16)
 
     attended, fresh = call(

time: 29.9 us -> 29.8 us (level)
  no operation moved by 1% of the time
where the time goes in v10:
time: 29.8 us; the launch traced here: 29.6 us
  starting transfers between devices  11.8 us (40%)
  Pallas kernels  10.1 us (34%)
  waiting for transfers between devices  6.93 us (23%)
  between operations  0.74 us (2%)
    ppermute x10, starting transfers between devices, partner(): return lax.ppermute(array, axis, [(i, i ^ step) for i in range(count)])  11.8 us
    pallas_call x6, Pallas kernels, call(): pl.pallas_call(body, name=name, out_shape=outs, in_specs=in_specs, out_sp...  10.1 us
    ppermute x10, waiting for transfers between devices, partner(): return lax.ppermute(array, axis, [(i, i ^ step) for i in range(count)])  6.93 us
  transfers between devices with their start and end apart: 10, of which 4 were waited for; matrix products, arithmetic and copies ran while one was open for 0% of the time, Pallas kernels for 21%

profile of v10, /device:TPU:0, one launch (start us, length us, event | category | flops | bytes accessed | tf_op | source)
XLA Modules:
  0.0 29.6 jit_solution(11312564168460469731)
XLA Ops:
  0.6 0.0 copy-start.4
  0.6 1.1 %prepare.1 = (bf16[32,1024]{1,0:T(8,128)(2,1)S(1)}, bf16[32,1024]{1,0:T(8,128)(2,1)S(1)}, bf16[32,1024]{1,0:T(8,128)(2,1)S(1)}, bf16[32,1024]{1,0:T(8,128)(2,1)S(1)}) custom-call(s32[1,64]{1,0:T(1,128)} %bitcast.16, bf16[16,8192]{1,0:T(8,128)(2,1)} %x_ref.3), custom_call_target="tpu_custom_call" | custom-call | bytes 524288 | tf_op jit(solution)/shard_map/prepare/pallas_call | solution.py:23
  1.7 5.1 %collective-permute-start = (bf16[32,1024]{1,0:T(8,128)(2,1)S(1)}, bf16[32,1024]{1,0:T(8,128)(2,1)S(1)}, u32[]{:S(2)}, u32[]{:S(2)}) collective-permute-start(bf16[32,1024]{1,0:T(8,128)(2,1)S(1)} %get-tuple-element.25), channel_id=1, source_target_pairs={{0,12},{4,8},{8,4},{12,0},{1,13},{5,9},{9,5},{13,1},{2,14},{6,10},... | collective-permute-start | bytes 196616 | tf_op jit(solution)/shard_map/ppermute | solution.py:19
  6.8 0.0 collective-permute-start.1
  6.8 0.6 %collective-permute-start.2 = (bf16[32,1024]{1,0:T(8,128)(2,1)S(1)}, bf16[32,1024]{1,0:T(8,128)(2,1)S(1)}, u32[]{:S(2)}, u32[]{:S(2)}) collective-permute-start(bf16[32,1024]{1,0:T(8,128)(2,1)S(1)} %get-tuple-element.27), channel_id=1, source_target_pairs={{0,4},{4,0},{8,12},{12,8},{1,5},{5,1},{9,13},{13,9},{2,6},{6,2},{1... | collective-permute-start | bytes 196616 | tf_op jit(solution)/shard_map/ppermute | solution.py:19
  7.5 4.4 %survey.1 = (bf16[256,2048]{1,0:T(8,128)(2,1)S(1)}, bf16[2048,2048]{1,0:T(8,128)(2,1)S(1)}, bf16[2048,256]{1,0:T(8,128)(2,1)S(1)}, bf16[2048,256]{1,0:T(8,128)(2...) custom-call(s32[1,64]{1,0:T(1,128)} %bitcast.17, ...), custom_call_target="tpu_custom_call" | custom-call | bytes 12582912 | tf_op jit(solution)/shard_map/survey/pallas_call | solution.py:23
  11.9 0.0 copy-start.2
  11.9 0.0 copy-start.3
  11.9 0.0 copy-start
  11.9 0.0 copy-start.1
  12.0 0.0 collective-permute-done.refs_0_
  12.0 0.5 %collective-permute-done.1.refs_1_ = bf16[32,1024]{1,0:T(8,128)(2,1)S(1)} collective-permute-done((bf16[32,1024]{1,0:T(8,128)(2,1)S(1)}, bf16[32,1024]{1,0:T(8,128)(2,1)S(1)}, u32[]{:S(2)}, u32[]{:S(2)}) %collective-permute-start.1) | collective-permute-done | bytes 65568 | tf_op jit(solution)/shard_map/ppermute | solution.py:19
  12.4 0.0 collective-permute-done.2.refs_2_
  12.4 0.0 copy-done.4
  12.4 0.6 %lower.1 = (bf16[32,128]{1,0:T(8,128)(2,1)S(1)}, bf16[64,1024]{1,0:T(8,128)(2,1)S(1)}) custom-call(f32[1,8192]{1,0:T(1,128)S(1)} %bitcast.13, f32[32,256]{1,0:T(8,128)S(1)} %get-tuple-element.23.mask_ref, bf16[256,2048]{1,0:T(8,128)(2,1)S(1)} %get-tuple-element.24.down_ref, bf16[32,1024]{1,0:T(8,128)(2,1)S(1)} %collective-permute-done.refs_0_, ...), custom_call_target="tpu_custom_call" | custom-call | bytes 1048576 | tf_op jit(solution)/shard_map/lower/pallas_call | solution.py:23
  13.0 0.0 collective-permute-start.3
  13.0 1.6 %collective-permute-start.6 = (bf16[32,128]{1,0:T(8,128)(2,1)S(1)}, bf16[32,128]{1,0:T(8,128)(2,1)S(1)}, u32[]{:S(2)}, u32[]{:S(2)}) collective-permute-start(bf16[32,128]{1,0:T(8,128)(2,1)S(1)} %get-tuple-element.33.refs_0_), channel_id=1, source_target_pairs={{0,3},{1,2},{2,1},{3,0},{4,7},{5,6},{6,5},{7,4},{8,11},{9,10},{10,... | collective-permute-start | bytes 24584 | tf_op jit(solution)/shard_map/ppermute | solution.py:19
  14.6 0.5 %collective-permute-start.5 = (bf16[32,128]{1,0:T(8,128)(2,1)S(1)}, bf16[32,128]{1,0:T(8,128)(2,1)S(1)}, u32[]{:S(2)}, u32[]{:S(2)}) collective-permute-start(bf16[32,128]{1,0:T(8,128)(2,1)S(1)} %get-tuple-element.33.refs_0_), channel_id=1, source_target_pairs={{0,2},{1,3},{2,0},{3,1},{4,6},{5,7},{6,4},{7,5},{8,10},{9,11},{10,... | collective-permute-start | bytes 24584 | tf_op jit(solution)/shard_map/ppermute | solution.py:19
  15.2 0.0 collective-permute-start.4
  15.2 0.0 collective-permute-done.3.far_ref
  15.2 1.9 %project.1.based_ref = f32[64,2560]{1,0:T(8,128)S(1)} custom-call(bf16[64,1024]{1,0:T(8,128)(2,1)S(1)} %get-tuple-element.29.near_ref, bf16[64,1024]{1,0:T(8,128)(2,1)S(1)} %collective-permute-done.3.far_ref, bf16[2048,2048]{1,0:T(8,128)(2,1)S(1)} %get-tuple-element.30.wq_ref, bf16[2048,256]{1,0:T(8,128)(2,1)S(1)} %get-tuple-element.31.wk_ref, ...), custom_call_target="tpu_custom_call" | custom-call | flops 671088640 | bytes 10485760 | tf_op jit(solution)/shard_map/project/pallas_call | solution.py:23
  17.1 0.0 collective-permute-done.6.refs_3_
  17.2 1.1 %collective-permute-done.5.refs_2_ = bf16[32,128]{1,0:T(8,128)(2,1)S(1)} collective-permute-done((bf16[32,128]{1,0:T(8,128)(2,1)S(1)}, bf16[32,128]{1,0:T(8,128)(2,1)S(1)}, u32[]{:S(2)}, u32[]{:S(2)}) %collective-permute-start.5) | collective-permute-done | bytes 8224 | tf_op jit(solution)/shard_map/ppermute | solution.py:19
  18.3 0.0 collective-permute-done.4.refs_1_
  18.3 0.0 copy-done.2
  18.3 0.0 copy-done.3
  18.3 0.4 %raise_up.1 = (f32[16,2560]{1,0:T(8,128)S(1)}, bf16[16,2560]{1,0:T(8,128)(2,1)S(1)}, bf16[16,2560]{1,0:T(8,128)(2,1)S(1)}, bf16[16,2560]{1,0:T(8,128)(2,1)S(1)}) custom-call(bf16[32,64]{1,0:T(8,128)(2,1)S(1)} %get-tuple-element.22.seen_ref, f32[32,256]{1,0:T(8,128)S(1)} %get-tuple-element.23.mask_ref, f32[64,2560]{1,0:T(8,128)S(1)} %project.1.based_ref, ...), custom_call_target="tpu_custom_call" | custom-call | tf_op jit(solution)/shard_map/raise_up/pallas_call | solution.py:23
  18.7 1.9 %collective-permute-start.7 = (bf16[16,2560]{1,0:T(8,128)(2,1)S(1)}, bf16[16,2560]{1,0:T(8,128)(2,1)S(1)}, u32[]{:S(2)}, u32[]{:S(2)}) collective-permute-start(bf16[16,2560]{1,0:T(8,128)(2,1)S(1)} %get-tuple-element.34), channel_id=1, source_target_pairs={{0,8},{4,12},{8,0},{12,4},{1,9},{5,13},{9,1},{13,5},{2,10},{6,14},... | collective-permute-start | bytes 245768 | tf_op jit(solution)/shard_map/ppermute | solution.py:19
  20.6 1.6 %collective-permute-start.8 = (bf16[16,2560]{1,0:T(8,128)(2,1)S(1)}, bf16[16,2560]{1,0:T(8,128)(2,1)S(1)}, u32[]{:S(2)}, u32[]{:S(2)}) collective-permute-start(bf16[16,2560]{1,0:T(8,128)(2,1)S(1)} %get-tuple-element.35), channel_id=1, source_target_pairs={{0,12},{4,8},{8,4},{12,0},{1,13},{5,9},{9,5},{13,1},{2,14},{6,10},... | collective-permute-start | bytes 245768 | tf_op jit(solution)/shard_map/ppermute | solution.py:19
  22.2 0.4 %collective-permute-start.9 = (bf16[16,2560]{1,0:T(8,128)(2,1)S(1)}, bf16[16,2560]{1,0:T(8,128)(2,1)S(1)}, u32[]{:S(2)}, u32[]{:S(2)}) collective-permute-start(bf16[16,2560]{1,0:T(8,128)(2,1)S(1)} %get-tuple-element.36), channel_id=1, source_target_pairs={{0,4},{4,0},{8,12},{12,8},{1,5},{5,1},{9,13},{13,9},{2,6},{6,2},{1... | collective-permute-start | bytes 245768 | tf_op jit(solution)/shard_map/ppermute | solution.py:19
  22.7 4.8 %collective-permute-done.7.refs_0_ = bf16[16,2560]{1,0:T(8,128)(2,1)S(1)} collective-permute-done((bf16[16,2560]{1,0:T(8,128)(2,1)S(1)}, bf16[16,2560]{1,0:T(8,128)(2,1)S(1)}, u32[]{:S(2)}, u32[]{:S(2)}) %collective-permute-start.7) | collective-permute-done | bytes 81952 | tf_op jit(solution)/shard_map/ppermute | solution.py:19
  27.5 0.0 collective-permute-done.8.refs_1_
  27.5 0.5 %collective-permute-done.9.refs_2_ = bf16[16,2560]{1,0:T(8,128)(2,1)S(1)} collective-permute-done((bf16[16,2560]{1,0:T(8,128)(2,1)S(1)}, bf16[16,2560]{1,0:T(8,128)(2,1)S(1)}, u32[]{:S(2)}, u32[]{:S(2)}) %collective-permute-start.9) | collective-permute-done | bytes 81952 | tf_op jit(solution)/shard_map/ppermute | solution.py:19
  28.0 0.0 copy-done
  28.0 0.0 copy-done.1
  28.0 1.7 %finish.1 = (bf16[16,2048]{1,0:T(8,128)(2,1)}, bf16[16,2,256]{2,1,0:T(2,128)(2,1)}) custom-call(f32[16,256]{1,0:T(8,128)S(1)} %get-tuple-element.20.length_ref, f32[16,128]{1,0:T(8,128)S(1)} %get-tuple-element.21.scale_ref, bf16[16,2,256,128]{3,2,1,0:T(8,128)(2,1)S(1)} %copy-done, bf16[16,2,256,128]{3,2,1,0:T(8,128)(2,1)S(1)} %copy-done.1, ...), custom_call_target="tpu_custom_call" | custom-call | tf_op jit(solution)/shard_map/finish/pallas_call | solution.py:23
Async XLA Ops:
  0.6 11.8 %copy-start.4 = (f32[8192]{0:T(1024)S(1)}, f32[8192]{0:T(1024)}, u32[]{:S(2)}) copy-start(f32[8192]{0:T(1024)} %param.14) | copy-start | bytes 98308
  1.7 10.2 %collective-permute-start = (bf16[32,1024]{1,0:T(8,128)(2,1)S(1)}, bf16[32,1024]{1,0:T(8,128)(2,1)S(1)}, u32[]{:S(2)}, u32[]{:S(2)}) collective-permute-start(bf16[32,1024]{1,0:T(8,128)(2,1)S(1)} %get-tuple-element.25), channel_id=1, source_target_pairs={{0,12},{4,8},{8,4},{12,0},{1,13},{5,9},{9,5},{13,1},{2,14},{6,10},... | collective-permute-start | bytes 196616 | tf_op jit(solution)/shard_map/ppermute | solution.py:19
  6.8 5.6 %collective-permute-start.1 = (bf16[32,1024]{1,0:T(8,128)(2,1)S(1)}, bf16[32,1024]{1,0:T(8,128)(2,1)S(1)}, u32[]{:S(2)}, u32[]{:S(2)}) collective-permute-start(bf16[32,1024]{1,0:T(8,128)(2,1)S(1)} %get-tuple-element.26), channel_id=1, source_target_pairs={{0,8},{4,12},{8,0},{12,4},{1,9},{5,13},{9,1},{13,5},{2,10},{6,14},... | collective-permute-start | bytes 196616 | tf_op jit(solution)/shard_map/ppermute | solution.py:19
  6.8 5.6 %collective-permute-start.2 = (bf16[32,1024]{1,0:T(8,128)(2,1)S(1)}, bf16[32,1024]{1,0:T(8,128)(2,1)S(1)}, u32[]{:S(2)}, u32[]{:S(2)}) collective-permute-start(bf16[32,1024]{1,0:T(8,128)(2,1)S(1)} %get-tuple-element.27), channel_id=1, source_target_pairs={{0,4},{4,0},{8,12},{12,8},{1,5},{5,1},{9,13},{13,9},{2,6},{6,2},{1... | collective-permute-start | bytes 196616 | tf_op jit(solution)/shard_map/ppermute | solution.py:19
  11.9 6.4 %copy-start.2 = (bf16[2,64,2048]{2,1,0:T(8,128)(2,1)S(1)}, bf16[2,64,2048]{2,1,0:T(8,128)(2,1)}, u32[]{:S(2)}) copy-start(bf16[2,64,2048]{2,1,0:T(8,128)(2,1)} %param.19) | copy-start | bytes 1572868
  11.9 6.4 %copy-start.3 = (bf16[2,64,256]{2,1,0:T(8,128)(2,1)S(1)}, bf16[2,64,256]{2,1,0:T(8,128)(2,1)}, u32[]{:S(2)}) copy-start(bf16[2,64,256]{2,1,0:T(8,128)(2,1)} %param.21) | copy-start | bytes 196612
  11.9 16.0 %copy-start = (bf16[16,2,256,128]{3,2,1,0:T(8,128)(2,1)S(1)}, bf16[16,2,256,128]{3,2,1,0:T(8,128)(2,1)}, u32[]{:S(2)}) copy-start(bf16[16,2,256,128]{3,2,1,0:T(8,128)(2,1)} %k_ref.1) | copy-start | bytes 6291460
  11.9 16.0 %copy-start.1 = (bf16[16,2,256,128]{3,2,1,0:T(8,128)(2,1)S(1)}, bf16[16,2,256,128]{3,2,1,0:T(8,128)(2,1)}, u32[]{:S(2)}) copy-start(bf16[16,2,256,128]{3,2,1,0:T(8,128)(2,1)} %v_ref.1) | copy-start | bytes 6291460
  13.0 2.2 %collective-permute-start.3 = (bf16[64,1024]{1,0:T(8,128)(2,1)S(1)}, bf16[64,1024]{1,0:T(8,128)(2,1)S(1)}, u32[]{:S(2)}, u32[]{:S(2)}) collective-permute-start(bf16[64,1024]{1,0:T(8,128)(2,1)S(1)} %get-tuple-element.29.near_ref), channel_id=1, source_target_pairs={{0,1},{1,0},{2,3},{3,2},{4,5},{5,4},{6,7},{7,6},{8,9},{9,8},{10,11... | collective-permute-start | bytes 393224 | tf_op jit(solution)/shard_map/ppermute | solution.py:19
  13.0 4.1 %collective-permute-start.6 = (bf16[32,128]{1,0:T(8,128)(2,1)S(1)}, bf16[32,128]{1,0:T(8,128)(2,1)S(1)}, u32[]{:S(2)}, u32[]{:S(2)}) collective-permute-start(bf16[32,128]{1,0:T(8,128)(2,1)S(1)} %get-tuple-element.33.refs_0_), channel_id=1, source_target_pairs={{0,3},{1,2},{2,1},{3,0},{4,7},{5,6},{6,5},{7,4},{8,11},{9,10},{10,... | collective-permute-start | bytes 24584 | tf_op jit(solution)/shard_map/ppermute | solution.py:19
  14.6 3.7 %collective-permute-start.5 = (bf16[32,128]{1,0:T(8,128)(2,1)S(1)}, bf16[32,128]{1,0:T(8,128)(2,1)S(1)}, u32[]{:S(2)}, u32[]{:S(2)}) collective-permute-start(bf16[32,128]{1,0:T(8,128)(2,1)S(1)} %get-tuple-element.33.refs_0_), channel_id=1, source_target_pairs={{0,2},{1,3},{2,0},{3,1},{4,6},{5,7},{6,4},{7,5},{8,10},{9,11},{10,... | collective-permute-start | bytes 24584 | tf_op jit(solution)/shard_map/ppermute | solution.py:19
  15.2 3.1 %collective-permute-start.4 = (bf16[32,128]{1,0:T(8,128)(2,1)S(1)}, bf16[32,128]{1,0:T(8,128)(2,1)S(1)}, u32[]{:S(2)}, u32[]{:S(2)}) collective-permute-start(bf16[32,128]{1,0:T(8,128)(2,1)S(1)} %get-tuple-element.33.refs_0_), channel_id=1, source_target_pairs={{0,1},{1,0},{2,3},{3,2},{4,5},{5,4},{6,7},{7,6},{8,9},{9,8},{10,11... | collective-permute-start | bytes 24584 | tf_op jit(solution)/shard_map/ppermute | solution.py:19
  18.7 8.8 %collective-permute-start.7 = (bf16[16,2560]{1,0:T(8,128)(2,1)S(1)}, bf16[16,2560]{1,0:T(8,128)(2,1)S(1)}, u32[]{:S(2)}, u32[]{:S(2)}) collective-permute-start(bf16[16,2560]{1,0:T(8,128)(2,1)S(1)} %get-tuple-element.34), channel_id=1, source_target_pairs={{0,8},{4,12},{8,0},{12,4},{1,9},{5,13},{9,1},{13,5},{2,10},{6,14},... | collective-permute-start | bytes 245768 | tf_op jit(solution)/shard_map/ppermute | solution.py:19
  20.6 6.9 %collective-permute-start.8 = (bf16[16,2560]{1,0:T(8,128)(2,1)S(1)}, bf16[16,2560]{1,0:T(8,128)(2,1)S(1)}, u32[]{:S(2)}, u32[]{:S(2)}) collective-permute-start(bf16[16,2560]{1,0:T(8,128)(2,1)S(1)} %get-tuple-element.35), channel_id=1, source_target_pairs={{0,12},{4,8},{8,4},{12,0},{1,13},{5,9},{9,5},{13,1},{2,14},{6,10},... | collective-permute-start | bytes 245768 | tf_op jit(solution)/shard_map/ppermute | solution.py:19
  22.2 5.7 %collective-permute-start.9 = (bf16[16,2560]{1,0:T(8,128)(2,1)S(1)}, bf16[16,2560]{1,0:T(8,128)(2,1)S(1)}, u32[]{:S(2)}, u32[]{:S(2)}) collective-permute-start(bf16[16,2560]{1,0:T(8,128)(2,1)S(1)} %get-tuple-element.36), channel_id=1, source_target_pairs={{0,4},{4,0},{8,12},{12,8},{1,5},{5,1},{9,13},{13,9},{2,6},{6,2},{1... | collective-permute-start | bytes 245768 | tf_op jit(solution)/shard_map/ppermute | solution.py:19
